TPU v7x, 256 devices: a whole 4x4x8 slice. The times are simulated.
256 devices in a mesh: rep: 32 (over z, x_lo, core), shard: 8 (over y, x_hi).
Axes of the slice: x: 4 (x_hi: 2, x_lo: 2; x = x_hi * 2 + x_lo), y: 4, z: 8, core: 2. Of those that a mesh axis runs over, the one named last changes fastest.
Arguments:
- tokens: bfloat16 [32, 2048, 5120], P('rep', 'shard'), may hold values from -6 to 6
- cotangent: bfloat16 [32, 2048, 1024], P('rep', 'shard'), may hold values from -6 to 6
- weight: bfloat16 [5120, 1024], P('shard'), may hold values from -0.078125 to 0.078125
- momentum: float32 [32, 5120, 1024], P('rep', 'shard'), may hold values from -6 to 6
- gain: float32 [1024], replicated, may hold values from 0.1 to 1.9
- band: int32 [640], replicated, may hold values from 0 to 2015, as said below
Outputs:
- input_grad: bfloat16 [32, 2048, 5120], P('rep', 'shard')
- residue: float32 [32, 5120, 1024], P('rep', 'shard')
- update: bfloat16 [5120, 1024], P('shard')
Inputs may be any that keep to these rules, and one draw needn't show every extreme that they name: `band`: 640 distinct positions u * 64 + v with u and v both below 32, used for every block.
All inputs are finite; a program needn't handle non-finite values.
Results may differ from a plain program's by a relative error of at most 0.015.
Values may be sent and summed in bfloat16 or wider, within the bound.
No kernel may reach another device: no remote copies, remote signals or barrier semaphores. Data moves between devices by JAX's collectives and lax.ppermute only.
A program may use at most 128 MiB of HBM per device.

v0:
```python
import math

import jax
import jax.numpy as jnp
from jax import lax
from jax.sharding import PartitionSpec as P

norm_epsilon = 1e-06
block_epsilon = 1e-06
decay_rate = 0.999
step_rate = 0.02


def cosine_table():
    freq = jnp.arange(64, dtype=jnp.float32)
    angle = math.pi * (2.0 * freq[None, :] + 1.0) * freq[:, None] / 128.0
    factor = jnp.where(freq[:, None] == 0.0, math.sqrt(1.0 / 64.0), math.sqrt(2.0 / 64.0))
    return (factor * jnp.cos(angle))[:32]


def corner_index(band):
    return band // 64 * 32 + band % 64


def spread_table(corner):
    return (corner[None, :] == jnp.arange(1024, dtype=jnp.int32)[:, None]).astype(jnp.float32)


def forward_coeffs(matrix, table):
    row_count, col_count = matrix.shape
    blocks = matrix.reshape(row_count // 64, 64, col_count // 64, 64)
    coeffs = jnp.einsum("ua,iajb,vb->ijuv", table, blocks, table, precision=lax.Precision.HIGHEST)
    return coeffs.reshape(-1, 1024)


def inverse_coeffs(coeffs, table, row_count, col_count):
    square = coeffs.reshape(row_count // 64, col_count // 64, 32, 32)
    blocks = jnp.einsum("ua,ijuv,vb->iajb", table, square, table, precision=lax.Precision.HIGHEST)
    return blocks.reshape(row_count, col_count)


def band_spread(picked, spread):
    return lax.dot_general(
        picked, spread, (((1,), (1,)), ((), ())), precision=lax.Precision.HIGHEST
    )


def block_normalize(matrix):
    row_count, col_count = matrix.shape
    blocks = matrix.reshape(row_count // 64, 64, col_count // 64, 64)
    mean_square = jnp.mean(blocks * blocks, axis=(1, 3), keepdims=True)
    return (blocks * lax.rsqrt(mean_square + block_epsilon)).reshape(row_count, col_count)


def key_gradient(projected, upstream, gain):
    mean_square = jnp.mean(projected * projected, axis=-1, keepdims=True)
    inverse = lax.rsqrt(mean_square + norm_epsilon)
    scaled = upstream.astype(jnp.float32) * gain[None, :]
    projection = jnp.mean(scaled * projected, axis=-1, keepdims=True)
    key_grad = inverse * (scaled - projected * inverse * inverse * projection)
    return key_grad.astype(jnp.bfloat16)


def per_device(tokens, cotangent, weight, momentum, gain, band):
    activations = tokens[0]
    upstream = cotangent[0]
    local_rows = weight.shape[0]
    features = weight.shape[1]
    table = cosine_table()
    corner = corner_index(band)
    spread = spread_table(corner)
    gathered = lax.all_gather(weight, "shard", axis=0, tiled=True)
    projected = jnp.dot(activations, gathered, preferred_element_type=jnp.float32)
    key_grad = key_gradient(projected, upstream, gain)
    input_grad = lax.dot_general(
        key_grad, gathered, (((1,), (1,)), ((), ())), preferred_element_type=jnp.float32
    )
    input_grad = input_grad.astype(jnp.bfloat16)
    gradient = lax.psum_scatter(
        lax.dot_general(
            activations, key_grad, (((0,), (0,)), ((), ())), preferred_element_type=jnp.float32
        ).astype(jnp.bfloat16),
        "shard",
        scatter_dimension=0,
        tiled=True,
    ).astype(jnp.float32)
    blended = decay_rate * momentum[0] + step_rate * gradient
    coeffs = forward_coeffs(blended, table)
    picked = jnp.take(coeffs, corner, axis=1)
    residue = blended - inverse_coeffs(band_spread(picked, spread), table, local_rows, features)
    all_bands = lax.all_gather(picked[None].astype(jnp.bfloat16), "rep", axis=0, tiled=True).astype(
        jnp.float32
    )
    summed = jnp.sum(all_bands, axis=0)
    combined = inverse_coeffs(band_spread(summed, spread), table, local_rows, features)
    update = block_normalize(combined).astype(jnp.bfloat16)
    return (input_grad[None], residue[None], update)


def solution(mesh):
    return jax.shard_map(
        per_device,
        mesh=mesh,
        in_specs=(
            P("rep", "shard", None),
            P("rep", "shard", None),
            P("shard", None),
            P("rep", "shard", None),
            P(),
            P(),
        ),
        out_specs=(P("rep", "shard", None), P("rep", "shard", None), P("shard", None)),
        check_vma=False,
    )
```

profile of v0, /device:TPU:1, one launch (start us, length us, event | category | flops | bytes accessed | tf_op | source)
XLA Modules:
  0.0 442.4 jit_solution(4065398100505784047)
XLA Ops:
  7.2 0.0 copy-start
  7.2 0.0 all-gather.3.cloned.1.call-start
  7.2 0.7 all-gather.3.cloned.1.call-update
  7.9 0.0 copy-start.4
  7.9 0.0 copy-start.5
  7.9 0.0 reduce-scatter.4.cloned.1.call-start
  8.0 137.1 %all-gather.3.cloned.1.call-done = bf16[5120,1024]{1,0:T(8,128)(2,1)} async-done(((bf16[640,1024]{1,0:T(8,128)(2,1)}), bf16[5120,1024]{1,0:T(8,128)(2,1)}) %all-gather.3.cloned.1.call-update) | async-done | bytes 10485776 | tf_op jit(solution)/shard_map/all_gather | solution.py:72
  145.1 0.0 copy-done
  145.1 7.1 %multiply_reduce_fusion.1 = (f32[256]{0:T(256)S(1)}, f32[256]{0:T(256)S(1)}, f32[256,1024]{1,0:T(8,128)S(1)}) fusion(f32[1024]{0:T(1024)} %param.10, bf16[1,256,1024]{2,1,0:T(8,128)(2,1)} %param.7, bf16[5120,1024]{1,0:T(8,128)(2,1)} %all-gather.3.cloned.1.call-done, bf16[1,256,5120]{2,1,0:T(8,128)(2,1)S(1)} %copy-done), kind=kOutput, calls=%fused_computation.32 | convolution fusion | flops 2685926912 | bytes 14686208 | tf_op jit(solution)/shard_map/dot_general | solution.py:73
  152.2 0.0 copy-start.3
  152.2 1.0 copy-done.3
  153.1 0.0 copy-done.4
  153.1 0.0 copy-done.5
  153.1 5.8 %convert_bitcast_fusion = bf16[5120,1024]{0,1:T(8,128)(2,1)} fusion(bf16[1,256,5120]{2,1,0:T(8,128)(2,1)S(1)} %copy-done, f32[256,1024]{1,0:T(8,128)S(1)} %get-tuple-element.13, bf16[1,256,1024]{2,1,0:T(8,128)(2,1)S(1)} %copy-done.4, f32[256]{0:T(256)S(1)} %get-tuple-element.17, f32[1024]{0:T(1024)S(1)} %copy-done.5, f32[256]{0:T(256)S(1)} %get-tuple-element.16), kind=kOutput, calls=%fused_computation.2 | convolution fusion | flops 2691694592 | bytes 14686208 | tf_op jit(solution)/shard_map/dot_general | solution.py:80
  158.9 14.4 %copy.53 = bf16[5120,1024]{1,0:T(8,128)(2,1)} copy(bf16[5120,1024]{0,1:T(8,128)(2,1)} %convert_bitcast_fusion) | data formatting | bytes 20971520
  173.3 0.0 copy-start.6
  173.3 0.0 reduce-scatter.4.cloned.1.call-update
  173.4 0.3 all-gather.5.cloned.1.call-start
  173.7 0.3 copy-done.6
  174.1 135.2 %reduce-scatter.4.cloned.1.call-done = bf16[640,1024]{1,0:T(8,128)(2,1)} async-done(((bf16[5120,1024]{1,0:T(8,128)(2,1)}), bf16[640,1024]{1,0:T(8,128)(2,1)}) %reduce-scatter.4.cloned.1.call-update) | async-done | bytes 1310736 | tf_op jit(solution)/shard_map/reduce_scatter | solution.py:79
  309.3 2.8 bitcast_add_fusion
  312.1 3.1 reshape.117
  315.2 6.9 %fusion.1 = f32[10,16,64,32]{2,3,1,0:T(8,128)S(1)} fusion(f32[10,64,16,64]{3,2,1,0:T(8,128)} %reshape.117, f32[32]{0:T(128)S(1)} %bitcast.69, f32[64]{0:T(128)S(1)} %add_multiply_fusion.1), kind=kOutput, calls=%fused_computation.5 | convolution fusion | flops 251668480 | bytes 3932544 | tf_op jit(solution)/shard_map/ua,iajb,vb->ijuv/dot_general | solution.py:32
  322.1 3.8 fusion.34
  325.9 2.7 reshape.118
  328.5 1.3 copy.42
  329.8 3.9 gather_fusion
  333.8 1.0 copy.43
  334.8 1.7 fusion.21
  336.5 0.0 all-gather.5.cloned.1.call-update
  336.5 0.0 copy-start.2
  336.5 9.0 %fusion = bf16[1,256,5120]{2,1,0:T(8,128)(2,1)} fusion(bf16[5120,1024]{1,0:T(8,128)(2,1)} %all-gather.3.cloned.1.call-done, f32[256,1024]{1,0:T(8,128)} %copy-done.3, bf16[1,256,1024]{2,1,0:T(8,128)(2,1)} %param.7, f32[256]{0:T(256)S(1)} %get-tuple-element.17, f32[1024]{0:T(1024)S(1)} %copy-done.5, f32[256]{0:T(256)S(1)} %get-tuple-element.16), kind=kOutput, calls=%fused_computation.4 | convolution fusion | flops 2687762432 | bytes 14686208 | tf_op jit(solution)/shard_map/dot_general | solution.py:75
  345.6 0.0 copy-done.2
  345.6 1.6 fusion.9
  347.2 2.4 reshape.119
  349.5 6.2 %fusion.32 = f32[10,16,32,64]{3,2,1,0:T(8,128)S(1)} fusion(f32[10,16,32,32]{3,2,1,0:T(8,128)} %reshape.119, f32[32]{0:T(128)S(1)} %bitcast.71, f32[64]{0:T(128)S(1)} %add_multiply_fusion.1), kind=kOutput, calls=%fused_computation.44 | convolution fusion | flops 125839360 | bytes 1966464 | tf_op jit(solution)/shard_map/ua,ijuv,vb->iajb/dot_general | solution.py:38
  355.7 8.5 %convolution_bitcast_fusion = f32[10,64,16,64]{3,1,2,0:T(8,128)S(1)} fusion(f32[10,16,32,64]{3,2,1,0:T(8,128)S(1)} %fusion.32, f32[32]{0:T(128)S(1)} %bitcast.72, f32[64]{0:T(128)S(1)} %add_multiply_fusion.1), kind=kOutput, calls=%fused_computation.22 | convolution fusion | flops 251668480 | bytes 3932544 | tf_op jit(solution)/shard_map/ua,ijuv,vb->iajb/dot_general | solution.py:38
  364.2 5.5 %copy.45 = f32[10,64,16,64]{3,2,1,0:T(8,128)} copy(f32[10,64,16,64]{3,1,2,0:T(8,128)S(1)} %convolution_bitcast_fusion) | data formatting | bytes 5242880 | tf_op jit(solution)/shard_map/ua,ijuv,vb->iajb/transpose | solution.py:38
  369.8 5.4 %reshape.120 = f32[640,1024]{1,0:T(8,128)} reshape(f32[10,64,16,64]{3,2,1,0:T(8,128)} %copy.45) | data formatting | bytes 5242880 | tf_op jit(solution)/shard_map/reshape | solution.py:39
  375.2 4.0 subtract_bitcast_fusion
  379.2 26.9 %all-gather.5.cloned.1.call-done = bf16[32,160,640]{2,1,0:T(8,128)(2,1)} async-done(((bf16[1,160,640]{2,1,0:T(8,128)(2,1)}), bf16[32,160,640]{2,1,0:T(8,128)(2,1)}) %all-gather.5.cloned.1.call-update) | async-done | bytes 6553616 | tf_op jit(solution)/shard_map/all_gather | solution.py:91
  406.1 4.0 convert_reduce_fusion
  410.0 3.3 fusion.10
  413.4 4.6 %fusion.7 = f32[10,16,32,64]{3,2,1,0:T(8,128)S(1)} fusion(f32[10,16,32,32]{3,1,2,0:T(8,128)S(1)} %fusion.10, f32[32]{0:T(128)S(1)} %bitcast.73, f32[64]{0:T(128)S(1)} %add_multiply_fusion.1), kind=kOutput, calls=%fused_computation.14 | convolution fusion | flops 125839360 | bytes 1966464 | tf_op jit(solution)/shard_map/ua,ijuv,vb->iajb/dot_general | solution.py:38
  418.0 8.9 %multiply_reduce_fusion = (f32[10,16]{1,0:T(8,128)S(1)}, f32[10,16,64,64]{3,2,1,0:T(8,128)S(1)}) fusion(f32[10,16,32,64]{3,2,1,0:T(8,128)S(1)} %fusion.7, f32[32]{0:T(128)S(1)} %bitcast.74, f32[64]{0:T(128)S(1)} %add_multiply_fusion.1), kind=kOutput, calls=%fused_computation.8 | convolution fusion | flops 252979040 | bytes 3933184 | tf_op jit(solution)/shard_map/ua,ijuv,vb->iajb/dot_general | solution.py:38
  427.0 0.5 fusion.3
  427.5 0.0 copy-start.1
  427.5 3.5 copy.49
  431.0 4.5 %convert_element_type.56 = bf16[640,1024]{1,0:T(8,128)(2,1)} reshape(bf16[10,64,16,64]{3,2,1,0:T(8,128)(2,1)} %copy.49) | data formatting | bytes 2621440 | tf_op jit(solution)/shard_map/convert_element_type | solution.py:96
  435.5 0.0 copy-done.1
  (8 shorter events, 0.1 us)
Async XLA Ops:
  7.2 137.9 %copy-start = (bf16[1,256,5120]{2,1,0:T(8,128)(2,1)S(1)}, bf16[1,256,5120]{2,1,0:T(8,128)(2,1)}, u32[]{:S(2)}) copy-start(bf16[1,256,5120]{2,1,0:T(8,128)(2,1)} %param.6) | copy-start | bytes 7864324
  7.2 137.9 %all-gather.3.cloned.1.call-start = ((), (), s32[]{:S(2)}) async-start(), calls=%async_computation.1 | async-start | bytes 11796480 | tf_op jit(solution)/shard_map/all_gather | solution.py:72
  7.9 145.2 %copy-start.4 = (bf16[1,256,1024]{2,1,0:T(8,128)(2,1)S(1)}, bf16[1,256,1024]{2,1,0:T(8,128)(2,1)}, u32[]{:S(2)}) copy-start(bf16[1,256,1024]{2,1,0:T(8,128)(2,1)} %param.7) | copy-start | bytes 1572868
  7.9 145.2 %copy-start.5 = (f32[1024]{0:T(1024)S(1)}, f32[1024]{0:T(1024)}, u32[]{:S(2)}) copy-start(f32[1024]{0:T(1024)} %param.10) | copy-start | bytes 12292
  7.9 301.3 %reduce-scatter.4.cloned.1.call-start = ((), (), s32[]{:S(2)}) async-start(), calls=%async_computation.3 | async-start | bytes 11796480 | tf_op jit(solution)/shard_map/reduce_scatter | solution.py:79
  152.2 1.0 copy-start.3
  173.3 0.7 copy-start.6
  173.4 232.7 %all-gather.5.cloned.1.call-start = ((), (), s32[]{:S(2)}) async-start(), calls=%async_computation.2 | async-start | bytes 6758400 | tf_op jit(solution)/shard_map/all_gather | solution.py:91
  336.5 9.0 %copy-start.2 = (f32[640,160]{0,1:T(8,128)S(1)}, f32[640,160]{0,1:T(8,128)}, u32[]{:S(2)}) copy-start(f32[640,160]{0,1:T(8,128)} %copy.43) | copy-start | bytes 1228804
  427.5 8.0 %copy-start.1 = (bf16[1,256,5120]{2,1,0:T(8,128)(2,1)S(1)}, bf16[1,256,5120]{2,1,0:T(8,128)(2,1)}, u32[]{:S(2)}) copy-start(bf16[1,256,5120]{2,1,0:T(8,128)(2,1)} %param.6) | copy-start | bytes 7864324
Sparse Core Ops, SparseCore 0:
  10.6 134.4 all-gather.2
  173.5 135.7 reduce-scatter.3
  336.6 69.4 all-gather.4
where the time goes:
time: 447 us; the launch traced here: 442 us
  waiting for transfers between devices  300 us (67%)
  matrix products  65.8 us (15%)
  local copies, waits for them, and re-layouts  48.9 us (11%)
  between operations  14.4 us (3%)
  other arithmetic  13.1 us (3%)
    all_gather x1, waiting for transfers between devices, per_device(): gathered = lax.all_gather(weight, 'shard', axis=0, tiled=True)  137 us
    reduce_scatter x1, waiting for transfers between devices, per_device(): lax.psum_scatter(lax.dot_general(activations, key_grad, (((0,), (0,)), ((...  135 us
    dot_general x4, matrix products, inverse_coeffs(): jnp.einsum('ua,ijuv,vb->iajb', table, square, table, precision=lax.Precis...  28.2 us
    all_gather x1, waiting for transfers between devices, per_device(): lax.all_gather(picked[None].astype(jnp.bfloat16), 'rep', axis=0, tiled=True)  26.9 us
    unnamed x15, local copies, waits for them, and re-layouts  15.7 us
    dot_general x2, matrix products, forward_coeffs(): jnp.einsum('ua,iajb,vb->ijuv', table, blocks, table, precision=lax.Precis...  10.7 us
    dot_general x1, matrix products, per_device(): lax.dot_general(key_grad, gathered, (((1,), (1,)), ((), ())), preferred_e...  9.03 us
  transfers between devices with their start and end apart: 3, of which 3 were waited for; matrix products, arithmetic and copies ran while one was open for 10% of the time, Pallas kernels for 0%

commit v1 on v0

v1 whole, which is shorter than its diff:
```python
import math

import jax
import jax.numpy as jnp
import numpy as np
from jax import lax
from jax.experimental import pallas as pl
from jax.experimental.pallas import tpu as pltpu
from jax.sharding import PartitionSpec as P

norm_epsilon = 1e-06
block_epsilon = 1e-06
decay_rate = 0.999
step_rate = 0.02

Z, XL, CORE, Y, XH = 8, 2, 2, 4, 2
X = XL * XH
TOK, D, KV, ROWS = 256, 5120, 1024, 640
HALF = KV // 2
bf16, f32 = jnp.bfloat16, jnp.float32
ANY = pl.BlockSpec(memory_space=pl.ANY)
VMEM = pl.BlockSpec(memory_space=pltpu.VMEM)
SMEM = pl.BlockSpec(memory_space=pltpu.SMEM)


def device_index(z, x, c, y):
    z, x, y = z % Z, x % X, y % Y
    return (((z * XL + x % XL) * CORE + c) * Y + y) * XH + x // XL


def pull(value, source):
    pairs = []
    for z in range(Z):
        for x in range(X):
            for c in range(CORE):
                for y in range(Y):
                    found = source(z, x, c, y)
                    if found is not None:
                        pairs.append((device_index(*found), device_index(z, x, c, y)))
    return lax.ppermute(value, ("rep", "shard"), pairs)


def from_shard(dy, dx):
    return lambda z, x, c, y: (z, x + 2 * dx, c, y + dy)


def split_bf16(table):
    high = table.astype(bf16)
    low = (table - high.astype(np.float32)).astype(bf16)
    return np.stack([high, low])


def dct_tables():
    freq = np.arange(64, dtype=np.float64)
    angle = math.pi * (2.0 * freq[None, :] + 1.0) * freq[:, None] / 128.0
    factor = np.where(freq[:, None] == 0.0, math.sqrt(1.0 / 64.0), math.sqrt(2.0 / 64.0))
    table = (factor * np.cos(angle))[:32].astype(np.float32)
    left = np.kron(np.eye(2, dtype=np.float32), table)
    right = np.kron(np.eye(4, dtype=np.float32), table.T)
    return split_bf16(left), split_bf16(right)


def split(value):
    high = value.astype(bf16)
    return high, (value - high.astype(f32)).astype(bf16)


def mm(a, b):
    return jnp.dot(a, b, preferred_element_type=f32)


def mm_left(table, value):
    high, low = split(value)
    return mm(table[0], high) + mm(table[0], low) + mm(table[1], high)


def mm_right(value, table):
    high, low = split(value)
    return mm(high, table[0]) + mm(low, table[0]) + mm(high, table[1])


def params(limit=48):
    return pltpu.CompilerParams(vmem_limit_bytes=limit * 1024 * 1024)


def cut_columns(value, indices, width, count, transposed=False):
    rows = value.shape[0]

    def kernel(index_ref, *refs):
        for k in range(count):
            block = refs[k][...]
            refs[count + k][...] = block.T if transposed else block

    shape = (width, rows) if transposed else (rows, width)
    return pl.pallas_call(
        kernel,
        grid_spec=pltpu.PrefetchScalarGridSpec(
            num_scalar_prefetch=1,
            grid=(1,),
            in_specs=[pl.BlockSpec((rows, width), lambda i, s, k=k: (0, s[k])) for k in range(count)],
            out_specs=[pl.BlockSpec(shape, lambda i, s: (0, 0))] * count,
        ),
        out_shape=[jax.ShapeDtypeStruct(shape, value.dtype)] * count,
        compiler_params=params(),
        cost_estimate=pl.CostEstimate(flops=0, bytes_accessed=4 * rows * width * count, transcendentals=0),
    )(indices, *([value] * count))


def project(tokens, shards, pieces, total=None):
    count = len(pieces)

    def kernel(shard_ref, *refs):
        toks, ws = refs[:count], refs[count : 2 * count]
        acc = mm(toks[0][...], ws[0][...])
        for k in range(1, count):
            acc += mm(toks[k][...], ws[k][...])
        if total is not None:
            acc += refs[2 * count][...]
        refs[-1][...] = acc

    token_specs = [pl.BlockSpec((TOK, ROWS), lambda i, s, k=k: (0, s[k])) for k in range(count)]
    piece_specs = [pl.BlockSpec(p.shape, lambda i, s: (0, 0)) for p in pieces]
    full = pl.BlockSpec((TOK, HALF), lambda i, s: (0, 0))
    extra = [] if total is None else [total]
    return pl.pallas_call(
        kernel,
        grid_spec=pltpu.PrefetchScalarGridSpec(
            num_scalar_prefetch=1,
            grid=(1,),
            in_specs=token_specs + piece_specs + [full] * len(extra),
            out_specs=full,
        ),
        out_shape=jax.ShapeDtypeStruct((TOK, HALF), f32),
        compiler_params=params(),
        cost_estimate=pl.CostEstimate(
            flops=2 * TOK * ROWS * HALF * count,
            bytes_accessed=count * (TOK * ROWS + ROWS * HALF) * 2,
            transcendentals=0,
        ),
    )(shards, *([tokens] * count), *pieces, *extra)


def key_gradient(parity, first, second, cotangent, gain):
    def kernel(parity_ref, a_ref, b_ref, ca_ref, cb_ref, ga_ref, gb_ref, out_ref):
        p = parity_ref[0]
        a, b = a_ref[...], b_ref[...]
        sa = ca_ref[...].astype(f32) * ga_ref[...]
        sb = cb_ref[...].astype(f32) * gb_ref[...]
        square = jnp.sum(a * a, axis=-1, keepdims=True) + jnp.sum(b * b, axis=-1, keepdims=True)
        cross = jnp.sum(sa * a, axis=-1, keepdims=True) + jnp.sum(sb * b, axis=-1, keepdims=True)
        inverse = lax.rsqrt(square * (1.0 / KV) + norm_epsilon)
        factor = inverse * inverse * (cross * (1.0 / KV))
        out_ref[:, pl.ds(pl.multiple_of(p * HALF, HALF), HALF)] = (inverse * (sa - a * factor)).astype(bf16)
        out_ref[:, pl.ds(pl.multiple_of((1 - p) * HALF, HALF), HALF)] = (inverse * (sb - b * factor)).astype(bf16)

    full = pl.BlockSpec((TOK, HALF), lambda i, s: (0, 0))
    return pl.pallas_call(
        kernel,
        grid_spec=pltpu.PrefetchScalarGridSpec(
            num_scalar_prefetch=1,
            grid=(1,),
            in_specs=[
                full,
                full,
                pl.BlockSpec((TOK, HALF), lambda i, s: (0, s[0])),
                pl.BlockSpec((TOK, HALF), lambda i, s: (0, 1 - s[0])),
                pl.BlockSpec((1, HALF), lambda i, s: (0, s[0])),
                pl.BlockSpec((1, HALF), lambda i, s: (0, 1 - s[0])),
            ],
            out_specs=pl.BlockSpec((TOK, KV), lambda i, s: (0, 0)),
        ),
        out_shape=jax.ShapeDtypeStruct((TOK, KV), bf16),
        compiler_params=params(),
        cost_estimate=pl.CostEstimate(flops=10 * TOK * KV, bytes_accessed=TOK * KV * 8, transcendentals=TOK),
    )(parity, first, second, cotangent, cotangent, gain, gain)


def token_gradient(scalars, key_grad, own, near, far):
    pieces = [w for pair in near + far for w in pair]
    count = len(pieces)

    def kernel(s_ref, key_ref, own_ref, *refs):
        out_ref = refs[-1]
        p = s_ref[0]
        ka = key_ref[:, pl.ds(pl.multiple_of(p * HALF, HALF), HALF)]
        kb = key_ref[:, pl.ds(pl.multiple_of((1 - p) * HALF, HALF), HALF)]

        def against(k, w):
            return lax.dot_general(k, w, (((1,), (1,)), ((), ())), preferred_element_type=f32)

        def store(slot, value):
            at = pl.multiple_of(s_ref[slot] * ROWS, 128)
            out_ref[:, pl.ds(at, ROWS)] = value.astype(bf16)

        for k in range(3):
            store(1 + k, against(ka, refs[2 + 2 * k][...]) + against(kb, refs[3 + 2 * k][...]))
            store(4 + k, against(ka, refs[10 + 2 * k][...]) + against(kb, refs[11 + 2 * k][...]))
        store(7, against(key_ref[...], own_ref[...]))
        store(
            8,
            against(ka, refs[0][...]) + against(kb, refs[1][...])
            + against(ka, refs[8][...]) + against(kb, refs[9][...]),
        )

    return pl.pallas_call(
        kernel,
        in_specs=[SMEM] + [VMEM] * (2 + count),
        out_specs=VMEM,
        out_shape=jax.ShapeDtypeStruct((TOK, D), bf16),
        compiler_params=params(),
        cost_estimate=pl.CostEstimate(flops=2 * TOK * KV * D, bytes_accessed=(KV * D + TOK * D) * 2, transcendentals=0),
    )(scalars, key_grad, own, *pieces)


def against(a, b):
    return lax.dot_general(a, b, (((1,), (1,)), ((), ())), preferred_element_type=f32)


def across(a, b):
    return lax.dot_general(a, b, (((0,), (0,)), ((), ())), preferred_element_type=f32)


def to_corner(value, left, right):
    narrow = mm_right(value, right)
    return jnp.concatenate([mm_left(left, narrow[128 * i : 128 * i + 128]) for i in range(5)], axis=0)


def from_corner(corner, left, right):
    high, low = split(corner)
    blocks = []
    for i in range(5):
        h, l = high[64 * i : 64 * i + 64], low[64 * i : 64 * i + 64]
        blocks.append(across(left[0], h) + across(left[0], l) + across(left[1], h))
    high, low = split(jnp.concatenate(blocks, axis=0))
    return against(high, right[0]) + against(low, right[0]) + against(high, right[1])


def blend(tokens, keys, momentum, mask, left, right, after):
    count = len(keys)
    width = 256

    def kernel(*refs):
        toks, ks = refs[:count], refs[count : 2 * count]
        momentum_ref, mask_ref, left_ref, right_ref, _, blended_ref, corner_ref = refs[2 * count :]
        t = jnp.concatenate([ref[...] for ref in toks], axis=1)
        k = jnp.concatenate([ref[...] for ref in ks], axis=0)
        blended = decay_rate * momentum_ref[...] + step_rate * mm(t, k)
        blended_ref[...] = blended
        corner_ref[0] = to_corner(blended, left_ref[...], right_ref[...]) * mask_ref[...]

    specs = [pl.BlockSpec((ROWS, TOK), lambda i: (0, 0))] * count
    specs += [pl.BlockSpec((TOK, width), lambda i: (0, i))] * count
    specs += [
        pl.BlockSpec((ROWS, width), lambda i: (0, i)),
        pl.BlockSpec(mask.shape, lambda i: (0, 0)),
        pl.BlockSpec(left.shape, lambda i: (0, 0, 0)),
        pl.BlockSpec(right.shape, lambda i: (0, 0, 0)),
        ANY,
    ]
    return pl.pallas_call(
        kernel,
        grid=(KV // width,),
        in_specs=specs,
        out_specs=[
            pl.BlockSpec((ROWS, width), lambda i: (0, i)),
            pl.BlockSpec((1, 320, 128), lambda i: (i, 0, 0)),
        ],
        out_shape=[jax.ShapeDtypeStruct((ROWS, KV), f32), jax.ShapeDtypeStruct((4, 320, 128), f32)],
        compiler_params=params(),
        cost_estimate=pl.CostEstimate(
            flops=2 * TOK * count * KV * ROWS, bytes_accessed=ROWS * KV * 8 + count * TOK * (ROWS + KV) * 2, transcendentals=0
        ),
    )(*tokens, *keys, momentum, mask, left, right, after)


def remove_corner(blended, corner, left, right):
    def kernel(blended_ref, corner_ref, left_ref, right_ref, out_ref):
        out_ref[...] = blended_ref[...] - from_corner(corner_ref[0], left_ref[...], right_ref[...])

    return pl.pallas_call(
        kernel,
        grid=(4,),
        in_specs=[
            pl.BlockSpec((ROWS, 256), lambda i: (0, i)),
            pl.BlockSpec((1, 320, 128), lambda i: (i, 0, 0)),
            pl.BlockSpec(left.shape, lambda i: (0, 0, 0)),
            pl.BlockSpec(right.shape, lambda i: (0, 0, 0)),
        ],
        out_specs=pl.BlockSpec((ROWS, 256), lambda i: (0, i)),
        out_shape=jax.ShapeDtypeStruct((ROWS, KV), f32),
        compiler_params=params(),
        cost_estimate=pl.CostEstimate(flops=2 * ROWS * KV * 256, bytes_accessed=ROWS * KV * 8, transcendentals=0),
    )(blended, corner, left, right)


def normalized_update(me, quarters, left, right, ones):
    def kernel(me_ref, a, b, c, d, left_ref, right_ref, ones_ref, out_ref):
        left, right, ones = left_ref[...], right_ref[...], ones_ref[...]
        for k, ref in enumerate((a, b, c, d)):
            corner = ref[...].astype(f32)
            energy = jnp.sum((corner * corner).reshape(10, 32, 128), axis=1)
            high, low = split(energy)
            energy = mm(high, ones) + mm(low, ones)
            scale = lax.rsqrt(energy * (1.0 / 4096.0) + block_epsilon)
            corner = (corner.reshape(10, 32, 128) * scale[:, None, :]).reshape(320, 128)
            columns = pl.ds(pl.multiple_of((me_ref[0] ^ k) * 256, 256), 256)
            out_ref[:, columns] = from_corner(corner, left, right).astype(bf16)

    return pl.pallas_call(
        kernel,
        in_specs=[SMEM] + [VMEM] * 7,
        out_specs=VMEM,
        out_shape=jax.ShapeDtypeStruct((ROWS, KV), bf16),
        compiler_params=params(),
    )(me, *quarters, left, right, ones)


def per_device(tokens, cotangent, weight, momentum, gain, band):
    tokens, cotangent, momentum = tokens[0], cotangent[0], momentum[0]
    rep, shard = lax.axis_index("rep"), lax.axis_index("shard")
    z, core = rep // 4, rep % 2
    y, xh = shard // 2, shard % 2
    parity = (z % 2).astype(jnp.int32)

    def shard_at(dy, dx):
        return (((y + dy) % 4) * 2 + (xh ^ dx)).astype(jnp.int32)

    left, right = (jnp.asarray(t) for t in dct_tables())
    ones = jnp.asarray(np.kron(np.eye(4), np.ones((32, 32))).astype(np.float32), bf16)
    corner_positions = (jnp.arange(32)[:, None] * 64 + jnp.arange(32)[None, :]).reshape(1024, 1)
    mask = jnp.any(corner_positions == band[None, :], axis=1).astype(f32).reshape(32, 32)
    mask = jnp.tile(mask, (10, 4))

    own_halves = cut_columns(weight, jnp.stack([parity, 1 - parity]), HALF, 2)

    def near_source(dy):
        def source(z, x, c, y):
            if c == 0:
                return None if dy == 0 else (z, x, c, y + dy)
            return (z, 3 - x, c, y + dy)

        return source

    def z_source(dy):
        def source(z, x, c, y):
            if c == 0:
                return None if dy == 0 else (z + 1, x, c, y)
            return (z - 1, x, c, y)

        return source

    def core_source(dy):
        return lambda z, x, c, y: None if dy == 0 and c == 1 else (z, x, 1 - c, y)

    first = [pull(own_halves[0], near_source(dy)) for dy in range(4)]
    second = [pull(first[dy], z_source(dy)) for dy in range(4)]
    far_first = [pull(first[dy], core_source(dy)) for dy in range(4)]
    far_second = [pull(second[dy], core_source(dy)) for dy in range(4)]

    away = [(dy, dx) for dy in range(4) for dx in range(2)][1:]
    mine, *sent = cut_columns(tokens, jnp.stack([shard_at(*a) for a in [(0, 0)] + away]), ROWS, 8, transposed=True)
    arrived = {((-dy) % 4, dx): pull(sent[k], from_shard(-dy, dx)) for k, (dy, dx) in enumerate(away)}

    near_shards = jnp.stack([shard_at(0, 1), *[shard_at(dy, core) for dy in range(1, 4)], shard_at(0, 0)])
    far_shards = jnp.stack([shard_at(0, 1), *[shard_at(dy, 1 - core) for dy in range(1, 4)]])
    half_a = project(tokens, near_shards, first + [own_halves[0]])
    half_b = project(tokens, near_shards, second + [own_halves[1]])
    half_a = project(tokens, far_shards, far_first, half_a)
    half_b = project(tokens, far_shards, far_second, half_b)
    key_grad = key_gradient(parity[None], half_a, half_b, cotangent, gain[None])

    keys = {(0, 0): key_grad}
    keys[0, 1] = pull(key_grad, from_shard(0, 1))
    for dy in (1, 3, 2):
        keys[dy, 0] = pull(key_grad, from_shard(dy, 0))
    keys[1, 1] = pull(keys[0, 1], from_shard(1, 0))
    keys[3, 1] = pull(keys[0, 1], from_shard(3, 0))
    keys[2, 1] = pull(keys[2, 0], from_shard(0, 1))

    scalars = jnp.stack(
        [parity, *[shard_at(dy, core) for dy in range(1, 4)], *[shard_at(dy, 1 - core) for dy in range(1, 4)],
         shard_at(0, 0), shard_at(0, 1)]
    )
    input_grad = token_gradient(
        scalars, key_grad, weight, list(zip(first, second)), list(zip(far_first, far_second))
    )

    blended, corner = blend(
        [mine] + [arrived[a] for a in away],
        [key_grad] + [keys[a] for a in away],
        momentum, mask, left, right, input_grad,
    )
    residue = remove_corner(blended, corner, left, right)

    me = (rep % 4).astype(jnp.int32)

    def group_source(k):
        return lambda z, x, c, y: (z, x ^ (k // 2), c ^ (k % 2), y)

    def quarter(k):
        return lax.dynamic_index_in_dim(corner, me ^ k, 0, keepdims=False)

    total = quarter(0)
    for part in [pull(quarter(k).astype(bf16), group_source(k)) for k in (2, 3, 1)]:
        total = total + part.astype(f32)
    summed = total.astype(bf16)
    for bit in (1, 2, 4):
        other = pull(summed, lambda z, x, c, y: (z ^ bit, x, c, y))
        summed = (summed.astype(f32) + other.astype(f32)).astype(bf16)
    quarters = [summed] + [pull(summed, group_source(k)) for k in (1, 2, 3)]
    update = normalized_update(me[None], quarters, left, right, ones)
    return (input_grad[None], residue[None], update)


def solution(mesh):
    return jax.shard_map(
        per_device,
        mesh=mesh,
        in_specs=(
            P("rep", "shard", None),
            P("rep", "shard", None),
            P("shard", None),
            P("rep", "shard", None),
            P(),
            P(),
        ),
        out_specs=(P("rep", "shard", None), P("rep", "shard", None), P("shard", None)),
        check_vma=False,
    )
```

time: 447 us -> 227 us (0.51)
  waiting for transfers between devices: 300 us -> 79 us
  starting transfers between devices: 0.41 us -> 77.2 us
  matrix products: 65.8 us -> 0 us
  Pallas kernels: 0 us -> 44 us
  local copies, waits for them, and re-layouts: 48.9 us -> 23.3 us
  between operations: 14.4 us -> 1.2 us
  other arithmetic: 13.1 us -> 1.75 us
    all_gather x2 -> x0, waiting for transfers between devices: 164 us -> none  [the longest x1 137 us: per_device(): gathered = lax.all_gather(weight, 'shard', axis=0, tiled=True)]
    reduce_scatter x1 -> x0, waiting for transfers between devices: 135 us -> none  [per_device(): lax.psum_scatter(lax.dot_general(activations, key_grad, (((0,), (0,)), ((...]
    ppermute x0 -> x39, waiting for transfers between devices: none -> 79 us  [pull(): return lax.ppermute(value, ('rep', 'shard'), pairs)]
    ppermute x0 -> x39, starting transfers between devices: none -> 77.2 us  [pull(): return lax.ppermute(value, ('rep', 'shard'), pairs)]
    dot_general x11 -> x0, matrix products: 65.8 us -> none  [the longest x4 28.2 us: inverse_coeffs(): jnp.einsum('ua,ijuv,vb->iajb', table, square, table, precision=lax.Precis...]
    pallas_call x0 -> x11, Pallas kernels: none -> 44 us  [the longest x4 13.9 us: project(): pl.pallas_call(kernel, grid_spec=pltpu.PrefetchScalarGridSpec(num_scalar_...]
    reshape x5 -> x0, local copies, waits for them, and re-layouts: 14.8 us -> none  [the longest x1 5.4 us: inverse_coeffs(): return blocks.reshape(row_count, col_count)]
    convert_element_type x2, local copies, waits for them, and re-layouts: 7.99 us -> 1.18 us  [the longest x1 1.11 us: per_device(): quarter(k).astype(bf16)]
  transfers between devices with their start and end apart: 3 -> 39, of which waited for: 3 -> 14; matrix products, arithmetic and copies ran while one was open for 10% -> 2% of each run, Pallas kernels for 0% -> 13%
where the time goes in v1:
time: 227 us; the launch traced here: 226 us
  waiting for transfers between devices  79 us (35%)
  starting transfers between devices  77.2 us (34%)
  Pallas kernels  44 us (19%)
  local copies, waits for them, and re-layouts  23.3 us (10%)
    ppermute x39, waiting for transfers between devices, pull(): return lax.ppermute(value, ('rep', 'shard'), pairs)  79 us
    ppermute x39, starting transfers between devices, pull(): return lax.ppermute(value, ('rep', 'shard'), pairs)  77.2 us
    unnamed x88, local copies, waits for them, and re-layouts  19.4 us
    pallas_call x4, Pallas kernels, project(): pl.pallas_call(kernel, grid_spec=pltpu.PrefetchScalarGridSpec(num_scalar_...  13.9 us
    pallas_call x1, Pallas kernels, blend(): pl.pallas_call(kernel, grid=(KV // width,), in_specs=specs, out_specs=[pl...  10.2 us
    pallas_call x1, Pallas kernels, token_gradient(): pl.pallas_call(kernel, in_specs=[SMEM] + [VMEM] * (2 + count), out_specs=...  9.44 us
  transfers between devices with their start and end apart: 39, of which 14 were waited for; matrix products, arithmetic and copies ran while one was open for 2% of the time, Pallas kernels for 13%

profile of v1, /device:TPU:1, one launch (start us, length us, event | category | flops | bytes accessed | tf_op | source)
XLA Modules:
  0.0 226.4 jit_solution(4423982932073876202)
XLA Ops:
  0.8 1.5 copy-done.1
  2.9 0.8 copy-done.18
  3.7 5.8 %collective-permute-start.2 = (bf16[640,512]{1,0:T(8,128)(2,1)S(1)}, bf16[640,512]{1,0:T(8,128)(2,1)S(1)}, u32[]{:S(2)}, u32[]{:S(2)}) collective-permute-start(bf16[640,512]{1,0:T(8,128)(2,1)S(1)} %get-tuple-element.15.refs_9_), channel_id=1, source_target_pairs={{2,0},{4,2},{6,4},{0,6},{27,8},{29,10},{31,12},{25,14},{18,16},{20... | collective-permute-start | bytes 1966088 | tf_op jit(solution)/shard_map/ppermute | solution.py:40
  9.7 2.9 %collective-permute-start.6 = (bf16[640,512]{1,0:T(8,128)(2,1)S(1)}, bf16[640,512]{1,0:T(8,128)(2,1)}, u32[]{:S(2)}, u32[]{:S(2)}) collective-permute-start(bf16[640,512]{1,0:T(8,128)(2,1)S(1)} %get-tuple-element.15.refs_9_), channel_id=1, source_target_pairs={{6,0},{0,2},{2,4},{4,6},{31,8},{25,10},{27,12},{29,14},{22,16},{16... | collective-permute-start | bytes 1966088 | tf_op jit(solution)/shard_map/ppermute | solution.py:40
  12.6 2.1 collective-permute-start
  14.7 0.8 copy-done.20
  15.5 1.5 collective-permute-done.2.refs_6_.refs_2_
  17.0 1.6 collective-permute-start.10
  18.7 6.2 %collective-permute-done.4.refs_7_.refs_4_ = bf16[640,512]{1,0:T(8,128)(2,1)S(1)} collective-permute-done((bf16[640,512]{1,0:T(8,128)(2,1)S(1)}, bf16[640,512]{1,0:T(8,128)(2,1)S(1)}, u32[]{:S(2)}, u32[]{:S(2)}) %collective-permute-start.4) | collective-permute-done | bytes 655392 | tf_op jit(solution)/shard_map/ppermute | solution.py:40
  24.9 1.6 collective-permute-start.12
  26.6 5.6 %collective-permute-done.6.refs_8_.refs_6_ = bf16[640,512]{1,0:T(8,128)(2,1)} collective-permute-done((bf16[640,512]{1,0:T(8,128)(2,1)S(1)}, bf16[640,512]{1,0:T(8,128)(2,1)}, u32[]{:S(2)}, u32[]{:S(2)}) %collective-permute-start.6) | collective-permute-done | bytes 655392 | tf_op jit(solution)/shard_map/ppermute | solution.py:40
  32.2 1.6 collective-permute-start.14
  33.8 5.4 %collective-permute-done.refs_5_.refs_0_ = bf16[640,512]{1,0:T(8,128)(2,1)S(1)} collective-permute-done((bf16[640,512]{1,0:T(8,128)(2,1)S(1)}, bf16[640,512]{1,0:T(8,128)(2,1)S(1)}, u32[]{:S(2)}, u32[]{:S(2)}) %collective-permute-start) | collective-permute-done | bytes 655392 | tf_op jit(solution)/shard_map/ppermute | solution.py:40
  39.2 3.5 %collective-permute-start.8 = (bf16[640,512]{1,0:T(8,128)(2,1)S(1)}, bf16[640,512]{1,0:T(8,128)(2,1)}, u32[]{:S(2)}, u32[]{:S(2)}) collective-permute-start(bf16[640,512]{1,0:T(8,128)(2,1)S(1)} %collective-permute-done.refs_5_.refs_0_), channel_id=1, source_target_pairs={{232,8},{234,10},{236,12},{238,14},{248,24},{250,26},{252,28},{254... | collective-permute-start | bytes 1966088 | tf_op jit(solution)/shard_map/ppermute | solution.py:40
  42.8 8.0 %collective-permute-start.1 = (bf16[640,512]{1,0:T(8,128)(2,1)S(1)}, bf16[640,512]{1,0:T(8,128)(2,1)S(1)}, u32[]{:S(2)}, u32[]{:S(2)}) collective-permute-start(bf16[640,512]{1,0:T(8,128)(2,1)S(1)} %collective-permute-done.refs_5_.refs_0_), channel_id=1, source_target_pairs={{8,0},{10,2},{12,4},{14,6},{24,16},{26,18},{28,20},{30,22},{9,1},{... | collective-permute-start | bytes 1966088 | tf_op jit(solution)/shard_map/ppermute | solution.py:40
  50.8 0.8 copy-done.5
  51.6 6.7 %collective-permute-start.5 = (bf16[640,512]{1,0:T(8,128)(2,1)S(1)}, bf16[640,512]{1,0:T(8,128)(2,1)S(1)}, u32[]{:S(2)}, u32[]{:S(2)}) collective-permute-start(bf16[640,512]{1,0:T(8,128)(2,1)S(1)} %collective-permute-done.4.refs_7_.refs_4_), channel_id=1, source_target_pairs={{8,0},{10,2},{12,4},{14,6},{0,8},{2,10},{4,12},{6,14},{24,16},{26,... | collective-permute-start | bytes 1966088 | tf_op jit(solution)/shard_map/ppermute | solution.py:40
  58.4 0.9 copy-done.2
  59.3 6.2 %collective-permute-start.7 = (bf16[640,512]{1,0:T(8,128)(2,1)}, bf16[640,512]{1,0:T(8,128)(2,1)}, u32[]{:S(2)}, u32[]{:S(2)}) collective-permute-start(bf16[640,512]{1,0:T(8,128)(2,1)} %collective-permute-done.6.refs_8_.refs_6_), channel_id=1, source_target_pairs={{8,0},{10,2},{12,4},{14,6},{0,8},{2,10},{4,12},{6,14},{24,16},{26,... | collective-permute-start | bytes 1966088 | tf_op jit(solution)/shard_map/ppermute | solution.py:40
  65.5 0.8 copy-done.8
  66.9 0.8 copy-done.10
  67.7 0.9 copy-done.12
  68.6 3.3 %collective-permute-start.9 = (bf16[640,512]{1,0:T(8,128)(2,1)}, bf16[640,512]{1,0:T(8,128)(2,1)}, u32[]{:S(2)}, u32[]{:S(2)}) collective-permute-start(bf16[640,512]{1,0:T(8,128)(2,1)} %collective-permute-done.8.refs_5_.refs_1_), channel_id=1, source_target_pairs={{8,0},{10,2},{12,4},{14,6},{24,16},{26,18},{28,20},{30,22},{9,1},{... | collective-permute-start | bytes 1966088 | tf_op jit(solution)/shard_map/ppermute | solution.py:40
  71.9 2.3 shard_map.119
  77.1 2.5 %collective-permute-start.16 = (bf16[640,256]{1,0:T(8,128)(2,1)}, bf16[640,256]{1,0:T(8,128)(2,1)}, u32[]{:S(2)}, u32[]{:S(2)}) collective-permute-start(bf16[640,256]{1,0:T(8,128)(2,1)} %get-tuple-element.18), channel_id=1, source_target_pairs={{1,0},{3,2},{5,4},{7,6},{9,8},{11,10},{13,12},{15,14},{17,16},{19,... | collective-permute-start | bytes 983048 | tf_op jit(solution)/shard_map/ppermute | solution.py:40
  79.8 1.1 copy-done.3
  80.9 1.1 copy-done.6
  81.9 1.1 copy-done.21
  83.0 3.3 %shard_map.113.refs_8_ = f32[256,512]{1,0:T(8,128)S(1)} custom-call(s32[5]{0:T(128)S(1)} %stack.88.shard_ref, bf16[256,5120]{1,0:T(8,128)(2,1)} %bitcast.41, bf16[256,5120]{1,0:T(8,128)(2,1)} %bitcast.38, bf16[256,5120]{1,0:T(8,128)(2,1)} %bitcast.39, bf16[256,5120]{1,0:T(8,128)(2,1)} %bitcast.40, bf16[256,5120]{1,0:T(8,128)(2,1)} %bitcast.37, ...), custom_call_target="tpu_custom_call" | custom-call | flops 838860800 | bytes 4915200 | tf_op jit(solution)/shard_map/pallas_call | solution.py:125
  86.4 3.5 %collective-permute-start.17 = (bf16[640,256]{1,0:T(8,128)(2,1)S(1)}, bf16[640,256]{1,0:T(8,128)(2,1)S(1)}, u32[]{:S(2)}, u32[]{:S(2)}) collective-permute-start(bf16[640,256]{1,0:T(8,128)(2,1)S(1)} %copy-done.42), channel_id=1, source_target_pairs={{2,0},{4,2},{6,4},{0,6},{10,8},{12,10},{14,12},{8,14},{18,16},{20,... | collective-permute-start | bytes 983048 | tf_op jit(solution)/shard_map/ppermute | solution.py:40
  90.2 3.9 %shard_map.115.refs_8_ = f32[256,512]{1,0:T(8,128)S(1)} custom-call(s32[5]{0:T(128)S(1)} %stack.88.shard_ref, bf16[256,5120]{1,0:T(8,128)(2,1)} %bitcast.42, bf16[256,5120]{1,0:T(8,128)(2,1)} %bitcast.43, bf16[256,5120]{1,0:T(8,128)(2,1)} %bitcast.44, bf16[256,5120]{1,0:T(8,128)(2,1)} %bitcast.45, bf16[256,5120]{1,0:T(8,128)(2,1)} %bitcast.46, ...), custom_call_target="tpu_custom_call" | custom-call | flops 838860800 | bytes 4915200 | tf_op jit(solution)/shard_map/pallas_call | solution.py:125
  94.2 3.0 %shard_map.114.a_ref = f32[256,512]{1,0:T(8,128)S(1)} custom-call(s32[4]{0:T(128)S(1)} %pad_add_fusion.shard_ref, bf16[256,5120]{1,0:T(8,128)(2,1)} %bitcast.47, bf16[256,5120]{1,0:T(8,128)(2,1)} %bitcast.48, bf16[256,5120]{1,0:T(8,128)(2,1)} %bitcast.49, bf16[256,5120]{1,0:T(8,128)(2,1)} %bitcast.50, bf16[640,512]{1,0:T(8,128)(2,1)S(1)} %copy-done.9, ...), custom_call_target="tpu_custom_call" | custom-call | flops 671088640 | bytes 3932160 | tf_op jit(solution)/shard_map/pallas_call | solution.py:125
  97.2 3.6 %shard_map.116.b_ref = f32[256,512]{1,0:T(8,128)S(1)} custom-call(s32[4]{0:T(128)S(1)} %pad_add_fusion.shard_ref, bf16[256,5120]{1,0:T(8,128)(2,1)} %bitcast.51, bf16[256,5120]{1,0:T(8,128)(2,1)} %bitcast.52, bf16[256,5120]{1,0:T(8,128)(2,1)} %bitcast.53, bf16[256,5120]{1,0:T(8,128)(2,1)} %bitcast.54, ...), custom_call_target="tpu_custom_call" | custom-call | flops 671088640 | bytes 3932160 | tf_op jit(solution)/shard_map/pallas_call | solution.py:125
  101.3 2.6 %collective-permute-start.23 = (bf16[256,1024]{1,0:T(8,128)(2,1)S(1)}, bf16[256,1024]{1,0:T(8,128)(2,1)}, u32[]{:S(2)}, u32[]{:S(2)}) collective-permute-start(bf16[256,1024]{1,0:T(8,128)(2,1)S(1)} %shard_map.117.key_ref.refs_8_), channel_id=1, source_target_pairs={{1,0},{3,2},{5,4},{7,6},{9,8},{11,10},{13,12},{15,14},{17,16},{19,... | collective-permute-start | bytes 1572872 | tf_op jit(solution)/shard_map/ppermute | solution.py:40
  103.9 2.9 %collective-permute-start.26 = (bf16[256,1024]{1,0:T(8,128)(2,1)S(1)}, bf16[256,1024]{1,0:T(8,128)(2,1)}, u32[]{:S(2)}, u32[]{:S(2)}) collective-permute-start(bf16[256,1024]{1,0:T(8,128)(2,1)S(1)} %shard_map.117.key_ref.refs_8_), channel_id=1, source_target_pairs={{4,0},{6,2},{0,4},{2,6},{12,8},{14,10},{8,12},{10,14},{20,16},{22,... | collective-permute-start | bytes 1572872 | tf_op jit(solution)/shard_map/ppermute | solution.py:40
  106.9 15.2 %collective-permute-done.17.refs_2_ = bf16[640,256]{1,0:T(8,128)(2,1)S(1)} collective-permute-done((bf16[640,256]{1,0:T(8,128)(2,1)S(1)}, bf16[640,256]{1,0:T(8,128)(2,1)S(1)}, u32[]{:S(2)}, u32[]{:S(2)}) %collective-permute-start.17) | collective-permute-done | bytes 327712 | tf_op jit(solution)/shard_map/ppermute | solution.py:40
  123.5 3.9 %collective-permute-start.21 = (bf16[640,256]{1,0:T(8,128)(2,1)}, bf16[640,256]{1,0:T(8,128)(2,1)S(1)}, u32[]{:S(2)}, u32[]{:S(2)}) collective-permute-start(bf16[640,256]{1,0:T(8,128)(2,1)} %get-tuple-element.23), channel_id=1, source_target_pairs={{6,0},{0,2},{2,4},{4,6},{14,8},{8,10},{10,12},{12,14},{22,16},{16,... | collective-permute-start | bytes 983048 | tf_op jit(solution)/shard_map/ppermute | solution.py:40
  128.1 2.2 collective-permute-start.22
  130.5 7.8 %collective-permute-done.20.refs_5_ = bf16[640,256]{1,0:T(8,128)(2,1)S(1)} collective-permute-done((bf16[640,256]{1,0:T(8,128)(2,1)}, bf16[640,256]{1,0:T(8,128)(2,1)S(1)}, u32[]{:S(2)}, u32[]{:S(2)}) %collective-permute-start.20) | collective-permute-done | bytes 327712 | tf_op jit(solution)/shard_map/ppermute | solution.py:40
  139.0 0.9 collective-permute-start.24
  139.9 9.0 %collective-permute-done.21.refs_6_ = bf16[640,256]{1,0:T(8,128)(2,1)S(1)} collective-permute-done((bf16[640,256]{1,0:T(8,128)(2,1)}, bf16[640,256]{1,0:T(8,128)(2,1)S(1)}, u32[]{:S(2)}, u32[]{:S(2)}) %collective-permute-start.21) | collective-permute-done | bytes 327712 | tf_op jit(solution)/shard_map/ppermute | solution.py:40
  148.9 2.7 %collective-permute-start.25 = (bf16[256,1024]{1,0:T(8,128)(2,1)}, bf16[256,1024]{1,0:T(8,128)(2,1)}, u32[]{:S(2)}, u32[]{:S(2)}) collective-permute-start(bf16[256,1024]{1,0:T(8,128)(2,1)} %collective-permute-done.23.refs_9_), channel_id=1, source_target_pairs={{2,0},{4,2},{6,4},{0,6},{10,8},{12,10},{14,12},{8,14},{18,16},{20,... | collective-permute-start | bytes 1572872 | tf_op jit(solution)/shard_map/ppermute | solution.py:40
  151.6 0.8 collective-permute-start.27
  153.0 1.0 tile.8
  154.0 1.4 tile.9.refs_17_
  155.5 9.4 %shard_map.118.refs_20_ = bf16[256,5120]{1,0:T(8,128)(2,1)} custom-call(s32[9]{0:T(128)S(1)} %stack.84.s_ref, bf16[256,1024]{1,0:T(8,128)(2,1)S(1)} %shard_map.117.key_ref.refs_8_, bf16[640,1024]{1,0:T(8,128)(2,1)} %own_ref.1, bf16[640,512]{1,0:T(8,128)(2,1)S(1)} %copy-done.7, bf16[640,512]{1,0:T(8,128)(2,1)} %collective-permute-done.8.refs_5_.refs_1_, ...), custom_call_target="tpu_custom_call" | custom-call | flops 2684354560 | bytes 13107200 | tf_op jit(solution)/shard_map/pallas_call | solution.py:205
  165.0 0.8 collective-permute-done.27.refs_13_
  165.8 8.3 %collective-permute-done.29.refs_15_ = bf16[256,1024]{1,0:T(8,128)(2,1)} collective-permute-done((bf16[256,1024]{1,0:T(8,128)(2,1)}, bf16[256,1024]{1,0:T(8,128)(2,1)}, u32[]{:S(2)}, u32[]{:S(2)}) %collective-permute-start.29) | collective-permute-done | bytes 524320 | tf_op jit(solution)/shard_map/ppermute | solution.py:40
  174.2 10.2 %shard_map.120 = (f32[640,1024]{1,0:T(8,128)}, f32[4,320,128]{2,1,0:T(8,128)}) custom-call(bf16[640,256]{1,0:T(8,128)(2,1)S(1)} %copy-done.23, bf16[640,256]{1,0:T(8,128)(2,1)} %collective-permute-done.16.refs_1_, bf16[640,256]{1,0:T(8,128)(2,1)S(1)} %copy-done.25, bf16[640,256]{1,0:T(8,128)(2,1)S(1)} %copy-done.27, bf16[640,256]{1,0:T(8,128)(2,1)S(1)} %copy-done.29, ...), custom_call_target="tpu_custom_call" | custom-call | flops 2684354560 | bytes 12058624 | tf_op jit(solution)/shard_map/pallas_call | solution.py:260
  184.4 1.1 fusion.3
  186.2 2.7 %collective-permute-start.31 = (bf16[320,128]{1,0:T(8,128)(2,1)S(1)}, bf16[320,128]{1,0:T(8,128)(2,1)S(1)}, u32[]{:S(2)}, u32[]{:S(2)}) collective-permute-start(bf16[320,128]{1,0:T(8,128)(2,1)S(1)} %get-tuple-element.29), channel_id=1, source_target_pairs={{24,0},{26,2},{28,4},{30,6},{16,8},{18,10},{20,12},{22,14},{8,16},... | collective-permute-start | bytes 245768 | tf_op jit(solution)/shard_map/ppermute | solution.py:40
  188.9 3.8 %collective-permute-done.31 = bf16[320,128]{1,0:T(8,128)(2,1)S(1)} collective-permute-done((bf16[320,128]{1,0:T(8,128)(2,1)S(1)}, bf16[320,128]{1,0:T(8,128)(2,1)S(1)}, u32[]{:S(2)}, u32[]{:S(2)}) %collective-permute-start.31) | collective-permute-done | bytes 81952 | tf_op jit(solution)/shard_map/ppermute | solution.py:40
  192.7 1.0 fusion.2
  193.8 4.0 %collective-permute-done.33 = bf16[320,128]{1,0:T(8,128)(2,1)S(1)} collective-permute-done((bf16[320,128]{1,0:T(8,128)(2,1)S(1)}, bf16[320,128]{1,0:T(8,128)(2,1)S(1)}, u32[]{:S(2)}, u32[]{:S(2)}) %collective-permute-start.33) | collective-permute-done | bytes 81952 | tf_op jit(solution)/shard_map/ppermute | solution.py:40
  197.8 1.3 collective-permute-start.34
  199.1 5.6 %collective-permute-done.34 = bf16[320,128]{1,0:T(8,128)(2,1)S(1)} collective-permute-done((bf16[320,128]{1,0:T(8,128)(2,1)S(1)}, bf16[320,128]{1,0:T(8,128)(2,1)S(1)}, u32[]{:S(2)}, u32[]{:S(2)}) %collective-permute-start.34) | collective-permute-done | bytes 81952 | tf_op jit(solution)/shard_map/ppermute | solution.py:40
  204.8 3.3 %collective-permute-start.35 = (bf16[320,128]{1,0:T(8,128)(2,1)S(1)}, bf16[320,128]{1,0:T(8,128)(2,1)S(1)}, u32[]{:S(2)}, u32[]{:S(2)}) collective-permute-start(bf16[320,128]{1,0:T(8,128)(2,1)S(1)} %add_convert_fusion.1), channel_id=1, source_target_pairs={{128,0},{130,2},{132,4},{134,6},{136,8},{138,10},{140,12},{142,14}... | collective-permute-start | bytes 245768 | tf_op jit(solution)/shard_map/ppermute | solution.py:40
  208.0 5.5 %collective-permute-done.35 = bf16[320,128]{1,0:T(8,128)(2,1)S(1)} collective-permute-done((bf16[320,128]{1,0:T(8,128)(2,1)S(1)}, bf16[320,128]{1,0:T(8,128)(2,1)S(1)}, u32[]{:S(2)}, u32[]{:S(2)}) %collective-permute-start.35) | collective-permute-done | bytes 81952 | tf_op jit(solution)/shard_map/ppermute | solution.py:40
  213.5 1.1 collective-permute-start.36
  214.6 1.7 collective-permute-start.38
  216.4 1.7 copy-done.14
  218.1 1.1 copy-done.16
  219.2 3.9 %shard_map.121 = f32[640,1024]{1,0:T(8,128)} custom-call(f32[640,1024]{1,0:T(8,128)S(1)} %copy-done.14, f32[4,320,128]{2,1,0:T(8,128)S(1)} %copy-done.16, bf16[2,64,128]{2,1,0:T(8,128)(2,1)S(1)} %copy-done.34, bf16[2,256,128]{2,1,0:T(8,128)(2,1)S(1)} %copy-done.17), custom_call_target="tpu_custom_call" | custom-call | flops 335544320 | bytes 5242880 | tf_op jit(solution)/shard_map/pallas_call | solution.py:280
  223.1 3.3 %shard_map.122 = bf16[640,1024]{1,0:T(8,128)(2,1)} custom-call(s32[1]{0:T(128)} %bitcast.22.me_ref, bf16[320,128]{1,0:T(8,128)(2,1)S(1)} %add_convert_fusion.a, bf16[320,128]{1,0:T(8,128)(2,1)S(1)} %collective-permute-done.36.b, bf16[320,128]{1,0:T(8,128)(2,1)S(1)} %collective-permute-done.37.c, bf16[320,128]{1,0:T(8,128)(2,1)S(1)} %collective-permute-done.38.d, ...), custom_call_target="tpu_custom_call" | custom-call | tf_op jit(solution)/shard_map/pallas_call | solution.py:309
  (131 shorter events, 10.2 us)
Async XLA Ops:
  0.6 71.3 %copy-start = (bf16[1,256,5120]{2,1,0:T(8,128)(2,1)S(1)}, bf16[1,256,5120]{2,1,0:T(8,128)(2,1)}, u32[]{:S(2)}) copy-start(bf16[1,256,5120]{2,1,0:T(8,128)(2,1)} %param.9) | copy-start | bytes 7864324
  0.8 1.5 copy-start.1
  3.7 13.3 %collective-permute-start.2 = (bf16[640,512]{1,0:T(8,128)(2,1)S(1)}, bf16[640,512]{1,0:T(8,128)(2,1)S(1)}, u32[]{:S(2)}, u32[]{:S(2)}) collective-permute-start(bf16[640,512]{1,0:T(8,128)(2,1)S(1)} %get-tuple-element.15.refs_9_), channel_id=1, source_target_pairs={{2,0},{4,2},{6,4},{0,6},{27,8},{29,10},{31,12},{25,14},{18,16},{20... | collective-permute-start | bytes 1966088 | tf_op jit(solution)/shard_map/ppermute | solution.py:40
  9.5 15.5 %collective-permute-start.4 = (bf16[640,512]{1,0:T(8,128)(2,1)S(1)}, bf16[640,512]{1,0:T(8,128)(2,1)S(1)}, u32[]{:S(2)}, u32[]{:S(2)}) collective-permute-start(bf16[640,512]{1,0:T(8,128)(2,1)S(1)} %get-tuple-element.15.refs_9_), channel_id=1, source_target_pairs={{4,0},{6,2},{0,4},{2,6},{29,8},{31,10},{25,12},{27,14},{20,16},{22... | collective-permute-start | bytes 1966088 | tf_op jit(solution)/shard_map/ppermute | solution.py:40
  9.7 22.4 %collective-permute-start.6 = (bf16[640,512]{1,0:T(8,128)(2,1)S(1)}, bf16[640,512]{1,0:T(8,128)(2,1)}, u32[]{:S(2)}, u32[]{:S(2)}) collective-permute-start(bf16[640,512]{1,0:T(8,128)(2,1)S(1)} %get-tuple-element.15.refs_9_), channel_id=1, source_target_pairs={{6,0},{0,2},{2,4},{4,6},{31,8},{25,10},{27,12},{29,14},{22,16},{16... | collective-permute-start | bytes 1966088 | tf_op jit(solution)/shard_map/ppermute | solution.py:40
  12.6 26.6 %collective-permute-start = (bf16[640,512]{1,0:T(8,128)(2,1)S(1)}, bf16[640,512]{1,0:T(8,128)(2,1)S(1)}, u32[]{:S(2)}, u32[]{:S(2)}) collective-permute-start(bf16[640,512]{1,0:T(8,128)(2,1)S(1)} %get-tuple-element.15.refs_9_), channel_id=1, source_target_pairs={{25,8},{27,10},{29,12},{31,14},{9,24},{11,26},{13,28},{15,30},{24,... | collective-permute-start | bytes 1966088 | tf_op jit(solution)/shard_map/ppermute | solution.py:40
  17.0 34.6 %collective-permute-start.10 = (bf16[640,512]{1,0:T(8,128)(2,1)S(1)}, bf16[640,512]{1,0:T(8,128)(2,1)}, u32[]{:S(2)}, u32[]{:S(2)}) collective-permute-start(bf16[640,512]{1,0:T(8,128)(2,1)S(1)} %collective-permute-done.2.refs_6_.refs_2_), channel_id=1, source_target_pairs={{32,0},{34,2},{36,4},{38,6},{232,8},{234,10},{236,12},{238,14},{48... | collective-permute-start | bytes 1966088 | tf_op jit(solution)/shard_map/ppermute | solution.py:40
  24.9 26.7 %collective-permute-start.12 = (bf16[640,512]{1,0:T(8,128)(2,1)S(1)}, bf16[640,512]{1,0:T(8,128)(2,1)}, u32[]{:S(2)}, u32[]{:S(2)}) collective-permute-start(bf16[640,512]{1,0:T(8,128)(2,1)S(1)} %collective-permute-done.4.refs_7_.refs_4_), channel_id=1, source_target_pairs={{32,0},{34,2},{36,4},{38,6},{232,8},{234,10},{236,12},{238,14},{48... | collective-permute-start | bytes 1966088 | tf_op jit(solution)/shard_map/ppermute | solution.py:40
  32.2 27.1 %collective-permute-start.14 = (bf16[640,512]{1,0:T(8,128)(2,1)}, bf16[640,512]{1,0:T(8,128)(2,1)}, u32[]{:S(2)}, u32[]{:S(2)}) collective-permute-start(bf16[640,512]{1,0:T(8,128)(2,1)} %collective-permute-done.6.refs_8_.refs_6_), channel_id=1, source_target_pairs={{32,0},{34,2},{36,4},{38,6},{232,8},{234,10},{236,12},{238,14},{48... | collective-permute-start | bytes 1966088 | tf_op jit(solution)/shard_map/ppermute | solution.py:40
  39.2 26.3 %collective-permute-start.8 = (bf16[640,512]{1,0:T(8,128)(2,1)S(1)}, bf16[640,512]{1,0:T(8,128)(2,1)}, u32[]{:S(2)}, u32[]{:S(2)}) collective-permute-start(bf16[640,512]{1,0:T(8,128)(2,1)S(1)} %collective-permute-done.refs_5_.refs_0_), channel_id=1, source_target_pairs={{232,8},{234,10},{236,12},{238,14},{248,24},{250,26},{252,28},{254... | collective-permute-start | bytes 1966088 | tf_op jit(solution)/shard_map/ppermute | solution.py:40
  42.8 22.7 %collective-permute-start.1 = (bf16[640,512]{1,0:T(8,128)(2,1)S(1)}, bf16[640,512]{1,0:T(8,128)(2,1)S(1)}, u32[]{:S(2)}, u32[]{:S(2)}) collective-permute-start(bf16[640,512]{1,0:T(8,128)(2,1)S(1)} %collective-permute-done.refs_5_.refs_0_), channel_id=1, source_target_pairs={{8,0},{10,2},{12,4},{14,6},{24,16},{26,18},{28,20},{30,22},{9,1},{... | collective-permute-start | bytes 1966088 | tf_op jit(solution)/shard_map/ppermute | solution.py:40
  51.6 15.2 %collective-permute-start.3 = (bf16[640,512]{1,0:T(8,128)(2,1)S(1)}, bf16[640,512]{1,0:T(8,128)(2,1)S(1)}, u32[]{:S(2)}, u32[]{:S(2)}) collective-permute-start(bf16[640,512]{1,0:T(8,128)(2,1)S(1)} %collective-permute-done.2.refs_6_.refs_2_), channel_id=1, source_target_pairs={{8,0},{10,2},{12,4},{14,6},{0,8},{2,10},{4,12},{6,14},{24,16},{26,... | collective-permute-start | bytes 1966088 | tf_op jit(solution)/shard_map/ppermute | solution.py:40
  51.6 16.1 %collective-permute-start.5 = (bf16[640,512]{1,0:T(8,128)(2,1)S(1)}, bf16[640,512]{1,0:T(8,128)(2,1)S(1)}, u32[]{:S(2)}, u32[]{:S(2)}) collective-permute-start(bf16[640,512]{1,0:T(8,128)(2,1)S(1)} %collective-permute-done.4.refs_7_.refs_4_), channel_id=1, source_target_pairs={{8,0},{10,2},{12,4},{14,6},{0,8},{2,10},{4,12},{6,14},{24,16},{26,... | collective-permute-start | bytes 1966088 | tf_op jit(solution)/shard_map/ppermute | solution.py:40
  59.3 17.8 %collective-permute-start.7 = (bf16[640,512]{1,0:T(8,128)(2,1)}, bf16[640,512]{1,0:T(8,128)(2,1)}, u32[]{:S(2)}, u32[]{:S(2)}) collective-permute-start(bf16[640,512]{1,0:T(8,128)(2,1)} %collective-permute-done.6.refs_8_.refs_6_), channel_id=1, source_target_pairs={{8,0},{10,2},{12,4},{14,6},{0,8},{2,10},{4,12},{6,14},{24,16},{26,... | collective-permute-start | bytes 1966088 | tf_op jit(solution)/shard_map/ppermute | solution.py:40
  65.5 20.8 %collective-permute-start.11 = (bf16[640,512]{1,0:T(8,128)(2,1)}, bf16[640,512]{1,0:T(8,128)(2,1)}, u32[]{:S(2)}, u32[]{:S(2)}) collective-permute-start(bf16[640,512]{1,0:T(8,128)(2,1)} %collective-permute-done.10.refs_6_.refs_3_), channel_id=1, source_target_pairs={{8,0},{10,2},{12,4},{14,6},{0,8},{2,10},{4,12},{6,14},{24,16},{26,... | collective-permute-start | bytes 1966088 | tf_op jit(solution)/shard_map/ppermute | solution.py:40
  66.4 23.5 %collective-permute-start.13 = (bf16[640,512]{1,0:T(8,128)(2,1)}, bf16[640,512]{1,0:T(8,128)(2,1)}, u32[]{:S(2)}, u32[]{:S(2)}) collective-permute-start(bf16[640,512]{1,0:T(8,128)(2,1)} %collective-permute-done.12.refs_7_.refs_5_), channel_id=1, source_target_pairs={{8,0},{10,2},{12,4},{14,6},{0,8},{2,10},{4,12},{6,14},{24,16},{26,... | collective-permute-start | bytes 1966088 | tf_op jit(solution)/shard_map/ppermute | solution.py:40
  67.7 22.4 %collective-permute-start.15 = (bf16[640,512]{1,0:T(8,128)(2,1)}, bf16[640,512]{1,0:T(8,128)(2,1)}, u32[]{:S(2)}, u32[]{:S(2)}) collective-permute-start(bf16[640,512]{1,0:T(8,128)(2,1)} %collective-permute-done.14.refs_8_.refs_7_), channel_id=1, source_target_pairs={{8,0},{10,2},{12,4},{14,6},{0,8},{2,10},{4,12},{6,14},{24,16},{26,... | collective-permute-start | bytes 1966088 | tf_op jit(solution)/shard_map/ppermute | solution.py:40
  68.6 28.7 %collective-permute-start.9 = (bf16[640,512]{1,0:T(8,128)(2,1)}, bf16[640,512]{1,0:T(8,128)(2,1)}, u32[]{:S(2)}, u32[]{:S(2)}) collective-permute-start(bf16[640,512]{1,0:T(8,128)(2,1)} %collective-permute-done.8.refs_5_.refs_1_), channel_id=1, source_target_pairs={{8,0},{10,2},{12,4},{14,6},{24,16},{26,18},{28,20},{30,22},{9,1},{... | collective-permute-start | bytes 1966088 | tf_op jit(solution)/shard_map/ppermute | solution.py:40
  77.1 26.8 %collective-permute-start.16 = (bf16[640,256]{1,0:T(8,128)(2,1)}, bf16[640,256]{1,0:T(8,128)(2,1)}, u32[]{:S(2)}, u32[]{:S(2)}) collective-permute-start(bf16[640,256]{1,0:T(8,128)(2,1)} %get-tuple-element.18), channel_id=1, source_target_pairs={{1,0},{3,2},{5,4},{7,6},{9,8},{11,10},{13,12},{15,14},{17,16},{19,... | collective-permute-start | bytes 983048 | tf_op jit(solution)/shard_map/ppermute | solution.py:40
  83.0 3.3 %copy-start.42 = (bf16[640,256]{1,0:T(8,128)(2,1)S(1)}, bf16[640,256]{1,0:T(8,128)(2,1)}, u32[]{:S(2)}) copy-start(bf16[640,256]{1,0:T(8,128)(2,1)} %copy-done.41) | copy-start | bytes 983044
  83.0 6.8 %copy-start.40 = (bf16[640,256]{1,0:T(8,128)(2,1)S(1)}, bf16[640,256]{1,0:T(8,128)(2,1)}, u32[]{:S(2)}) copy-start(bf16[640,256]{1,0:T(8,128)(2,1)} %copy-done.39) | copy-start | bytes 983044
  83.0 7.1 %copy-start.38 = (bf16[640,256]{1,0:T(8,128)(2,1)S(1)}, bf16[640,256]{1,0:T(8,128)(2,1)}, u32[]{:S(2)}) copy-start(bf16[640,256]{1,0:T(8,128)(2,1)} %copy-done.37) | copy-start | bytes 983044
  83.0 7.1 %copy-start.19 = (bf16[640,512]{1,0:T(8,128)(2,1)S(1)}, bf16[640,512]{1,0:T(8,128)(2,1)}, u32[]{:S(2)}) copy-start(bf16[640,512]{1,0:T(8,128)(2,1)} %copy-done.18) | copy-start | bytes 1966084
  86.4 35.7 %collective-permute-start.17 = (bf16[640,256]{1,0:T(8,128)(2,1)S(1)}, bf16[640,256]{1,0:T(8,128)(2,1)S(1)}, u32[]{:S(2)}, u32[]{:S(2)}) collective-permute-start(bf16[640,256]{1,0:T(8,128)(2,1)S(1)} %copy-done.42), channel_id=1, source_target_pairs={{2,0},{4,2},{6,4},{0,6},{10,8},{12,10},{14,12},{8,14},{18,16},{20,... | collective-permute-start | bytes 983048 | tf_op jit(solution)/shard_map/ppermute | solution.py:40
  89.9 32.9 %collective-permute-start.18 = (bf16[640,256]{1,0:T(8,128)(2,1)S(1)}, bf16[640,256]{1,0:T(8,128)(2,1)S(1)}, u32[]{:S(2)}, u32[]{:S(2)}) collective-permute-start(bf16[640,256]{1,0:T(8,128)(2,1)S(1)} %copy-done.40), channel_id=1, source_target_pairs={{3,0},{5,2},{7,4},{1,6},{11,8},{13,10},{15,12},{9,14},{19,16},{21,... | collective-permute-start | bytes 983048 | tf_op jit(solution)/shard_map/ppermute | solution.py:40
  90.1 37.3 %collective-permute-start.19 = (bf16[640,256]{1,0:T(8,128)(2,1)S(1)}, bf16[640,256]{1,0:T(8,128)(2,1)S(1)}, u32[]{:S(2)}, u32[]{:S(2)}) collective-permute-start(bf16[640,256]{1,0:T(8,128)(2,1)S(1)} %copy-done.38), channel_id=1, source_target_pairs={{4,0},{6,2},{0,4},{2,6},{12,8},{14,10},{8,12},{10,14},{20,16},{22,... | collective-permute-start | bytes 983048 | tf_op jit(solution)/shard_map/ppermute | solution.py:40
  90.2 4.0 %copy-start.9 = (bf16[640,512]{1,0:T(8,128)(2,1)S(1)}, bf16[640,512]{1,0:T(8,128)(2,1)}, u32[]{:S(2)}) copy-start(bf16[640,512]{1,0:T(8,128)(2,1)} %copy-done.8) | copy-start | bytes 1966084
  90.2 4.0 %copy-start.11 = (bf16[640,512]{1,0:T(8,128)(2,1)S(1)}, bf16[640,512]{1,0:T(8,128)(2,1)}, u32[]{:S(2)}) copy-start(bf16[640,512]{1,0:T(8,128)(2,1)} %copy-done.10) | copy-start | bytes 1966084
  90.2 4.0 %copy-start.13 = (bf16[640,512]{1,0:T(8,128)(2,1)S(1)}, bf16[640,512]{1,0:T(8,128)(2,1)}, u32[]{:S(2)}) copy-start(bf16[640,512]{1,0:T(8,128)(2,1)} %copy-done.12) | copy-start | bytes 1966084
  97.2 3.7 %copy-start.15 = (bf16[1,256,1024]{2,1,0:T(8,128)(2,1)S(1)}, bf16[1,256,1024]{2,1,0:T(8,128)(2,1)}, u32[]{:S(2)}) copy-start(bf16[1,256,1024]{2,1,0:T(8,128)(2,1)} %param.10) | copy-start | bytes 1572868
  97.2 3.7 %copy-start.36 = (f32[1024]{0:T(1024)S(1)}, f32[1024]{0:T(1024)}, u32[]{:S(2)}) copy-start(f32[1024]{0:T(1024)} %param.13) | copy-start | bytes 12292
  100.9 51.6 %copy-start.43 = (s32[640]{0:T(1024)S(1)}, s32[640]{0:T(1024)}, u32[]{:S(2)}) copy-start(s32[640]{0:T(1024)} %param.14) | copy-start | bytes 7684
  100.9 54.6 %copy-start.4 = (bf16[640,512]{1,0:T(8,128)(2,1)S(1)}, bf16[640,512]{1,0:T(8,128)(2,1)}, u32[]{:S(2)}) copy-start(bf16[640,512]{1,0:T(8,128)(2,1)} %copy-done.2) | copy-start | bytes 1966084
  100.9 54.6 %copy-start.7 = (bf16[640,512]{1,0:T(8,128)(2,1)S(1)}, bf16[640,512]{1,0:T(8,128)(2,1)}, u32[]{:S(2)}) copy-start(bf16[640,512]{1,0:T(8,128)(2,1)} %copy-done.5) | copy-start | bytes 1966084
  101.3 47.5 %collective-permute-start.23 = (bf16[256,1024]{1,0:T(8,128)(2,1)S(1)}, bf16[256,1024]{1,0:T(8,128)(2,1)}, u32[]{:S(2)}, u32[]{:S(2)}) collective-permute-start(bf16[256,1024]{1,0:T(8,128)(2,1)S(1)} %shard_map.117.key_ref.refs_8_), channel_id=1, source_target_pairs={{1,0},{3,2},{5,4},{7,6},{9,8},{11,10},{13,12},{15,14},{17,16},{19,... | collective-permute-start | bytes 1572872 | tf_op jit(solution)/shard_map/ppermute | solution.py:40
  103.9 47.6 %collective-permute-start.26 = (bf16[256,1024]{1,0:T(8,128)(2,1)S(1)}, bf16[256,1024]{1,0:T(8,128)(2,1)}, u32[]{:S(2)}, u32[]{:S(2)}) collective-permute-start(bf16[256,1024]{1,0:T(8,128)(2,1)S(1)} %shard_map.117.key_ref.refs_8_), channel_id=1, source_target_pairs={{4,0},{6,2},{0,4},{2,6},{12,8},{14,10},{8,12},{10,14},{20,16},{22,... | collective-permute-start | bytes 1572872 | tf_op jit(solution)/shard_map/ppermute | solution.py:40
  122.8 15.5 %collective-permute-start.20 = (bf16[640,256]{1,0:T(8,128)(2,1)}, bf16[640,256]{1,0:T(8,128)(2,1)S(1)}, u32[]{:S(2)}, u32[]{:S(2)}) collective-permute-start(bf16[640,256]{1,0:T(8,128)(2,1)} %get-tuple-element.22), channel_id=1, source_target_pairs={{5,0},{7,2},{1,4},{3,6},{13,8},{15,10},{9,12},{11,14},{21,16},{23,... | collective-permute-start | bytes 983048 | tf_op jit(solution)/shard_map/ppermute | solution.py:40
  123.5 25.3 %collective-permute-start.21 = (bf16[640,256]{1,0:T(8,128)(2,1)}, bf16[640,256]{1,0:T(8,128)(2,1)S(1)}, u32[]{:S(2)}, u32[]{:S(2)}) collective-permute-start(bf16[640,256]{1,0:T(8,128)(2,1)} %get-tuple-element.23), channel_id=1, source_target_pairs={{6,0},{0,2},{2,4},{4,6},{14,8},{8,10},{10,12},{12,14},{22,16},{16,... | collective-permute-start | bytes 983048 | tf_op jit(solution)/shard_map/ppermute | solution.py:40
  128.1 23.4 %collective-permute-start.22 = (bf16[640,256]{1,0:T(8,128)(2,1)}, bf16[640,256]{1,0:T(8,128)(2,1)}, u32[]{:S(2)}, u32[]{:S(2)}) collective-permute-start(bf16[640,256]{1,0:T(8,128)(2,1)} %get-tuple-element.24), channel_id=1, source_target_pairs={{7,0},{1,2},{3,4},{5,6},{15,8},{9,10},{11,12},{13,14},{23,16},{17,... | collective-permute-start | bytes 983048 | tf_op jit(solution)/shard_map/ppermute | solution.py:40
  139.0 26.0 %collective-permute-start.24 = (bf16[256,1024]{1,0:T(8,128)(2,1)S(1)}, bf16[256,1024]{1,0:T(8,128)(2,1)}, u32[]{:S(2)}, u32[]{:S(2)}) collective-permute-start(bf16[256,1024]{1,0:T(8,128)(2,1)S(1)} %shard_map.117.key_ref.refs_8_), channel_id=1, source_target_pairs={{2,0},{4,2},{6,4},{0,6},{10,8},{12,10},{14,12},{8,14},{18,16},{20,... | collective-permute-start | bytes 1572872 | tf_op jit(solution)/shard_map/ppermute | solution.py:40
  148.9 6.6 %copy-start.32 = (bf16[640,256]{1,0:T(8,128)(2,1)}, bf16[640,256]{1,0:T(8,128)(2,1)S(1)}, u32[]{:S(2)}) copy-start(bf16[640,256]{1,0:T(8,128)(2,1)S(1)} %collective-permute-done.21.refs_6_) | copy-start | bytes 983044
  148.9 16.1 %collective-permute-start.28 = (bf16[256,1024]{1,0:T(8,128)(2,1)S(1)}, bf16[256,1024]{1,0:T(8,128)(2,1)}, u32[]{:S(2)}, u32[]{:S(2)}) collective-permute-start(bf16[256,1024]{1,0:T(8,128)(2,1)S(1)} %shard_map.117.key_ref.refs_8_), channel_id=1, source_target_pairs={{6,0},{0,2},{2,4},{4,6},{14,8},{8,10},{10,12},{12,14},{22,16},{16,... | collective-permute-start | bytes 1572872 | tf_op jit(solution)/shard_map/ppermute | solution.py:40
  148.9 16.1 %collective-permute-start.25 = (bf16[256,1024]{1,0:T(8,128)(2,1)}, bf16[256,1024]{1,0:T(8,128)(2,1)}, u32[]{:S(2)}, u32[]{:S(2)}) collective-permute-start(bf16[256,1024]{1,0:T(8,128)(2,1)} %collective-permute-done.23.refs_9_), channel_id=1, source_target_pairs={{2,0},{4,2},{6,4},{0,6},{10,8},{12,10},{14,12},{8,14},{18,16},{20,... | collective-permute-start | bytes 1572872 | tf_op jit(solution)/shard_map/ppermute | solution.py:40
  151.5 22.6 %collective-permute-start.29 = (bf16[256,1024]{1,0:T(8,128)(2,1)}, bf16[256,1024]{1,0:T(8,128)(2,1)}, u32[]{:S(2)}, u32[]{:S(2)}) collective-permute-start(bf16[256,1024]{1,0:T(8,128)(2,1)} %collective-permute-done.23.refs_9_), channel_id=1, source_target_pairs={{6,0},{0,2},{2,4},{4,6},{14,8},{8,10},{10,12},{12,14},{22,16},{16,... | collective-permute-start | bytes 1572872 | tf_op jit(solution)/shard_map/ppermute | solution.py:40
  151.6 14.3 %collective-permute-start.27 = (bf16[256,1024]{1,0:T(8,128)(2,1)}, bf16[256,1024]{1,0:T(8,128)(2,1)}, u32[]{:S(2)}, u32[]{:S(2)}) collective-permute-start(bf16[256,1024]{1,0:T(8,128)(2,1)} %collective-permute-done.26.refs_12_), channel_id=1, source_target_pairs={{1,0},{3,2},{5,4},{7,6},{9,8},{11,10},{13,12},{15,14},{17,16},{19,... | collective-permute-start | bytes 1572872 | tf_op jit(solution)/shard_map/ppermute | solution.py:40
  155.4 18.7 %copy-start.17 = (bf16[2,256,128]{2,1,0:T(8,128)(2,1)S(1)}, bf16[2,256,128]{2,1,0:T(8,128)(2,1)}, u32[]{:S(2)}) copy-start(bf16[2,256,128]{2,1,0:T(8,128)(2,1)} %constant.140.clone.refs_19_.right_ref) | copy-start | bytes 393220
  155.5 18.7 %copy-start.23 = (bf16[640,256]{1,0:T(8,128)(2,1)S(1)}, bf16[640,256]{1,0:T(8,128)(2,1)}, u32[]{:S(2)}) copy-start(bf16[640,256]{1,0:T(8,128)(2,1)} %copy-done.22) | copy-start | bytes 983044
  155.5 18.7 %copy-start.25 = (bf16[640,256]{1,0:T(8,128)(2,1)S(1)}, bf16[640,256]{1,0:T(8,128)(2,1)}, u32[]{:S(2)}) copy-start(bf16[640,256]{1,0:T(8,128)(2,1)} %copy-done.24) | copy-start | bytes 983044
  155.5 18.7 %copy-start.27 = (bf16[640,256]{1,0:T(8,128)(2,1)S(1)}, bf16[640,256]{1,0:T(8,128)(2,1)}, u32[]{:S(2)}) copy-start(bf16[640,256]{1,0:T(8,128)(2,1)} %copy-done.26) | copy-start | bytes 983044
  155.5 18.7 %copy-start.29 = (bf16[640,256]{1,0:T(8,128)(2,1)S(1)}, bf16[640,256]{1,0:T(8,128)(2,1)}, u32[]{:S(2)}) copy-start(bf16[640,256]{1,0:T(8,128)(2,1)} %copy-done.28) | copy-start | bytes 983044
  155.5 18.7 %copy-start.31 = (bf16[640,256]{1,0:T(8,128)(2,1)S(1)}, bf16[640,256]{1,0:T(8,128)(2,1)}, u32[]{:S(2)}) copy-start(bf16[640,256]{1,0:T(8,128)(2,1)} %copy-done.30) | copy-start | bytes 983044
  155.5 18.7 %copy-start.33 = (bf16[640,256]{1,0:T(8,128)(2,1)S(1)}, bf16[640,256]{1,0:T(8,128)(2,1)}, u32[]{:S(2)}) copy-start(bf16[640,256]{1,0:T(8,128)(2,1)} %copy-done.32) | copy-start | bytes 983044
  155.5 18.7 %copy-start.34 = (bf16[2,64,128]{2,1,0:T(8,128)(2,1)S(1)}, bf16[2,64,128]{2,1,0:T(8,128)(2,1)}, u32[]{:S(2)}) copy-start(bf16[2,64,128]{2,1,0:T(8,128)(2,1)} %constant.139.clone.refs_18_.left_ref) | copy-start | bytes 98308
  185.6 3.4 %collective-permute-start.30 = (bf16[320,128]{1,0:T(8,128)(2,1)S(1)}, bf16[320,128]{1,0:T(8,128)(2,1)S(1)}, u32[]{:S(2)}, u32[]{:S(2)}) collective-permute-start(bf16[320,128]{1,0:T(8,128)(2,1)S(1)} %get-tuple-element.27), channel_id=1, source_target_pairs={{16,0},{18,2},{20,4},{22,6},{24,8},{26,10},{28,12},{30,14},{0,16},... | collective-permute-start | bytes 245768 | tf_op jit(solution)/shard_map/ppermute | solution.py:40
  186.2 6.5 %collective-permute-start.31 = (bf16[320,128]{1,0:T(8,128)(2,1)S(1)}, bf16[320,128]{1,0:T(8,128)(2,1)S(1)}, u32[]{:S(2)}, u32[]{:S(2)}) collective-permute-start(bf16[320,128]{1,0:T(8,128)(2,1)S(1)} %get-tuple-element.29), channel_id=1, source_target_pairs={{24,0},{26,2},{28,4},{30,6},{16,8},{18,10},{20,12},{22,14},{8,16},... | collective-permute-start | bytes 245768 | tf_op jit(solution)/shard_map/ppermute | solution.py:40
  188.9 3.9 %collective-permute-start.32 = (bf16[320,128]{1,0:T(8,128)(2,1)S(1)}, bf16[320,128]{1,0:T(8,128)(2,1)S(1)}, u32[]{:S(2)}, u32[]{:S(2)}) collective-permute-start(bf16[320,128]{1,0:T(8,128)(2,1)S(1)} %get-tuple-element.28), channel_id=1, source_target_pairs={{8,0},{10,2},{12,4},{14,6},{0,8},{2,10},{4,12},{6,14},{24,16},{26,... | collective-permute-start | bytes 245768 | tf_op jit(solution)/shard_map/ppermute | solution.py:40
  193.7 4.1 %collective-permute-start.33 = (bf16[320,128]{1,0:T(8,128)(2,1)S(1)}, bf16[320,128]{1,0:T(8,128)(2,1)S(1)}, u32[]{:S(2)}, u32[]{:S(2)}) collective-permute-start(bf16[320,128]{1,0:T(8,128)(2,1)S(1)} %fusion.2), channel_id=1, source_target_pairs={{32,0},{34,2},{36,4},{38,6},{40,8},{42,10},{44,12},{46,14},{48,16}... | collective-permute-start | bytes 245768 | tf_op jit(solution)/shard_map/ppermute | solution.py:40
  197.8 6.9 %collective-permute-start.34 = (bf16[320,128]{1,0:T(8,128)(2,1)S(1)}, bf16[320,128]{1,0:T(8,128)(2,1)S(1)}, u32[]{:S(2)}, u32[]{:S(2)}) collective-permute-start(bf16[320,128]{1,0:T(8,128)(2,1)S(1)} %add_convert_fusion.2), channel_id=1, source_target_pairs={{64,0},{66,2},{68,4},{70,6},{72,8},{74,10},{76,12},{78,14},{80,16}... | collective-permute-start | bytes 245768 | tf_op jit(solution)/shard_map/ppermute | solution.py:40
  204.8 8.7 %collective-permute-start.35 = (bf16[320,128]{1,0:T(8,128)(2,1)S(1)}, bf16[320,128]{1,0:T(8,128)(2,1)S(1)}, u32[]{:S(2)}, u32[]{:S(2)}) collective-permute-start(bf16[320,128]{1,0:T(8,128)(2,1)S(1)} %add_convert_fusion.1), channel_id=1, source_target_pairs={{128,0},{130,2},{132,4},{134,6},{136,8},{138,10},{140,12},{142,14}... | collective-permute-start | bytes 245768 | tf_op jit(solution)/shard_map/ppermute | solution.py:40
  213.5 9.5 %collective-permute-start.36 = (bf16[320,128]{1,0:T(8,128)(2,1)S(1)}, bf16[320,128]{1,0:T(8,128)(2,1)S(1)}, u32[]{:S(2)}, u32[]{:S(2)}) collective-permute-start(bf16[320,128]{1,0:T(8,128)(2,1)S(1)} %add_convert_fusion.a), channel_id=1, source_target_pairs={{8,0},{10,2},{12,4},{14,6},{0,8},{2,10},{4,12},{6,14},{24,16},{26,... | collective-permute-start | bytes 245768 | tf_op jit(solution)/shard_map/ppermute | solution.py:40
  214.6 8.4 %collective-permute-start.37 = (bf16[320,128]{1,0:T(8,128)(2,1)S(1)}, bf16[320,128]{1,0:T(8,128)(2,1)S(1)}, u32[]{:S(2)}, u32[]{:S(2)}) collective-permute-start(bf16[320,128]{1,0:T(8,128)(2,1)S(1)} %add_convert_fusion.a), channel_id=1, source_target_pairs={{16,0},{18,2},{20,4},{22,6},{24,8},{26,10},{28,12},{30,14},{0,16},... | collective-permute-start | bytes 245768 | tf_op jit(solution)/shard_map/ppermute | solution.py:40
  214.6 8.4 %collective-permute-start.38 = (bf16[320,128]{1,0:T(8,128)(2,1)S(1)}, bf16[320,128]{1,0:T(8,128)(2,1)S(1)}, u32[]{:S(2)}, u32[]{:S(2)}) collective-permute-start(bf16[320,128]{1,0:T(8,128)(2,1)S(1)} %add_convert_fusion.a), channel_id=1, source_target_pairs={{24,0},{26,2},{28,4},{30,6},{16,8},{18,10},{20,12},{22,14},{8,16},... | collective-permute-start | bytes 245768 | tf_op jit(solution)/shard_map/ppermute | solution.py:40
  216.4 1.7 copy-start.14
  219.2 3.9 %copy-start.35 = (bf16[128,128]{1,0:T(8,128)(2,1)S(1)}, bf16[128,128]{1,0:T(8,128)(2,1)}, u32[]{:S(2)}) copy-start(bf16[128,128]{1,0:T(8,128)(2,1)} %constant.141.clone.ones_ref) | copy-start | bytes 98308
  (19 other events, 16.1 us)

commit v2 on v1

v2 whole, which is shorter than its diff:
```python
import math

import jax
import jax.numpy as jnp
import numpy as np
from jax import lax
from jax.experimental import pallas as pl
from jax.experimental.pallas import tpu as pltpu
from jax.sharding import PartitionSpec as P

norm_epsilon = 1e-06
block_epsilon = 1e-06
decay_rate = 0.999
step_rate = 0.02

Z, XL, CORE, Y, XH = 8, 2, 2, 4, 2
X = XL * XH
TOK, D, KV, ROWS = 256, 5120, 1024, 640
HALF = KV // 2
bf16, f32 = jnp.bfloat16, jnp.float32
PARITY, IS_CORE1, ME, NEAR, FAR, AWAY_AT, OTHER_HALF = 0, 1, 2, 3, 7, 11, 19
AWAY = [(0, 0), (1, 0), (3, 0), (0, 1), (2, 0), (1, 1), (3, 1), (2, 1)]
STEPS = ((1, 0), (3, 1), (2, 3), (0, 2))
ANY = pl.BlockSpec(memory_space=pl.ANY)
VMEM = pl.BlockSpec(memory_space=pltpu.VMEM)
SMEM = pl.BlockSpec(memory_space=pltpu.SMEM)


def device_index(z, x, c, y):
    z, x, y = z % Z, x % X, y % Y
    return (((z * XL + x % XL) * CORE + c) * Y + y) * XH + x // XL


def pull(value, source):
    pairs = []
    for z in range(Z):
        for x in range(X):
            for c in range(CORE):
                for y in range(Y):
                    found = source(z, x, c, y)
                    if found is not None:
                        pairs.append((device_index(*found), device_index(z, x, c, y)))
    return lax.ppermute(value, ("rep", "shard"), pairs)


def from_shard(dy, dx):
    return lambda z, x, c, y: (z, x + 2 * dx, c, y + dy)


def split_bf16(table):
    high = table.astype(bf16)
    low = (table - high.astype(np.float32)).astype(bf16)
    return np.stack([high, low])


def dct_tables():
    freq = np.arange(64, dtype=np.float64)
    angle = math.pi * (2.0 * freq[None, :] + 1.0) * freq[:, None] / 128.0
    factor = np.where(freq[:, None] == 0.0, math.sqrt(1.0 / 64.0), math.sqrt(2.0 / 64.0))
    table = (factor * np.cos(angle))[:32].astype(np.float32)
    left = np.kron(np.eye(2, dtype=np.float32), table)
    right = np.kron(np.eye(4, dtype=np.float32), table.T)
    return split_bf16(left), split_bf16(right)


def split(value):
    high = value.astype(bf16)
    return high, (value - high.astype(f32)).astype(bf16)


def mm(a, b):
    return jnp.dot(a, b, preferred_element_type=f32)


def mm_left(table, value):
    high, low = split(value)
    return mm(table[0], high) + mm(table[0], low) + mm(table[1], high)


def mm_right(value, table):
    high, low = split(value)
    return mm(high, table[0]) + mm(low, table[0]) + mm(high, table[1])


def params(limit=56):
    return pltpu.CompilerParams(vmem_limit_bytes=limit * 1024 * 1024)


def cut_columns(info, value, slots, width, transposed=False, joined=False, after=()):
    rows, count = value.shape[0], len(slots)

    def kernel(info_ref, *refs):
        for k in range(count):
            block = refs[k][...]
            block = block.T if transposed else block
            if joined:
                refs[-1][:, width * k : width * k + width] = block
            else:
                refs[count + len(after) + k][...] = block

    shape = (rows, width * count) if joined else (width, rows) if transposed else (rows, width)
    outs = 1 if joined else count
    return pl.pallas_call(
        kernel,
        grid_spec=pltpu.PrefetchScalarGridSpec(
            num_scalar_prefetch=1,
            grid=(1,),
            in_specs=[pl.BlockSpec((rows, width), lambda i, s, k=k: (0, s[k])) for k in slots] + [ANY] * len(after),
            out_specs=[pl.BlockSpec(shape, lambda i, s: (0, 0))] * outs,
        ),
        out_shape=[jax.ShapeDtypeStruct(shape, value.dtype)] * outs,
        compiler_params=params(),
        cost_estimate=pl.CostEstimate(flops=0, bytes_accessed=4 * rows * width * count, transcendentals=0),
    )(info, *([value] * count), *after)


def column_half(ref, p):
    return ref[:, pl.ds(pl.multiple_of(p * HALF, HALF), HALF)]


def project(info, tokens, others, own, first, second, after):
    def kernel(info_ref, t_ref, o_ref, own_ref, *refs):
        ws, outs = refs[:8], refs[8 + len(after) : 10 + len(after)]
        toks, other, weights, sems = refs[10 + len(after) :]
        p, core = info_ref[PARITY], info_ref[IS_CORE1]
        copies = []

        def start(source, target):
            copies.append(pltpu.make_async_copy(source, target, sems.at[len(copies)]))
            copies[-1].start()

        start(o_ref, other)
        for k in range(4):
            at = pl.ds(pl.multiple_of(info_ref[NEAR + k] * ROWS, 128), ROWS)
            start(t_ref.at[:, at], toks.at[k])
        for k in range(4):
            for h in range(2):
                start(ws[4 * h + k], weights.at[2 * k + h])
        for copy in copies[:5]:
            copy.wait()
        sums = [[None, None], [None, None]]
        for k in range(4):
            for h in range(2):
                copies[5 + 2 * k + h].wait()
                w = weights[2 * k + h]
                if k == 3:
                    w = jnp.where(core == 0, column_half(own_ref, p if h == 0 else 1 - p), w)
                for n, t in enumerate((toks[k], other[:, ROWS * k : ROWS * k + ROWS])):
                    term = mm(t, w)
                    sums[n][h] = term if k == 0 else sums[n][h] + term
        for n in range(2):
            for h in range(2):
                outs[n][:, HALF * h : HALF * h + HALF] = sums[n][h]

    return pl.pallas_call(
        kernel,
        in_specs=[SMEM, ANY, ANY, VMEM] + [ANY] * (8 + len(after)),
        out_specs=[VMEM] * 2,
        out_shape=[jax.ShapeDtypeStruct((TOK, KV), f32)] * 2,
        scratch_shapes=[
            pltpu.VMEM((4, TOK, ROWS), bf16),
            pltpu.VMEM((TOK, 4 * ROWS), bf16),
            pltpu.VMEM((8, ROWS, HALF), bf16),
            pltpu.SemaphoreType.DMA((13,)),
        ],
        compiler_params=params(),
        cost_estimate=pl.CostEstimate(flops=2 * TOK * D * KV, bytes_accessed=(KV * D + TOK * D) * 2, transcendentals=0),
    )(info, tokens, others, own, *first, *second, *after)


def key_gradient(info, mine, arrived, cotangent, gain, after):
    def kernel(s_ref, m_ref, r_ref, ca_ref, cb_ref, ga_ref, gb_ref, *refs):
        out_ref = refs[-1]
        p = s_ref[PARITY]
        both = m_ref[...] + r_ref[...]
        a, b = both[:, :HALF], both[:, HALF:]
        sa = ca_ref[...].astype(f32) * ga_ref[...]
        sb = cb_ref[...].astype(f32) * gb_ref[...]
        square = jnp.sum(a * a, axis=-1, keepdims=True) + jnp.sum(b * b, axis=-1, keepdims=True)
        cross = jnp.sum(sa * a, axis=-1, keepdims=True) + jnp.sum(sb * b, axis=-1, keepdims=True)
        inverse = lax.rsqrt(square * (1.0 / KV) + norm_epsilon)
        factor = inverse * inverse * (cross * (1.0 / KV))
        out_ref[:, pl.ds(pl.multiple_of(p * HALF, HALF), HALF)] = (inverse * (sa - a * factor)).astype(bf16)
        out_ref[:, pl.ds(pl.multiple_of((1 - p) * HALF, HALF), HALF)] = (inverse * (sb - b * factor)).astype(bf16)

    full = pl.BlockSpec((TOK, KV), lambda i, s: (0, 0))
    return pl.pallas_call(
        kernel,
        grid_spec=pltpu.PrefetchScalarGridSpec(
            num_scalar_prefetch=1,
            grid=(1,),
            in_specs=[
                full,
                full,
                pl.BlockSpec((TOK, HALF), lambda i, s: (0, s[PARITY])),
                pl.BlockSpec((TOK, HALF), lambda i, s: (0, 1 - s[PARITY])),
                pl.BlockSpec((1, HALF), lambda i, s: (0, s[PARITY])),
                pl.BlockSpec((1, HALF), lambda i, s: (0, 1 - s[PARITY])),
            ]
            + [ANY] * len(after),
            out_specs=full,
        ),
        out_shape=jax.ShapeDtypeStruct((TOK, KV), bf16),
        compiler_params=params(),
        cost_estimate=pl.CostEstimate(flops=10 * TOK * KV, bytes_accessed=TOK * KV * 12, transcendentals=TOK),
    )(info, mine, arrived, cotangent, cotangent, gain, gain, *after)


def token_gradient(info, key_grad, other_keys, own, first, second, after):
    def kernel(info_ref, k_ref, o_ref, own_ref, *refs):
        ws, outs = refs[:8], refs[8 + len(after) :]
        p, core = info_ref[PARITY], info_ref[IS_CORE1]
        for k in range(4):
            wa, wb = ws[k][...], ws[4 + k][...]
            if k == 3:
                wa = jnp.where(core == 0, column_half(own_ref, p), wa)
                wb = jnp.where(core == 0, column_half(own_ref, 1 - p), wb)
            for keys, out in zip((k_ref, o_ref), outs):
                value = against(column_half(keys, p), wa) + against(column_half(keys, 1 - p), wb)
                out[:, ROWS * k : ROWS * k + ROWS] = value.astype(bf16)

    return pl.pallas_call(
        kernel,
        in_specs=[SMEM] + [VMEM] * 11 + [ANY] * len(after),
        out_specs=[VMEM] * 2,
        out_shape=[jax.ShapeDtypeStruct((TOK, 4 * ROWS), bf16)] * 2,
        compiler_params=params(),
        cost_estimate=pl.CostEstimate(flops=2 * TOK * KV * D, bytes_accessed=(KV * D + TOK * D) * 2, transcendentals=0),
    )(info, key_grad, other_keys, own, *first, *second, *after)


def place_columns(info, mine, arrived):
    def kernel(info_ref, m_ref, r_ref, out_ref):
        for slot, ref in ((NEAR, m_ref), (FAR, r_ref)):
            for k in range(4):
                at = pl.ds(pl.multiple_of(info_ref[slot + k] * ROWS, 128), ROWS)
                out_ref[:, at] = ref[:, ROWS * k : ROWS * k + ROWS]

    return pl.pallas_call(
        kernel,
        in_specs=[SMEM] + [VMEM] * 2,
        out_specs=VMEM,
        out_shape=jax.ShapeDtypeStruct((TOK, D), bf16),
        compiler_params=params(),
        cost_estimate=pl.CostEstimate(flops=0, bytes_accessed=4 * TOK * D, transcendentals=0),
    )(info, mine, arrived)


def against(a, b):
    return lax.dot_general(a, b, (((1,), (1,)), ((), ())), preferred_element_type=f32)


def across(a, b):
    return lax.dot_general(a, b, (((0,), (0,)), ((), ())), preferred_element_type=f32)


def to_corner(value, left, right):
    narrow = mm_right(value, right)
    return jnp.concatenate([mm_left(left, narrow[128 * i : 128 * i + 128]) for i in range(5)], axis=0)


def from_corner(corner, left, right):
    high, low = split(corner)
    blocks = []
    for i in range(5):
        h, l = high[64 * i : 64 * i + 64], low[64 * i : 64 * i + 64]
        blocks.append(across(left[0], h) + across(left[0], l) + across(left[1], h))
    high, low = split(jnp.concatenate(blocks, axis=0))
    return against(high, right[0]) + against(low, right[0]) + against(high, right[1])


def blend(info, tokens, keys, momentum, mask, tables, after):
    count = len(keys)
    width = 256

    def kernel(info_ref, *refs):
        toks, ks = refs[:count], refs[count : 2 * count]
        momentum_ref, mask_ref, left_ref, right_ref, _, blended_ref, corner_ref, *parts = refs[2 * count :]
        t = jnp.concatenate([ref[...] for ref in toks], axis=1)
        k = jnp.concatenate([ref[...] for ref in ks], axis=0)
        blended = decay_rate * momentum_ref[...] + step_rate * mm(t, k)
        blended_ref[...] = blended
        corner = to_corner(blended, left_ref[...], right_ref[...]) * mask_ref[...]
        corner_ref[0] = corner
        for i in range(4):

            @pl.when(pl.program_id(0) == i)
            def _():
                parts[i][...] = corner.astype(parts[i].dtype)

    def whole(a):
        return pl.BlockSpec(a.shape, lambda i, s: (0,) * a.ndim)

    columns = pl.BlockSpec((ROWS, width), lambda i, s: (0, s[ME] ^ i))
    specs = [pl.BlockSpec((ROWS, TOK), lambda i, s: (0, 0))] * count
    specs += [pl.BlockSpec((TOK, width), lambda i, s: (0, s[ME] ^ i))] * count
    specs += [columns, whole(mask), whole(tables[0]), whole(tables[1]), ANY]
    part = pl.BlockSpec((320, 128), lambda i, s: (0, 0))
    return pl.pallas_call(
        kernel,
        grid_spec=pltpu.PrefetchScalarGridSpec(
            num_scalar_prefetch=1,
            grid=(KV // width,),
            in_specs=specs,
            out_specs=[columns, pl.BlockSpec((1, 320, 128), lambda i, s: (s[ME] ^ i, 0, 0))] + [part] * 4,
        ),
        out_shape=[jax.ShapeDtypeStruct((ROWS, KV), f32), jax.ShapeDtypeStruct((4, 320, 128), f32)]
        + [jax.ShapeDtypeStruct((320, 128), t) for t in (f32, bf16, bf16, bf16)],
        compiler_params=params(),
        cost_estimate=pl.CostEstimate(
            flops=2 * TOK * count * KV * ROWS, bytes_accessed=ROWS * KV * 8 + count * TOK * (ROWS + KV) * 2, transcendentals=0
        ),
    )(info, *tokens, *keys, momentum, mask, *tables, after)


def remove_corner(blended, corner, tables):
    def kernel(blended_ref, corner_ref, left_ref, right_ref, out_ref):
        out_ref[...] = blended_ref[...] - from_corner(corner_ref[0], left_ref[...], right_ref[...])

    return pl.pallas_call(
        kernel,
        grid=(4,),
        in_specs=[
            pl.BlockSpec((ROWS, 256), lambda i: (0, i)),
            pl.BlockSpec((1, 320, 128), lambda i: (i, 0, 0)),
            pl.BlockSpec(tables[0].shape, lambda i: (0, 0, 0)),
            pl.BlockSpec(tables[1].shape, lambda i: (0, 0, 0)),
        ],
        out_specs=pl.BlockSpec((ROWS, 256), lambda i: (0, i)),
        out_shape=jax.ShapeDtypeStruct((ROWS, KV), f32),
        compiler_params=params(),
        cost_estimate=pl.CostEstimate(flops=2 * ROWS * KV * 256, bytes_accessed=ROWS * KV * 8, transcendentals=0),
    )(blended, corner, *tables)


def add_parts(own, parts, after):
    def kernel(a, b, c, d, _, out_ref):
        out_ref[...] = (a[...] + b[...].astype(f32) + (c[...].astype(f32) + d[...].astype(f32))).astype(bf16)

    return pl.pallas_call(
        kernel,
        in_specs=[VMEM] * 4 + [ANY],
        out_specs=VMEM,
        out_shape=jax.ShapeDtypeStruct(own.shape, bf16),
        compiler_params=params(),
    )(own, *parts, after)


def normalized_update(info, quarters, tables, ones):
    def kernel(info_ref, a, b, c, d, left_ref, right_ref, ones_ref, out_ref):
        for k, ref in enumerate((a, b, c, d)):
            corner = ref[...].astype(f32)
            energy = jnp.sum((corner * corner).reshape(10, 32, 128), axis=1)
            high, low = split(energy)
            energy = mm(high, ones_ref[...]) + mm(low, ones_ref[...])
            scale = lax.rsqrt(energy * (1.0 / 4096.0) + block_epsilon)
            corner = (corner.reshape(10, 32, 128) * scale[:, None, :]).reshape(320, 128)
            columns = pl.ds(pl.multiple_of((info_ref[ME] ^ k) * 256, 256), 256)
            out_ref[:, columns] = from_corner(corner, left_ref[...], right_ref[...]).astype(bf16)

    return pl.pallas_call(
        kernel,
        in_specs=[SMEM] + [VMEM] * 7,
        out_specs=VMEM,
        out_shape=jax.ShapeDtypeStruct((ROWS, KV), bf16),
        compiler_params=params(),
    )(info, *quarters, *tables, ones)


def per_device(tokens, cotangent, weight, momentum, gain, band):
    tokens, cotangent, momentum = tokens[0], cotangent[0], momentum[0]
    rep, shard = lax.axis_index("rep"), lax.axis_index("shard")
    z, core = rep // 4, rep % 2
    y, xh = shard // 2, shard % 2
    parity = (z % 2).astype(jnp.int32)

    def shard_at(dy, dx):
        return (((y + dy) % 4) * 2 + (xh ^ dx)).astype(jnp.int32)

    def step_shard(k, c):
        return jnp.where(c == 0, shard_at(STEPS[k][0], 0), shard_at(STEPS[k][1], 1))

    info = jnp.stack(
        [parity, core, rep % 4, *[step_shard(k, core) for k in range(4)], *[step_shard(k, 1 - core) for k in range(4)],
         *[shard_at(*a) for a in AWAY], 1 - parity]
    ).astype(jnp.int32)
    tables = [jnp.asarray(t) for t in dct_tables()]
    ones = jnp.asarray(np.kron(np.eye(4), np.ones((32, 32))).astype(np.float32), bf16)
    corner_positions = (jnp.arange(32)[:, None] * 64 + jnp.arange(32)[None, :]).reshape(1024, 1)
    mask = jnp.any(corner_positions == band[None, :], axis=1).astype(f32).reshape(32, 32)
    mask = jnp.tile(mask, (10, 4))

    def is_own(k, c):
        return c == 0 and STEPS[k][c] == 0

    def near_source(k):
        return lambda z, x, c, y: None if is_own(k, c) else (z, 3 - x if c else x, c, y + STEPS[k][c])

    def z_source(k):
        return lambda z, x, c, y: None if is_own(k, c) else (z - 1 if c else z + 1, x, c, y)

    def core_swap(value):
        return pull(value, lambda z, x, c, y: (z, x, 1 - c, y))

    own_half, = cut_columns(info, weight, [PARITY], HALF)
    first = [pull(own_half, near_source(k)) for k in range(4)]
    others, = cut_columns(info, tokens, [FAR + k for k in range(4)], ROWS, joined=True, after=(own_half,))
    others = core_swap(others)
    second = [pull(first[k], z_source(k)) for k in range(4)]
    cut = cut_columns(info, tokens, [AWAY_AT + k for k in range(4)], ROWS, True, after=(first[0],))
    cut += cut_columns(info, tokens, [AWAY_AT + k for k in range(4, 8)], ROWS, True, after=(second[0],))
    arrived = [pull(cut[k], from_shard(-dy, dx)) if k else cut[k] for k, (dy, dx) in enumerate(AWAY)]

    mine, theirs = project(info, tokens, others, weight, first, second, arrived[1:8])
    key_grad = key_gradient(info, mine, core_swap(theirs), cotangent, gain[None], [])

    keys = {(0, 1): pull(key_grad, from_shard(0, 1))}
    for dy in (1, 3, 2):
        keys[dy, 0] = pull(key_grad, from_shard(dy, 0))
    keys[1, 1] = pull(keys[0, 1], from_shard(1, 0))
    keys[3, 1] = pull(keys[0, 1], from_shard(3, 0))
    keys[2, 1] = pull(keys[2, 0], from_shard(0, 1))

    mine, theirs = token_gradient(
        info, key_grad, core_swap(key_grad), weight, first, second,
        [keys[a] for a in ((0, 1), (1, 0), (3, 0), (2, 0))],
    )
    input_grad = place_columns(info, mine, core_swap(theirs))

    keys[0, 0] = key_grad
    blended, corner, quarter, *parts = blend(
        info, arrived, [keys[(-dy) % 4, dx] for dy, dx in AWAY], momentum, mask, tables, input_grad
    )
    residue = remove_corner(blended, corner, tables)

    def group_source(k):
        return lambda z, x, c, y: (z, x ^ (k // 2), c ^ (k % 2), y)

    def pull_z(value, flip):
        return pull(value, lambda z, x, c, y: (z ^ flip, x, c, y)).astype(f32)

    parts = {k: pull(parts[k - 1], group_source(k)) for k in (2, 3, 1)}
    summed = add_parts(quarter, [parts[k] for k in (1, 2, 3)], residue)
    summed = (summed.astype(f32) + pull_z(summed, 1)).astype(bf16)
    p4, p2, p6 = (pull_z(summed, flip) for flip in (4, 2, 6))
    summed = ((summed.astype(f32) + p2) + (p4 + p6)).astype(bf16)
    quarters = [summed] + [pull(summed, group_source(k)) for k in (1, 2, 3)]
    update = normalized_update(info, quarters, tables, ones)
    return (input_grad[None], residue[None], update)


def solution(mesh):
    return jax.shard_map(
        per_device,
        mesh=mesh,
        in_specs=(
            P("rep", "shard", None),
            P("rep", "shard", None),
            P("shard", None),
            P("rep", "shard", None),
            P(),
            P(),
        ),
        out_specs=(P("rep", "shard", None), P("rep", "shard", None), P("shard", None)),
        check_vma=False,
    )
```

time: 227 us -> 223 us (0.982)
  Pallas kernels: 44 us -> 59.8 us
  local copies, waits for them, and re-layouts: 23.3 us -> 7.59 us
  waiting for transfers between devices: 79 us -> 74.6 us
    unnamed x88 -> x70, local copies, waits for them, and re-layouts: 19.4 us -> 5.75 us
    pallas_call x2 -> x4, Pallas kernels: 2.89 us -> 12.1 us  [cut_columns(): pl.pallas_call(kernel, grid_spec=pltpu.PrefetchScalarGridSpec(num_scalar_...]
    ppermute x39 -> x36, waiting for transfers between devices: 79 us -> 74.6 us  [pull(): return lax.ppermute(value, ('rep', 'shard'), pairs)]
    pallas_call x1, Pallas kernels: 0.41 us -> 3.56 us  [key_gradient(): pl.pallas_call(kernel, grid_spec=pltpu.PrefetchScalarGridSpec(num_scalar_...]
    pallas_call x6 -> x5, Pallas kernels: 33.5 us -> 34.3 us  [the longest x1 12.6 us: blend(): pl.pallas_call(kernel, grid_spec=pltpu.PrefetchScalarGridSpec(num_scalar_...]
    ppermute x39 -> x36, starting transfers between devices: 77.2 us -> 77.7 us  [pull(): return lax.ppermute(value, ('rep', 'shard'), pairs)]
  transfers between devices with their start and end apart: 39 -> 36, of which waited for: 14 -> 17; matrix products, arithmetic and copies ran while one was open for 2% -> 1% of each run, Pallas kernels for 13% -> 8%
where the time goes in v2:
time: 223 us; the launch traced here: 222 us
  starting transfers between devices  77.7 us (35%)
  waiting for transfers between devices  74.6 us (33%)
  Pallas kernels  59.8 us (27%)
  local copies, waits for them, and re-layouts  7.59 us (3%)
    ppermute x36, starting transfers between devices, pull(): return lax.ppermute(value, ('rep', 'shard'), pairs)  77.7 us
    ppermute x36, waiting for transfers between devices, pull(): return lax.ppermute(value, ('rep', 'shard'), pairs)  74.6 us
    pallas_call x1, Pallas kernels, blend(): pl.pallas_call(kernel, grid_spec=pltpu.PrefetchScalarGridSpec(num_scalar_...  12.6 us
    pallas_call x4, Pallas kernels, cut_columns(): pl.pallas_call(kernel, grid_spec=pltpu.PrefetchScalarGridSpec(num_scalar_...  12.1 us
    pallas_call x1, Pallas kernels, project(): pl.pallas_call(kernel, in_specs=[SMEM, ANY, ANY, VMEM] + [ANY] * (8 + len...  8.7 us
    pallas_call x1, Pallas kernels, token_gradient(): pl.pallas_call(kernel, in_specs=[SMEM] + [VMEM] * 11 + [ANY] * len(after)...  7.87 us
    unnamed x70, local copies, waits for them, and re-layouts  5.75 us
    pallas_call x1, Pallas kernels, remove_corner(): pl.pallas_call(kernel, grid=(4,), in_specs=[pl.BlockSpec((ROWS, 256), lam...  5.46 us
  transfers between devices with their start and end apart: 36, of which 17 were waited for; matrix products, arithmetic and copies ran while one was open for 1% of the time, Pallas kernels for 8%

profile of v2, /device:TPU:1, one launch (start us, length us, event | category | flops | bytes accessed | tf_op | source)
XLA Modules:
  0.0 222.3 jit_solution(14778062637542822516)
XLA Ops:
  0.8 0.6 stack.83.info_ref.s_ref
  1.4 2.6 %shard_map.112.refs_4_ = bf16[640,512]{1,0:T(8,128)(2,1)} custom-call(s32[20]{0:T(128)} %stack.83.info_ref.s_ref, bf16[640,1024]{1,0:T(8,128)(2,1)} %own_ref.3), custom_call_target="tpu_custom_call" | custom-call | bytes 1310720 | tf_op jit(solution)/shard_map/pallas_call | solution.py:103
  4.0 3.3 %collective-permute-start.1 = (bf16[640,512]{1,0:T(8,128)(2,1)}, bf16[640,512]{1,0:T(8,128)(2,1)S(1)}, u32[]{:S(2)}, u32[]{:S(2)}) collective-permute-start(bf16[640,512]{1,0:T(8,128)(2,1)} %shard_map.112.refs_4_), channel_id=1, source_target_pairs={{2,0},{4,2},{6,4},{0,6},{25,8},{27,10},{29,12},{31,14},{18,16},{20... | collective-permute-start | bytes 1966088 | tf_op jit(solution)/shard_map/ppermute | solution.py:43
  7.3 2.6 %collective-permute-start.2 = (bf16[640,512]{1,0:T(8,128)(2,1)}, bf16[640,512]{1,0:T(8,128)(2,1)S(1)}, u32[]{:S(2)}, u32[]{:S(2)}) collective-permute-start(bf16[640,512]{1,0:T(8,128)(2,1)} %shard_map.112.refs_4_), channel_id=1, source_target_pairs={{6,0},{0,2},{2,4},{4,6},{27,8},{29,10},{31,12},{25,14},{22,16},{16... | collective-permute-start | bytes 1966088 | tf_op jit(solution)/shard_map/ppermute | solution.py:43
  10.0 0.9 collective-permute-start.3
  10.9 3.2 %shard_map.113 = bf16[256,2560]{1,0:T(8,128)(2,1)} custom-call(s32[20]{0:T(128)} %stack.83.info_ref.s_ref, bf16[256,5120]{1,0:T(8,128)(2,1)} %bitcast.26, bf16[256,5120]{1,0:T(8,128)(2,1)} %bitcast.27, bf16[256,5120]{1,0:T(8,128)(2,1)} %bitcast.28, bf16[256,5120]{1,0:T(8,128)(2,1)} %bitcast.29, bf16[640,512]{1,0:T(8,128)(2,1)} %shard_map.112.refs_4_), custom_call_target="tpu_custom_call" | custom-call | bytes 2621440 | tf_op jit(solution)/shard_map/pallas_call | solution.py:103
  14.1 5.0 %collective-permute-start.4 = (bf16[640,512]{1,0:T(8,128)(2,1)S(1)}, bf16[640,512]{1,0:T(8,128)(2,1)S(1)}, u32[]{:S(2)}, u32[]{:S(2)}) collective-permute-start(bf16[640,512]{1,0:T(8,128)(2,1)S(1)} %copy-done.2), channel_id=1, source_target_pairs={{29,8},{31,10},{25,12},{27,14},{13,24},{15,26},{9,28},{11,30},{28,... | collective-permute-start | bytes 1966088 | tf_op jit(solution)/shard_map/ppermute | solution.py:43
  19.1 1.7 collective-permute-start.5
  20.9 3.1 %shard_map.114 = (bf16[640,256]{1,0:T(8,128)(2,1)}, bf16[640,256]{1,0:T(8,128)(2,1)}, bf16[640,256]{1,0:T(8,128)(2,1)}, bf16[640,256]{1,0:T(8,128)(2,1)}) custom-call(s32[20]{0:T(128)} %stack.83.info_ref.s_ref, bf16[256,5120]{1,0:T(8,128)(2,1)} %bitcast.30, bf16[256,5120]{1,0:T(8,128)(2,1)} %bitcast.31, bf16[256,5120]{1,0:T(8,128)(2,1)} %bitcast.32, ...), custom_call_target="tpu_custom_call" | custom-call | bytes 2621440 | tf_op jit(solution)/shard_map/pallas_call | solution.py:103
  24.1 3.0 %collective-permute-start.10 = (bf16[640,256]{1,0:T(8,128)(2,1)}, bf16[640,256]{1,0:T(8,128)(2,1)S(1)}, u32[]{:S(2)}, u32[]{:S(2)}) collective-permute-start(bf16[640,256]{1,0:T(8,128)(2,1)} %get-tuple-element.22), channel_id=1, source_target_pairs={{2,0},{4,2},{6,4},{0,6},{10,8},{12,10},{14,12},{8,14},{18,16},{20,... | collective-permute-start | bytes 983048 | tf_op jit(solution)/shard_map/ppermute | solution.py:43
  27.0 5.9 %collective-permute-done.3.refs_2_ = bf16[640,512]{1,0:T(8,128)(2,1)S(1)} collective-permute-done((bf16[640,512]{1,0:T(8,128)(2,1)}, bf16[640,512]{1,0:T(8,128)(2,1)S(1)}, u32[]{:S(2)}, u32[]{:S(2)}) %collective-permute-start.3) | collective-permute-done | bytes 655392 | tf_op jit(solution)/shard_map/ppermute | solution.py:43
  33.0 1.4 collective-permute-start.11
  34.4 9.3 %collective-permute-done.4.refs_3_ = bf16[640,512]{1,0:T(8,128)(2,1)S(1)} collective-permute-done((bf16[640,512]{1,0:T(8,128)(2,1)S(1)}, bf16[640,512]{1,0:T(8,128)(2,1)S(1)}, u32[]{:S(2)}, u32[]{:S(2)}) %collective-permute-start.4) | collective-permute-done | bytes 655392 | tf_op jit(solution)/shard_map/ppermute | solution.py:43
  43.7 1.6 collective-permute-start.6
  45.3 1.6 collective-permute-start.7
  47.5 4.0 %collective-permute-start.8 = (bf16[640,512]{1,0:T(8,128)(2,1)S(1)}, bf16[640,512]{1,0:T(8,128)(2,1)S(1)}, u32[]{:S(2)}, u32[]{:S(2)}) collective-permute-start(bf16[640,512]{1,0:T(8,128)(2,1)S(1)} %collective-permute-done.4.refs_3_), channel_id=1, source_target_pairs={{232,8},{234,10},{236,12},{238,14},{248,24},{250,26},{252,28},{254... | collective-permute-start | bytes 1966088 | tf_op jit(solution)/shard_map/ppermute | solution.py:43
  51.5 3.1 %shard_map.115 = (bf16[640,256]{1,0:T(8,128)(2,1)}, bf16[640,256]{1,0:T(8,128)(2,1)}, bf16[640,256]{1,0:T(8,128)(2,1)}, bf16[640,256]{1,0:T(8,128)(2,1)}) custom-call(s32[20]{0:T(128)} %stack.83.info_ref.s_ref, bf16[256,5120]{1,0:T(8,128)(2,1)} %bitcast.34, bf16[256,5120]{1,0:T(8,128)(2,1)} %bitcast.35, bf16[256,5120]{1,0:T(8,128)(2,1)} %bitcast.36, ...), custom_call_target="tpu_custom_call" | custom-call | bytes 2621440 | tf_op jit(solution)/shard_map/pallas_call | solution.py:103
  54.7 1.5 collective-permute-start.12
  56.1 1.5 collective-permute-start.13
  57.6 3.6 %collective-permute-start.14 = (bf16[640,256]{1,0:T(8,128)(2,1)}, bf16[640,256]{1,0:T(8,128)(2,1)S(1)}, u32[]{:S(2)}, u32[]{:S(2)}) collective-permute-start(bf16[640,256]{1,0:T(8,128)(2,1)} %get-tuple-element.26), channel_id=1, source_target_pairs={{3,0},{5,2},{7,4},{1,6},{11,8},{13,10},{15,12},{9,14},{19,16},{21,... | collective-permute-start | bytes 983048 | tf_op jit(solution)/shard_map/ppermute | solution.py:43
  61.2 3.3 %collective-permute-done.7.refs_6_ = bf16[640,512]{1,0:T(8,128)(2,1)S(1)} collective-permute-done((bf16[640,512]{1,0:T(8,128)(2,1)S(1)}, bf16[640,512]{1,0:T(8,128)(2,1)S(1)}, u32[]{:S(2)}, u32[]{:S(2)}) %collective-permute-start.7) | collective-permute-done | bytes 655392 | tf_op jit(solution)/shard_map/ppermute | solution.py:43
  64.5 6.7 %collective-permute-done.8.refs_7_ = bf16[640,512]{1,0:T(8,128)(2,1)S(1)} collective-permute-done((bf16[640,512]{1,0:T(8,128)(2,1)S(1)}, bf16[640,512]{1,0:T(8,128)(2,1)S(1)}, u32[]{:S(2)}, u32[]{:S(2)}) %collective-permute-start.8) | collective-permute-done | bytes 655392 | tf_op jit(solution)/shard_map/ppermute | solution.py:43
  71.3 3.3 %collective-permute-done.15.refs_14_.refs_7_ = bf16[640,256]{1,0:T(8,128)(2,1)S(1)} collective-permute-done((bf16[640,256]{1,0:T(8,128)(2,1)}, bf16[640,256]{1,0:T(8,128)(2,1)S(1)}, u32[]{:S(2)}, u32[]{:S(2)}) %collective-permute-start.15) | collective-permute-done | bytes 327712 | tf_op jit(solution)/shard_map/ppermute | solution.py:43
  74.7 0.7 copy-done.9
  75.4 8.7 %shard_map.116 = (f32[256,1024]{1,0:T(8,128)}, f32[256,1024]{1,0:T(8,128)}) custom-call(s32[20]{0:T(128)} %stack.83.info_ref.s_ref, bf16[256,5120]{1,0:T(8,128)(2,1)} %bitcast.38, bf16[256,2560]{1,0:T(8,128)(2,1)} %copy-done.10, bf16[640,1024]{1,0:T(8,128)(2,1)} %own_ref.3, bf16[640,512]{1,0:T(8,128)(2,1)} %copy-done, bf16[640,512]{1,0:T(8,128)(2,1)} %copy-done.13, ...), custom_call_target="tpu_custom_call" | custom-call | flops 2684354560 | bytes 13107200 | tf_op jit(solution)/shard_map/pallas_call | solution.py:155
  84.1 14.7 %collective-permute-start.16 = (f32[256,1024]{1,0:T(8,128)}, f32[256,1024]{1,0:T(8,128)S(1)}, u32[]{:S(2)}, u32[]{:S(2)}) collective-permute-start(f32[256,1024]{1,0:T(8,128)} %get-tuple-element.29), channel_id=1, source_target_pairs={{8,0},{10,2},{12,4},{14,6},{0,8},{2,10},{4,12},{6,14},{24,16},{26,... | collective-permute-start | bytes 3145736 | tf_op jit(solution)/shard_map/ppermute | solution.py:43
  98.8 2.5 %collective-permute-done.16.r_ref = f32[256,1024]{1,0:T(8,128)S(1)} collective-permute-done((f32[256,1024]{1,0:T(8,128)}, f32[256,1024]{1,0:T(8,128)S(1)}, u32[]{:S(2)}, u32[]{:S(2)}) %collective-permute-start.16) | collective-permute-done | bytes 1048608 | tf_op jit(solution)/shard_map/ppermute | solution.py:43
  101.3 1.0 copy-done.12
  102.3 3.6 %shard_map.117.k_ref.refs_8_ = bf16[256,1024]{1,0:T(8,128)(2,1)} custom-call(s32[20]{0:T(128)} %stack.83.info_ref.s_ref, f32[256,1024]{1,0:T(8,128)} %get-tuple-element.28.m_ref, f32[256,1024]{1,0:T(8,128)} %copy-done.12, bf16[256,1024]{1,0:T(8,128)(2,1)} %bitcast.42, bf16[256,1024]{1,0:T(8,128)(2,1)} %bitcast.43, f32[1,1024]{1,0:T(1,128)} %bitcast.44, ...), custom_call_target="tpu_custom_call" | custom-call | flops 2621440 | bytes 3145728 | tf_op jit(solution)/shard_map/pallas_call | solution.py:187
  106.2 0.9 collective-permute-start.18
  107.1 1.4 collective-permute-start.19
  108.6 1.4 collective-permute-start.21
  110.0 11.3 %collective-permute-done.18.refs_8_.refs_11_ = bf16[256,1024]{1,0:T(8,128)(2,1)S(1)} collective-permute-done((bf16[256,1024]{1,0:T(8,128)(2,1)}, bf16[256,1024]{1,0:T(8,128)(2,1)S(1)}, u32[]{:S(2)}, u32[]{:S(2)}) %collective-permute-start.18) | collective-permute-done | bytes 524320 | tf_op jit(solution)/shard_map/ppermute | solution.py:43
  121.3 2.6 %collective-permute-done.20.refs_10_.refs_9_ = bf16[256,1024]{1,0:T(8,128)(2,1)S(1)} collective-permute-done((bf16[256,1024]{1,0:T(8,128)(2,1)}, bf16[256,1024]{1,0:T(8,128)(2,1)S(1)}, u32[]{:S(2)}, u32[]{:S(2)}) %collective-permute-start.20) | collective-permute-done | bytes 524320 | tf_op jit(solution)/shard_map/ppermute | solution.py:43
  123.9 8.8 %collective-permute-done.21.refs_11_.refs_12_ = bf16[256,1024]{1,0:T(8,128)(2,1)S(1)} collective-permute-done((bf16[256,1024]{1,0:T(8,128)(2,1)}, bf16[256,1024]{1,0:T(8,128)(2,1)S(1)}, u32[]{:S(2)}, u32[]{:S(2)}) %collective-permute-start.21) | collective-permute-done | bytes 524320 | tf_op jit(solution)/shard_map/ppermute | solution.py:43
  132.8 0.8 copy-done.22
  133.6 7.9 %shard_map.118 = (bf16[256,2560]{1,0:T(8,128)(2,1)}, bf16[256,2560]{1,0:T(8,128)(2,1)}) custom-call(s32[20]{0:T(128)} %stack.83.info_ref.s_ref, bf16[256,1024]{1,0:T(8,128)(2,1)} %shard_map.117.k_ref.refs_8_, bf16[256,1024]{1,0:T(8,128)(2,1)} %copy-done.34, bf16[640,1024]{1,0:T(8,128)(2,1)} %own_ref.3, bf16[640,512]{1,0:T(8,128)(2,1)} %copy-done, ...), custom_call_target="tpu_custom_call" | custom-call | flops 2684354560 | bytes 13107200 | tf_op jit(solution)/shard_map/pallas_call | solution.py:222
  141.5 3.6 %collective-permute-start.22 = (bf16[256,2560]{1,0:T(8,128)(2,1)}, bf16[256,2560]{1,0:T(8,128)(2,1)S(1)}, u32[]{:S(2)}, u32[]{:S(2)}) collective-permute-start(bf16[256,2560]{1,0:T(8,128)(2,1)} %get-tuple-element.31), channel_id=1, source_target_pairs={{8,0},{10,2},{12,4},{14,6},{0,8},{2,10},{4,12},{6,14},{24,16},{26,... | collective-permute-start | bytes 3932168 | tf_op jit(solution)/shard_map/ppermute | solution.py:43
  145.1 2.7 %collective-permute-start.24 = (bf16[256,1024]{1,0:T(8,128)(2,1)}, bf16[256,1024]{1,0:T(8,128)(2,1)S(1)}, u32[]{:S(2)}, u32[]{:S(2)}) collective-permute-start(bf16[256,1024]{1,0:T(8,128)(2,1)} %copy-done.19), channel_id=1, source_target_pairs={{2,0},{4,2},{6,4},{0,6},{10,8},{12,10},{14,12},{8,14},{18,16},{20,... | collective-permute-start | bytes 1572872 | tf_op jit(solution)/shard_map/ppermute | solution.py:43
  147.8 2.7 %collective-permute-start.25 = (bf16[256,1024]{1,0:T(8,128)(2,1)}, bf16[256,1024]{1,0:T(8,128)(2,1)S(1)}, u32[]{:S(2)}, u32[]{:S(2)}) collective-permute-start(bf16[256,1024]{1,0:T(8,128)(2,1)} %copy-done.22), channel_id=1, source_target_pairs={{1,0},{3,2},{5,4},{7,6},{9,8},{11,10},{13,12},{15,14},{17,16},{19,... | collective-permute-start | bytes 1572872 | tf_op jit(solution)/shard_map/ppermute | solution.py:43
  151.3 1.0 tile.9.refs_17_
  152.3 1.1 copy-done.11
  153.4 3.4 %shard_map.119.refs_20_ = bf16[256,5120]{1,0:T(8,128)(2,1)} custom-call(s32[20]{0:T(128)} %stack.83.info_ref.s_ref, bf16[256,2560]{1,0:T(8,128)(2,1)} %get-tuple-element.30.m_ref, bf16[256,2560]{1,0:T(8,128)(2,1)} %copy-done.11), custom_call_target="tpu_custom_call" | custom-call | bytes 5242880 | tf_op jit(solution)/shard_map/pallas_call | solution.py:239
  156.8 3.3 %collective-permute-done.23.refs_13_ = bf16[256,1024]{1,0:T(8,128)(2,1)S(1)} collective-permute-done((bf16[256,1024]{1,0:T(8,128)(2,1)}, bf16[256,1024]{1,0:T(8,128)(2,1)S(1)}, u32[]{:S(2)}, u32[]{:S(2)}) %collective-permute-start.23) | collective-permute-done | bytes 524320 | tf_op jit(solution)/shard_map/ppermute | solution.py:43
  160.1 2.3 %collective-permute-done.25.refs_15_ = bf16[256,1024]{1,0:T(8,128)(2,1)S(1)} collective-permute-done((bf16[256,1024]{1,0:T(8,128)(2,1)}, bf16[256,1024]{1,0:T(8,128)(2,1)S(1)}, u32[]{:S(2)}, u32[]{:S(2)}) %collective-permute-start.25) | collective-permute-done | bytes 524320 | tf_op jit(solution)/shard_map/ppermute | solution.py:43
  162.4 0.8 copy-done.25
  163.2 12.6 %shard_map.120 = (f32[640,1024]{1,0:T(8,128)}, f32[4,320,128]{2,1,0:T(8,128)}, f32[320,128]{1,0:T(8,128)}, bf16[320,128]{1,0:T(8,128)(2,1)}, bf16[320,128]{1,0:T(8,128)(2,1)}, /*index=5*/bf16[320,128]{1,0:T(8,128)(2,1)}) custom-call(s32[20]{0:T(128)} %stack.83.info_ref.s_ref, bf16[640,256]{1,0:T(8,128)(2,1)} %get-tuple-element.32.refs_0_, ...), custom_call_target="tpu_custom_call" | custom-call | flops 2684354560 | bytes 12058624 | tf_op jit(solution)/shard_map/pallas_call | solution.py:299
  175.8 1.5 collective-permute-start.26
  177.4 2.8 %collective-permute-start.27 = (bf16[320,128]{1,0:T(8,128)(2,1)}, bf16[320,128]{1,0:T(8,128)(2,1)S(1)}, u32[]{:S(2)}, u32[]{:S(2)}) collective-permute-start(bf16[320,128]{1,0:T(8,128)(2,1)} %get-tuple-element.37), channel_id=1, source_target_pairs={{16,0},{18,2},{20,4},{22,6},{24,8},{26,10},{28,12},{30,14},{0,16},... | collective-permute-start | bytes 245768 | tf_op jit(solution)/shard_map/ppermute | solution.py:43
  180.2 5.5 %shard_map.121._ = f32[640,1024]{1,0:T(8,128)} custom-call(f32[640,1024]{1,0:T(8,128)} %get-tuple-element.33.blended_ref, f32[4,320,128]{2,1,0:T(8,128)} %get-tuple-element.34.corner_ref, bf16[2,64,128]{2,1,0:T(8,128)(2,1)} %constant.128.clone.refs_18_.left_ref, bf16[2,256,128]{2,1,0:T(8,128)(2,1)} %constant.129.clone.refs_19_.right_ref), custom_call_target="tpu_custom_call" | custom-call | flops 335544320 | bytes 5242880 | tf_op jit(solution)/shard_map/pallas_call | solution.py:320
  186.4 1.7 shard_map.122
  188.1 5.0 %collective-permute-start.29 = (bf16[320,128]{1,0:T(8,128)(2,1)}, bf16[320,128]{1,0:T(8,128)(2,1)S(1)}, u32[]{:S(2)}, u32[]{:S(2)}) collective-permute-start(bf16[320,128]{1,0:T(8,128)(2,1)} %shard_map.122), channel_id=1, source_target_pairs={{32,0},{34,2},{36,4},{38,6},{40,8},{42,10},{44,12},{46,14},{48,16}... | collective-permute-start | bytes 245768 | tf_op jit(solution)/shard_map/ppermute | solution.py:43
  193.0 3.0 %collective-permute-done.29 = bf16[320,128]{1,0:T(8,128)(2,1)S(1)} collective-permute-done((bf16[320,128]{1,0:T(8,128)(2,1)}, bf16[320,128]{1,0:T(8,128)(2,1)S(1)}, u32[]{:S(2)}, u32[]{:S(2)}) %collective-permute-start.29) | collective-permute-done | bytes 81952 | tf_op jit(solution)/shard_map/ppermute | solution.py:43
  196.0 0.9 add_convert_fusion.1
  197.0 4.0 %collective-permute-start.31 = (bf16[320,128]{1,0:T(8,128)(2,1)S(1)}, bf16[320,128]{1,0:T(8,128)(2,1)S(1)}, u32[]{:S(2)}, u32[]{:S(2)}) collective-permute-start(bf16[320,128]{1,0:T(8,128)(2,1)S(1)} %add_convert_fusion.1), channel_id=1, source_target_pairs={{128,0},{130,2},{132,4},{134,6},{136,8},{138,10},{140,12},{142,14}... | collective-permute-start | bytes 245768 | tf_op jit(solution)/shard_map/ppermute | solution.py:43
  201.0 1.7 collective-permute-start.32
  202.7 2.0 collective-permute-done.31
  204.7 5.9 %collective-permute-done.32 = bf16[320,128]{1,0:T(8,128)(2,1)S(1)} collective-permute-done((bf16[320,128]{1,0:T(8,128)(2,1)S(1)}, bf16[320,128]{1,0:T(8,128)(2,1)S(1)}, u32[]{:S(2)}, u32[]{:S(2)}) %collective-permute-start.32) | collective-permute-done | bytes 81952 | tf_op jit(solution)/shard_map/ppermute | solution.py:43
  210.6 0.8 collective-permute-start.33
  211.4 1.7 collective-permute-start.35
  213.1 2.3 %collective-permute-done.34.c = bf16[320,128]{1,0:T(8,128)(2,1)S(1)} collective-permute-done((bf16[320,128]{1,0:T(8,128)(2,1)S(1)}, bf16[320,128]{1,0:T(8,128)(2,1)S(1)}, u32[]{:S(2)}, u32[]{:S(2)}) %collective-permute-start.34) | collective-permute-done | bytes 81952 | tf_op jit(solution)/shard_map/ppermute | solution.py:43
  215.4 1.9 collective-permute-done.35.d
  217.3 0.6 copy-done.32
  218.0 4.4 %shard_map.123 = bf16[640,1024]{1,0:T(8,128)(2,1)} custom-call(s32[20]{0:T(128)} %stack.83.info_ref.s_ref, bf16[320,128]{1,0:T(8,128)(2,1)} %copy-done.26, bf16[320,128]{1,0:T(8,128)(2,1)} %copy-done.30, bf16[320,128]{1,0:T(8,128)(2,1)} %copy-done.31, bf16[320,128]{1,0:T(8,128)(2,1)} %copy-done.32, bf16[2,64,128]{2,1,0:T(8,128)(2,1)} %constant.128.clone.refs_18_.left_ref, ...), custom_call_target="tpu_custom_call" | custom-call | tf_op jit(solution)/shard_map/pallas_call | solution.py:361
  (101 shorter events, 2.9 us)
Async XLA Ops:
  4.0 15.1 %collective-permute-start.1 = (bf16[640,512]{1,0:T(8,128)(2,1)}, bf16[640,512]{1,0:T(8,128)(2,1)S(1)}, u32[]{:S(2)}, u32[]{:S(2)}) collective-permute-start(bf16[640,512]{1,0:T(8,128)(2,1)} %shard_map.112.refs_4_), channel_id=1, source_target_pairs={{2,0},{4,2},{6,4},{0,6},{25,8},{27,10},{29,12},{31,14},{18,16},{20... | collective-permute-start | bytes 1966088 | tf_op jit(solution)/shard_map/ppermute | solution.py:43
  7.3 16.7 %collective-permute-start.2 = (bf16[640,512]{1,0:T(8,128)(2,1)}, bf16[640,512]{1,0:T(8,128)(2,1)S(1)}, u32[]{:S(2)}, u32[]{:S(2)}) collective-permute-start(bf16[640,512]{1,0:T(8,128)(2,1)} %shard_map.112.refs_4_), channel_id=1, source_target_pairs={{6,0},{0,2},{2,4},{4,6},{27,8},{29,10},{31,12},{25,14},{22,16},{16... | collective-permute-start | bytes 1966088 | tf_op jit(solution)/shard_map/ppermute | solution.py:43
  10.0 23.0 %collective-permute-start.3 = (bf16[640,512]{1,0:T(8,128)(2,1)}, bf16[640,512]{1,0:T(8,128)(2,1)S(1)}, u32[]{:S(2)}, u32[]{:S(2)}) collective-permute-start(bf16[640,512]{1,0:T(8,128)(2,1)} %shard_map.112.refs_4_), channel_id=1, source_target_pairs={{4,0},{6,2},{0,4},{2,6},{31,8},{25,10},{27,12},{29,14},{20,16},{22... | collective-permute-start | bytes 1966088 | tf_op jit(solution)/shard_map/ppermute | solution.py:43
  10.9 3.2 %copy-start.2 = (bf16[640,512]{1,0:T(8,128)(2,1)S(1)}, bf16[640,512]{1,0:T(8,128)(2,1)}, u32[]{:S(2)}) copy-start(bf16[640,512]{1,0:T(8,128)(2,1)} %shard_map.112.refs_4_) | copy-start | bytes 1966084
  14.1 42.0 %collective-permute-start = (bf16[256,2560]{1,0:T(8,128)(2,1)}, bf16[256,2560]{1,0:T(8,128)(2,1)S(1)}, u32[]{:S(2)}, u32[]{:S(2)}) collective-permute-start(bf16[256,2560]{1,0:T(8,128)(2,1)} %shard_map.113), channel_id=1, source_target_pairs={{8,0},{10,2},{12,4},{14,6},{0,8},{2,10},{4,12},{6,14},{24,16},{26,... | collective-permute-start | bytes 3932168 | tf_op jit(solution)/shard_map/ppermute | solution.py:43
  14.1 29.5 %collective-permute-start.4 = (bf16[640,512]{1,0:T(8,128)(2,1)S(1)}, bf16[640,512]{1,0:T(8,128)(2,1)S(1)}, u32[]{:S(2)}, u32[]{:S(2)}) collective-permute-start(bf16[640,512]{1,0:T(8,128)(2,1)S(1)} %copy-done.2), channel_id=1, source_target_pairs={{29,8},{31,10},{25,12},{27,14},{13,24},{15,26},{9,28},{11,30},{28,... | collective-permute-start | bytes 1966088 | tf_op jit(solution)/shard_map/ppermute | solution.py:43
  19.1 1.7 copy-start
  19.1 28.4 %collective-permute-start.5 = (bf16[640,512]{1,0:T(8,128)(2,1)S(1)}, bf16[640,512]{1,0:T(8,128)(2,1)S(1)}, u32[]{:S(2)}, u32[]{:S(2)}) collective-permute-start(bf16[640,512]{1,0:T(8,128)(2,1)S(1)} %collective-permute-done.1.refs_4_.refs_0_), channel_id=1, source_target_pairs={{32,0},{34,2},{36,4},{38,6},{232,8},{234,10},{236,12},{238,14},{48... | collective-permute-start | bytes 1966088 | tf_op jit(solution)/shard_map/ppermute | solution.py:43
  24.1 50.5 %copy-start.13 = (bf16[640,512]{1,0:T(8,128)(2,1)}, bf16[640,512]{1,0:T(8,128)(2,1)S(1)}, u32[]{:S(2)}) copy-start(bf16[640,512]{1,0:T(8,128)(2,1)S(1)} %collective-permute-done.2.refs_1_) | copy-start | bytes 1966084
  24.1 21.2 %collective-permute-start.10 = (bf16[640,256]{1,0:T(8,128)(2,1)}, bf16[640,256]{1,0:T(8,128)(2,1)S(1)}, u32[]{:S(2)}, u32[]{:S(2)}) collective-permute-start(bf16[640,256]{1,0:T(8,128)(2,1)} %get-tuple-element.22), channel_id=1, source_target_pairs={{2,0},{4,2},{6,4},{0,6},{10,8},{12,10},{14,12},{8,14},{18,16},{20,... | collective-permute-start | bytes 983048 | tf_op jit(solution)/shard_map/ppermute | solution.py:43
  33.0 41.6 %copy-start.14 = (bf16[640,512]{1,0:T(8,128)(2,1)}, bf16[640,512]{1,0:T(8,128)(2,1)S(1)}, u32[]{:S(2)}) copy-start(bf16[640,512]{1,0:T(8,128)(2,1)S(1)} %collective-permute-done.3.refs_2_) | copy-start | bytes 1966084
  33.0 14.0 %collective-permute-start.11 = (bf16[640,256]{1,0:T(8,128)(2,1)}, bf16[640,256]{1,0:T(8,128)(2,1)S(1)}, u32[]{:S(2)}, u32[]{:S(2)}) collective-permute-start(bf16[640,256]{1,0:T(8,128)(2,1)} %get-tuple-element.23), channel_id=1, source_target_pairs={{1,0},{3,2},{5,4},{7,6},{9,8},{11,10},{13,12},{15,14},{17,16},{19,... | collective-permute-start | bytes 983048 | tf_op jit(solution)/shard_map/ppermute | solution.py:43
  43.7 30.9 %copy-start.15 = (bf16[640,512]{1,0:T(8,128)(2,1)}, bf16[640,512]{1,0:T(8,128)(2,1)S(1)}, u32[]{:S(2)}) copy-start(bf16[640,512]{1,0:T(8,128)(2,1)S(1)} %collective-permute-done.4.refs_3_) | copy-start | bytes 1966084
  43.7 13.9 %collective-permute-start.6 = (bf16[640,512]{1,0:T(8,128)(2,1)S(1)}, bf16[640,512]{1,0:T(8,128)(2,1)S(1)}, u32[]{:S(2)}, u32[]{:S(2)}) collective-permute-start(bf16[640,512]{1,0:T(8,128)(2,1)S(1)} %collective-permute-done.2.refs_1_), channel_id=1, source_target_pairs={{32,0},{34,2},{36,4},{38,6},{232,8},{234,10},{236,12},{238,14},{48... | collective-permute-start | bytes 1966088 | tf_op jit(solution)/shard_map/ppermute | solution.py:43
  45.3 29.3 %copy-start.3 = (bf16[640,256]{1,0:T(8,128)(2,1)}, bf16[640,256]{1,0:T(8,128)(2,1)S(1)}, u32[]{:S(2)}) copy-start(bf16[640,256]{1,0:T(8,128)(2,1)S(1)} %collective-permute-done.10.refs_9_.refs_2_) | copy-start | bytes 983044
  45.3 19.2 %collective-permute-start.7 = (bf16[640,512]{1,0:T(8,128)(2,1)S(1)}, bf16[640,512]{1,0:T(8,128)(2,1)S(1)}, u32[]{:S(2)}, u32[]{:S(2)}) collective-permute-start(bf16[640,512]{1,0:T(8,128)(2,1)S(1)} %collective-permute-done.3.refs_2_), channel_id=1, source_target_pairs={{32,0},{34,2},{36,4},{38,6},{232,8},{234,10},{236,12},{238,14},{48... | collective-permute-start | bytes 1966088 | tf_op jit(solution)/shard_map/ppermute | solution.py:43
  47.0 27.7 %copy-start.4 = (bf16[640,256]{1,0:T(8,128)(2,1)}, bf16[640,256]{1,0:T(8,128)(2,1)S(1)}, u32[]{:S(2)}) copy-start(bf16[640,256]{1,0:T(8,128)(2,1)S(1)} %collective-permute-done.11.refs_10_.refs_3_) | copy-start | bytes 983044
  47.0 7.7 %collective-permute-start.9 = (bf16[640,256]{1,0:T(8,128)(2,1)}, bf16[640,256]{1,0:T(8,128)(2,1)S(1)}, u32[]{:S(2)}, u32[]{:S(2)}) collective-permute-start(bf16[640,256]{1,0:T(8,128)(2,1)} %get-tuple-element.21), channel_id=1, source_target_pairs={{6,0},{0,2},{2,4},{4,6},{14,8},{8,10},{10,12},{12,14},{22,16},{16,... | collective-permute-start | bytes 983048 | tf_op jit(solution)/shard_map/ppermute | solution.py:43
  47.5 4.0 %copy-start.1 = (bf16[640,512]{1,0:T(8,128)(2,1)}, bf16[640,512]{1,0:T(8,128)(2,1)S(1)}, u32[]{:S(2)}) copy-start(bf16[640,512]{1,0:T(8,128)(2,1)S(1)} %collective-permute-done.5.refs_4_) | copy-start | bytes 1966084
  47.5 23.7 %collective-permute-start.8 = (bf16[640,512]{1,0:T(8,128)(2,1)S(1)}, bf16[640,512]{1,0:T(8,128)(2,1)S(1)}, u32[]{:S(2)}, u32[]{:S(2)}) collective-permute-start(bf16[640,512]{1,0:T(8,128)(2,1)S(1)} %collective-permute-done.4.refs_3_), channel_id=1, source_target_pairs={{232,8},{234,10},{236,12},{238,14},{248,24},{250,26},{252,28},{254... | collective-permute-start | bytes 1966088 | tf_op jit(solution)/shard_map/ppermute | solution.py:43
  54.7 20.0 %copy-start.5 = (bf16[640,256]{1,0:T(8,128)(2,1)}, bf16[640,256]{1,0:T(8,128)(2,1)S(1)}, u32[]{:S(2)}) copy-start(bf16[640,256]{1,0:T(8,128)(2,1)S(1)} %collective-permute-done.9.refs_8_.refs_1_) | copy-start | bytes 983044
  54.7 16.6 %collective-permute-start.12 = (bf16[640,256]{1,0:T(8,128)(2,1)}, bf16[640,256]{1,0:T(8,128)(2,1)S(1)}, u32[]{:S(2)}, u32[]{:S(2)}) collective-permute-start(bf16[640,256]{1,0:T(8,128)(2,1)} %get-tuple-element.24), channel_id=1, source_target_pairs={{4,0},{6,2},{0,4},{2,6},{12,8},{14,10},{8,12},{10,14},{20,16},{22,... | collective-permute-start | bytes 983048 | tf_op jit(solution)/shard_map/ppermute | solution.py:43
  56.1 18.5 %copy-start.10 = (bf16[256,2560]{1,0:T(8,128)(2,1)}, bf16[256,2560]{1,0:T(8,128)(2,1)S(1)}, u32[]{:S(2)}) copy-start(bf16[256,2560]{1,0:T(8,128)(2,1)S(1)} %collective-permute-done.o_ref) | copy-start | bytes 3932164
  56.1 15.2 %collective-permute-start.13 = (bf16[640,256]{1,0:T(8,128)(2,1)}, bf16[640,256]{1,0:T(8,128)(2,1)S(1)}, u32[]{:S(2)}, u32[]{:S(2)}) collective-permute-start(bf16[640,256]{1,0:T(8,128)(2,1)} %get-tuple-element.25), channel_id=1, source_target_pairs={{7,0},{1,2},{3,4},{5,6},{15,8},{9,10},{11,12},{13,14},{23,16},{17,... | collective-permute-start | bytes 983048 | tf_op jit(solution)/shard_map/ppermute | solution.py:43
  57.6 17.1 %copy-start.16 = (bf16[640,512]{1,0:T(8,128)(2,1)}, bf16[640,512]{1,0:T(8,128)(2,1)S(1)}, u32[]{:S(2)}) copy-start(bf16[640,512]{1,0:T(8,128)(2,1)S(1)} %collective-permute-done.6.refs_5_) | copy-start | bytes 1966084
  57.6 13.7 %collective-permute-start.14 = (bf16[640,256]{1,0:T(8,128)(2,1)}, bf16[640,256]{1,0:T(8,128)(2,1)S(1)}, u32[]{:S(2)}, u32[]{:S(2)}) collective-permute-start(bf16[640,256]{1,0:T(8,128)(2,1)} %get-tuple-element.26), channel_id=1, source_target_pairs={{3,0},{5,2},{7,4},{1,6},{11,8},{13,10},{15,12},{9,14},{19,16},{21,... | collective-permute-start | bytes 983048 | tf_op jit(solution)/shard_map/ppermute | solution.py:43
  64.5 10.1 %copy-start.17 = (bf16[640,512]{1,0:T(8,128)(2,1)}, bf16[640,512]{1,0:T(8,128)(2,1)S(1)}, u32[]{:S(2)}) copy-start(bf16[640,512]{1,0:T(8,128)(2,1)S(1)} %collective-permute-done.7.refs_6_) | copy-start | bytes 1966084
  64.5 10.0 %collective-permute-start.15 = (bf16[640,256]{1,0:T(8,128)(2,1)}, bf16[640,256]{1,0:T(8,128)(2,1)S(1)}, u32[]{:S(2)}, u32[]{:S(2)}) collective-permute-start(bf16[640,256]{1,0:T(8,128)(2,1)} %get-tuple-element.27), channel_id=1, source_target_pairs={{5,0},{7,2},{1,4},{3,6},{13,8},{15,10},{9,12},{11,14},{21,16},{23,... | collective-permute-start | bytes 983048 | tf_op jit(solution)/shard_map/ppermute | solution.py:43
  71.3 3.4 %copy-start.18 = (bf16[640,512]{1,0:T(8,128)(2,1)}, bf16[640,512]{1,0:T(8,128)(2,1)S(1)}, u32[]{:S(2)}) copy-start(bf16[640,512]{1,0:T(8,128)(2,1)S(1)} %collective-permute-done.8.refs_7_) | copy-start | bytes 1966084
  71.3 3.4 %copy-start.6 = (bf16[640,256]{1,0:T(8,128)(2,1)}, bf16[640,256]{1,0:T(8,128)(2,1)S(1)}, u32[]{:S(2)}) copy-start(bf16[640,256]{1,0:T(8,128)(2,1)S(1)} %collective-permute-done.12.refs_11_.refs_4_) | copy-start | bytes 983044
  71.3 3.4 %copy-start.7 = (bf16[640,256]{1,0:T(8,128)(2,1)}, bf16[640,256]{1,0:T(8,128)(2,1)S(1)}, u32[]{:S(2)}) copy-start(bf16[640,256]{1,0:T(8,128)(2,1)S(1)} %collective-permute-done.13.refs_12_.refs_5_) | copy-start | bytes 983044
  71.3 3.4 %copy-start.8 = (bf16[640,256]{1,0:T(8,128)(2,1)}, bf16[640,256]{1,0:T(8,128)(2,1)S(1)}, u32[]{:S(2)}) copy-start(bf16[640,256]{1,0:T(8,128)(2,1)S(1)} %collective-permute-done.14.refs_13_.refs_6_) | copy-start | bytes 983044
  84.1 17.2 %collective-permute-start.16 = (f32[256,1024]{1,0:T(8,128)}, f32[256,1024]{1,0:T(8,128)S(1)}, u32[]{:S(2)}, u32[]{:S(2)}) collective-permute-start(f32[256,1024]{1,0:T(8,128)} %get-tuple-element.29), channel_id=1, source_target_pairs={{8,0},{10,2},{12,4},{14,6},{0,8},{2,10},{4,12},{6,14},{24,16},{26,... | collective-permute-start | bytes 3145736 | tf_op jit(solution)/shard_map/ppermute | solution.py:43
  101.3 1.0 copy-start.12
  105.9 44.8 %copy-start.33 = (s32[640]{0:T(1024)S(1)}, s32[640]{0:T(1024)}, u32[]{:S(2)}) copy-start(s32[640]{0:T(1024)} %param.14) | copy-start | bytes 7684
  105.9 4.1 %collective-permute-start.17 = (bf16[256,1024]{1,0:T(8,128)(2,1)}, bf16[256,1024]{1,0:T(8,128)(2,1)S(1)}, u32[]{:S(2)}, u32[]{:S(2)}) collective-permute-start(bf16[256,1024]{1,0:T(8,128)(2,1)} %shard_map.117.k_ref.refs_8_), channel_id=1, source_target_pairs={{8,0},{10,2},{12,4},{14,6},{0,8},{2,10},{4,12},{6,14},{24,16},{26,... | collective-permute-start | bytes 1572872 | tf_op jit(solution)/shard_map/ppermute | solution.py:43
  106.2 15.1 %collective-permute-start.18 = (bf16[256,1024]{1,0:T(8,128)(2,1)}, bf16[256,1024]{1,0:T(8,128)(2,1)S(1)}, u32[]{:S(2)}, u32[]{:S(2)}) collective-permute-start(bf16[256,1024]{1,0:T(8,128)(2,1)} %shard_map.117.k_ref.refs_8_), channel_id=1, source_target_pairs={{1,0},{3,2},{5,4},{7,6},{9,8},{11,10},{13,12},{15,14},{17,16},{19,... | collective-permute-start | bytes 1572872 | tf_op jit(solution)/shard_map/ppermute | solution.py:43
  107.1 14.2 %collective-permute-start.19 = (bf16[256,1024]{1,0:T(8,128)(2,1)}, bf16[256,1024]{1,0:T(8,128)(2,1)S(1)}, u32[]{:S(2)}, u32[]{:S(2)}) collective-permute-start(bf16[256,1024]{1,0:T(8,128)(2,1)} %shard_map.117.k_ref.refs_8_), channel_id=1, source_target_pairs={{2,0},{4,2},{6,4},{0,6},{10,8},{12,10},{14,12},{8,14},{18,16},{20,... | collective-permute-start | bytes 1572872 | tf_op jit(solution)/shard_map/ppermute | solution.py:43
  108.6 15.4 %collective-permute-start.20 = (bf16[256,1024]{1,0:T(8,128)(2,1)}, bf16[256,1024]{1,0:T(8,128)(2,1)S(1)}, u32[]{:S(2)}, u32[]{:S(2)}) collective-permute-start(bf16[256,1024]{1,0:T(8,128)(2,1)} %shard_map.117.k_ref.refs_8_), channel_id=1, source_target_pairs={{6,0},{0,2},{2,4},{4,6},{14,8},{8,10},{10,12},{12,14},{22,16},{16,... | collective-permute-start | bytes 1572872 | tf_op jit(solution)/shard_map/ppermute | solution.py:43
  108.6 24.2 %collective-permute-start.21 = (bf16[256,1024]{1,0:T(8,128)(2,1)}, bf16[256,1024]{1,0:T(8,128)(2,1)S(1)}, u32[]{:S(2)}, u32[]{:S(2)}) collective-permute-start(bf16[256,1024]{1,0:T(8,128)(2,1)} %shard_map.117.k_ref.refs_8_), channel_id=1, source_target_pairs={{4,0},{6,2},{0,4},{2,6},{12,8},{14,10},{8,12},{10,14},{20,16},{22,... | collective-permute-start | bytes 1572872 | tf_op jit(solution)/shard_map/ppermute | solution.py:43
  110.0 22.8 %copy-start.34 = (bf16[256,1024]{1,0:T(8,128)(2,1)}, bf16[256,1024]{1,0:T(8,128)(2,1)S(1)}, u32[]{:S(2)}) copy-start(bf16[256,1024]{1,0:T(8,128)(2,1)S(1)} %collective-permute-done.17.o_ref) | copy-start | bytes 1572868
  121.3 11.4 %copy-start.19 = (bf16[256,1024]{1,0:T(8,128)(2,1)}, bf16[256,1024]{1,0:T(8,128)(2,1)S(1)}, u32[]{:S(2)}) copy-start(bf16[256,1024]{1,0:T(8,128)(2,1)S(1)} %collective-permute-done.18.refs_8_.refs_11_) | copy-start | bytes 1572868
  121.3 11.4 %copy-start.20 = (bf16[256,1024]{1,0:T(8,128)(2,1)}, bf16[256,1024]{1,0:T(8,128)(2,1)S(1)}, u32[]{:S(2)}) copy-start(bf16[256,1024]{1,0:T(8,128)(2,1)S(1)} %collective-permute-done.19.refs_9_.refs_10_) | copy-start | bytes 1572868
  123.9 8.8 %copy-start.21 = (bf16[256,1024]{1,0:T(8,128)(2,1)}, bf16[256,1024]{1,0:T(8,128)(2,1)S(1)}, u32[]{:S(2)}) copy-start(bf16[256,1024]{1,0:T(8,128)(2,1)S(1)} %collective-permute-done.20.refs_10_.refs_9_) | copy-start | bytes 1572868
  141.5 10.8 %collective-permute-start.22 = (bf16[256,2560]{1,0:T(8,128)(2,1)}, bf16[256,2560]{1,0:T(8,128)(2,1)S(1)}, u32[]{:S(2)}, u32[]{:S(2)}) collective-permute-start(bf16[256,2560]{1,0:T(8,128)(2,1)} %get-tuple-element.31), channel_id=1, source_target_pairs={{8,0},{10,2},{12,4},{14,6},{0,8},{2,10},{4,12},{6,14},{24,16},{26,... | collective-permute-start | bytes 3932168 | tf_op jit(solution)/shard_map/ppermute | solution.py:43
  145.1 15.0 %collective-permute-start.23 = (bf16[256,1024]{1,0:T(8,128)(2,1)}, bf16[256,1024]{1,0:T(8,128)(2,1)S(1)}, u32[]{:S(2)}, u32[]{:S(2)}) collective-permute-start(bf16[256,1024]{1,0:T(8,128)(2,1)} %copy-done.19), channel_id=1, source_target_pairs={{6,0},{0,2},{2,4},{4,6},{14,8},{8,10},{10,12},{12,14},{22,16},{16,... | collective-permute-start | bytes 1572872 | tf_op jit(solution)/shard_map/ppermute | solution.py:43
  145.1 15.0 %collective-permute-start.24 = (bf16[256,1024]{1,0:T(8,128)(2,1)}, bf16[256,1024]{1,0:T(8,128)(2,1)S(1)}, u32[]{:S(2)}, u32[]{:S(2)}) collective-permute-start(bf16[256,1024]{1,0:T(8,128)(2,1)} %copy-done.19), channel_id=1, source_target_pairs={{2,0},{4,2},{6,4},{0,6},{10,8},{12,10},{14,12},{8,14},{18,16},{20,... | collective-permute-start | bytes 1572872 | tf_op jit(solution)/shard_map/ppermute | solution.py:43
  147.8 14.6 %collective-permute-start.25 = (bf16[256,1024]{1,0:T(8,128)(2,1)}, bf16[256,1024]{1,0:T(8,128)(2,1)S(1)}, u32[]{:S(2)}, u32[]{:S(2)}) collective-permute-start(bf16[256,1024]{1,0:T(8,128)(2,1)} %copy-done.22), channel_id=1, source_target_pairs={{1,0},{3,2},{5,4},{7,6},{9,8},{11,10},{13,12},{15,14},{17,16},{19,... | collective-permute-start | bytes 1572872 | tf_op jit(solution)/shard_map/ppermute | solution.py:43
  152.3 1.1 copy-start.11
  160.1 2.3 %copy-start.23 = (bf16[256,1024]{1,0:T(8,128)(2,1)}, bf16[256,1024]{1,0:T(8,128)(2,1)S(1)}, u32[]{:S(2)}) copy-start(bf16[256,1024]{1,0:T(8,128)(2,1)S(1)} %collective-permute-done.23.refs_13_) | copy-start | bytes 1572868
  160.1 2.3 %copy-start.24 = (bf16[256,1024]{1,0:T(8,128)(2,1)}, bf16[256,1024]{1,0:T(8,128)(2,1)S(1)}, u32[]{:S(2)}) copy-start(bf16[256,1024]{1,0:T(8,128)(2,1)S(1)} %collective-permute-done.24.refs_14_) | copy-start | bytes 1572868
  175.8 9.8 %collective-permute-start.26 = (bf16[320,128]{1,0:T(8,128)(2,1)}, bf16[320,128]{1,0:T(8,128)(2,1)S(1)}, u32[]{:S(2)}, u32[]{:S(2)}) collective-permute-start(bf16[320,128]{1,0:T(8,128)(2,1)} %get-tuple-element.36), channel_id=1, source_target_pairs={{8,0},{10,2},{12,4},{14,6},{0,8},{2,10},{4,12},{6,14},{24,16},{26,... | collective-permute-start | bytes 245768 | tf_op jit(solution)/shard_map/ppermute | solution.py:43
  177.4 8.3 %collective-permute-start.27 = (bf16[320,128]{1,0:T(8,128)(2,1)}, bf16[320,128]{1,0:T(8,128)(2,1)S(1)}, u32[]{:S(2)}, u32[]{:S(2)}) collective-permute-start(bf16[320,128]{1,0:T(8,128)(2,1)} %get-tuple-element.37), channel_id=1, source_target_pairs={{16,0},{18,2},{20,4},{22,6},{24,8},{26,10},{28,12},{30,14},{0,16},... | collective-permute-start | bytes 245768 | tf_op jit(solution)/shard_map/ppermute | solution.py:43
  180.1 5.6 %collective-permute-start.28 = (bf16[320,128]{1,0:T(8,128)(2,1)}, bf16[320,128]{1,0:T(8,128)(2,1)S(1)}, u32[]{:S(2)}, u32[]{:S(2)}) collective-permute-start(bf16[320,128]{1,0:T(8,128)(2,1)} %get-tuple-element.38), channel_id=1, source_target_pairs={{24,0},{26,2},{28,4},{30,6},{16,8},{18,10},{20,12},{22,14},{8,16},... | collective-permute-start | bytes 245768 | tf_op jit(solution)/shard_map/ppermute | solution.py:43
  188.1 7.9 %collective-permute-start.29 = (bf16[320,128]{1,0:T(8,128)(2,1)}, bf16[320,128]{1,0:T(8,128)(2,1)S(1)}, u32[]{:S(2)}, u32[]{:S(2)}) collective-permute-start(bf16[320,128]{1,0:T(8,128)(2,1)} %shard_map.122), channel_id=1, source_target_pairs={{32,0},{34,2},{36,4},{38,6},{40,8},{42,10},{44,12},{46,14},{48,16}... | collective-permute-start | bytes 245768 | tf_op jit(solution)/shard_map/ppermute | solution.py:43
  196.9 5.7 %collective-permute-start.30 = (bf16[320,128]{1,0:T(8,128)(2,1)S(1)}, bf16[320,128]{1,0:T(8,128)(2,1)S(1)}, u32[]{:S(2)}, u32[]{:S(2)}) collective-permute-start(bf16[320,128]{1,0:T(8,128)(2,1)S(1)} %add_convert_fusion.1), channel_id=1, source_target_pairs={{64,0},{66,2},{68,4},{70,6},{72,8},{74,10},{76,12},{78,14},{80,16}... | collective-permute-start | bytes 245768 | tf_op jit(solution)/shard_map/ppermute | solution.py:43
  197.0 7.7 %collective-permute-start.31 = (bf16[320,128]{1,0:T(8,128)(2,1)S(1)}, bf16[320,128]{1,0:T(8,128)(2,1)S(1)}, u32[]{:S(2)}, u32[]{:S(2)}) collective-permute-start(bf16[320,128]{1,0:T(8,128)(2,1)S(1)} %add_convert_fusion.1), channel_id=1, source_target_pairs={{128,0},{130,2},{132,4},{134,6},{136,8},{138,10},{140,12},{142,14}... | collective-permute-start | bytes 245768 | tf_op jit(solution)/shard_map/ppermute | solution.py:43
  201.0 9.6 %collective-permute-start.32 = (bf16[320,128]{1,0:T(8,128)(2,1)S(1)}, bf16[320,128]{1,0:T(8,128)(2,1)S(1)}, u32[]{:S(2)}, u32[]{:S(2)}) collective-permute-start(bf16[320,128]{1,0:T(8,128)(2,1)S(1)} %add_convert_fusion.1), channel_id=1, source_target_pairs={{192,0},{194,2},{196,4},{198,6},{200,8},{202,10},{204,12},{206,14}... | collective-permute-start | bytes 245768 | tf_op jit(solution)/shard_map/ppermute | solution.py:43
  210.6 6.8 %copy-start.26 = (bf16[320,128]{1,0:T(8,128)(2,1)}, bf16[320,128]{1,0:T(8,128)(2,1)S(1)}, u32[]{:S(2)}) copy-start(bf16[320,128]{1,0:T(8,128)(2,1)S(1)} %add_convert_fusion.a) | copy-start | bytes 245764
  210.6 2.5 %collective-permute-start.33 = (bf16[320,128]{1,0:T(8,128)(2,1)S(1)}, bf16[320,128]{1,0:T(8,128)(2,1)S(1)}, u32[]{:S(2)}, u32[]{:S(2)}) collective-permute-start(bf16[320,128]{1,0:T(8,128)(2,1)S(1)} %add_convert_fusion.a), channel_id=1, source_target_pairs={{8,0},{10,2},{12,4},{14,6},{0,8},{2,10},{4,12},{6,14},{24,16},{26,... | collective-permute-start | bytes 245768 | tf_op jit(solution)/shard_map/ppermute | solution.py:43
  211.4 4.0 %collective-permute-start.34 = (bf16[320,128]{1,0:T(8,128)(2,1)S(1)}, bf16[320,128]{1,0:T(8,128)(2,1)S(1)}, u32[]{:S(2)}, u32[]{:S(2)}) collective-permute-start(bf16[320,128]{1,0:T(8,128)(2,1)S(1)} %add_convert_fusion.a), channel_id=1, source_target_pairs={{16,0},{18,2},{20,4},{22,6},{24,8},{26,10},{28,12},{30,14},{0,16},... | collective-permute-start | bytes 245768 | tf_op jit(solution)/shard_map/ppermute | solution.py:43
  211.4 5.9 %collective-permute-start.35 = (bf16[320,128]{1,0:T(8,128)(2,1)S(1)}, bf16[320,128]{1,0:T(8,128)(2,1)S(1)}, u32[]{:S(2)}, u32[]{:S(2)}) collective-permute-start(bf16[320,128]{1,0:T(8,128)(2,1)S(1)} %add_convert_fusion.a), channel_id=1, source_target_pairs={{24,0},{26,2},{28,4},{30,6},{16,8},{18,10},{20,12},{22,14},{8,16},... | collective-permute-start | bytes 245768 | tf_op jit(solution)/shard_map/ppermute | solution.py:43
  213.1 4.2 %copy-start.30 = (bf16[320,128]{1,0:T(8,128)(2,1)}, bf16[320,128]{1,0:T(8,128)(2,1)S(1)}, u32[]{:S(2)}) copy-start(bf16[320,128]{1,0:T(8,128)(2,1)S(1)} %collective-permute-done.33.b) | copy-start | bytes 245764
  215.4 1.9 copy-start.31
  (7 other events, 4.9 us)

commit v3 on v2

--- a/solution.py
+++ b/solution.py
@@ -201,7 +201,7 @@
             out_specs=full,
         ),
         out_shape=jax.ShapeDtypeStruct((TOK, KV), bf16),
-        compiler_params=params(),
+        compiler_params=params(32),
         cost_estimate=pl.CostEstimate(flops=10 * TOK * KV, bytes_accessed=TOK * KV * 12, transcendentals=TOK),
     )(info, mine, arrived, cotangent, cotangent, gain, gain, *after)
 
@@ -346,8 +346,8 @@
     )(own, *parts, after)
 
 
-def normalized_update(info, quarters, tables, ones):
-    def kernel(info_ref, a, b, c, d, left_ref, right_ref, ones_ref, out_ref):
+def normalized_update(info, quarters, tables, ones, after):
+    def kernel(info_ref, a, b, c, d, left_ref, right_ref, ones_ref, _, out_ref):
         for k, ref in enumerate((a, b, c, d)):
             corner = ref[...].astype(f32)
             energy = jnp.sum((corner * corner).reshape(10, 32, 128), axis=1)
@@ -360,11 +360,11 @@
 
     return pl.pallas_call(
         kernel,
-        in_specs=[SMEM] + [VMEM] * 7,
+        in_specs=[SMEM] + [VMEM] * 7 + [ANY],
         out_specs=VMEM,
         out_shape=jax.ShapeDtypeStruct((ROWS, KV), bf16),
         compiler_params=params(),
-    )(info, *quarters, *tables, ones)
+    )(info, *quarters, *tables, ones, after)
 
 
 def per_device(tokens, cotangent, weight, momentum, gain, band):
@@ -429,7 +429,7 @@
 
     keys[0, 0] = key_grad
     blended, corner, quarter, *parts = blend(
-        info, arrived, [keys[(-dy) % 4, dx] for dy, dx in AWAY], momentum, mask, tables, input_grad
+        info, arrived, [keys[(-dy) % 4, dx] for dy, dx in AWAY], momentum, mask, tables, mine
     )
     residue = remove_corner(blended, corner, tables)
 
@@ -445,7 +445,7 @@
     p4, p2, p6 = (pull_z(summed, flip) for flip in (4, 2, 6))
     summed = ((summed.astype(f32) + p2) + (p4 + p6)).astype(bf16)
     quarters = [summed] + [pull(summed, group_source(k)) for k in (1, 2, 3)]
-    update = normalized_update(info, quarters, tables, ones)
+    update = normalized_update(info, quarters, tables, ones, input_grad)
     return (input_grad[None], residue[None], update)
 
 

time: 223 us -> 203 us (0.910)
  waiting for transfers between devices: 74.6 us -> 61.8 us
  starting transfers between devices: 77.7 us -> 73 us
  Pallas kernels: 59.8 us -> 57.3 us
    ppermute x36, waiting for transfers between devices: 74.6 us -> 61.8 us  [pull(): return lax.ppermute(value, ('rep', 'shard'), pairs)]
    ppermute x36, starting transfers between devices: 77.7 us -> 73 us  [pull(): return lax.ppermute(value, ('rep', 'shard'), pairs)]
    pallas_call x1, Pallas kernels: 3.56 us -> 0.96 us  [key_gradient(): pl.pallas_call(kernel, grid_spec=pltpu.PrefetchScalarGridSpec(num_scalar_...]
  transfers between devices with their start and end apart: 36 -> 36, of which waited for: 17 -> 13; matrix products, arithmetic and copies ran while one was open for 1% -> 1% of each run, Pallas kernels for 8% -> 20%
where the time goes in v3:
time: 203 us; the launch traced here: 202 us
  starting transfers between devices  73 us (36%)
  waiting for transfers between devices  61.8 us (30%)
  Pallas kernels  57.3 us (28%)
  local copies, waits for them, and re-layouts  7.74 us (4%)
    ppermute x36, starting transfers between devices, pull(): return lax.ppermute(value, ('rep', 'shard'), pairs)  73 us
    ppermute x36, waiting for transfers between devices, pull(): return lax.ppermute(value, ('rep', 'shard'), pairs)  61.8 us
    pallas_call x1, Pallas kernels, blend(): pl.pallas_call(kernel, grid_spec=pltpu.PrefetchScalarGridSpec(num_scalar_...  12.6 us
    pallas_call x4, Pallas kernels, cut_columns(): pl.pallas_call(kernel, grid_spec=pltpu.PrefetchScalarGridSpec(num_scalar_...  12.2 us
    pallas_call x1, Pallas kernels, project(): pl.pallas_call(kernel, in_specs=[SMEM, ANY, ANY, VMEM] + [ANY] * (8 + len...  8.71 us
    pallas_call x1, Pallas kernels, token_gradient(): pl.pallas_call(kernel, in_specs=[SMEM] + [VMEM] * 11 + [ANY] * len(after)...  7.91 us
    unnamed x70, local copies, waits for them, and re-layouts  5.9 us
    pallas_call x1, Pallas kernels, remove_corner(): pl.pallas_call(kernel, grid=(4,), in_specs=[pl.BlockSpec((ROWS, 256), lam...  5.44 us
  transfers between devices with their start and end apart: 36, of which 13 were waited for; matrix products, arithmetic and copies ran while one was open for 1% of the time, Pallas kernels for 20%

profile of v3, /device:TPU:1, one launch (start us, length us, event | category | flops | bytes accessed | tf_op | source)
XLA Modules:
  0.0 202.4 jit_solution(1126904777981180499)
XLA Ops:
  0.8 0.6 stack.83.info_ref.s_ref
  1.4 2.6 %shard_map.112.refs_4_ = bf16[640,512]{1,0:T(8,128)(2,1)} custom-call(s32[20]{0:T(128)} %stack.83.info_ref.s_ref, bf16[640,1024]{1,0:T(8,128)(2,1)} %own_ref.3), custom_call_target="tpu_custom_call" | custom-call | bytes 1310720 | tf_op jit(solution)/shard_map/pallas_call | solution.py:103
  4.0 3.3 %collective-permute-start.1 = (bf16[640,512]{1,0:T(8,128)(2,1)}, bf16[640,512]{1,0:T(8,128)(2,1)S(1)}, u32[]{:S(2)}, u32[]{:S(2)}) collective-permute-start(bf16[640,512]{1,0:T(8,128)(2,1)} %shard_map.112.refs_4_), channel_id=1, source_target_pairs={{2,0},{4,2},{6,4},{0,6},{25,8},{27,10},{29,12},{31,14},{18,16},{20... | collective-permute-start | bytes 1966088 | tf_op jit(solution)/shard_map/ppermute | solution.py:43
  7.3 2.6 %collective-permute-start.2 = (bf16[640,512]{1,0:T(8,128)(2,1)}, bf16[640,512]{1,0:T(8,128)(2,1)S(1)}, u32[]{:S(2)}, u32[]{:S(2)}) collective-permute-start(bf16[640,512]{1,0:T(8,128)(2,1)} %shard_map.112.refs_4_), channel_id=1, source_target_pairs={{6,0},{0,2},{2,4},{4,6},{27,8},{29,10},{31,12},{25,14},{22,16},{16... | collective-permute-start | bytes 1966088 | tf_op jit(solution)/shard_map/ppermute | solution.py:43
  10.0 0.9 collective-permute-start.3
  10.9 3.2 %shard_map.113 = bf16[256,2560]{1,0:T(8,128)(2,1)} custom-call(s32[20]{0:T(128)} %stack.83.info_ref.s_ref, bf16[256,5120]{1,0:T(8,128)(2,1)} %bitcast.30, bf16[256,5120]{1,0:T(8,128)(2,1)} %bitcast.31, bf16[256,5120]{1,0:T(8,128)(2,1)} %bitcast.32, bf16[256,5120]{1,0:T(8,128)(2,1)} %bitcast.33, bf16[640,512]{1,0:T(8,128)(2,1)} %shard_map.112.refs_4_), custom_call_target="tpu_custom_call" | custom-call | bytes 2621440 | tf_op jit(solution)/shard_map/pallas_call | solution.py:103
  14.1 5.0 %collective-permute-start.4 = (bf16[640,512]{1,0:T(8,128)(2,1)S(1)}, bf16[640,512]{1,0:T(8,128)(2,1)S(1)}, u32[]{:S(2)}, u32[]{:S(2)}) collective-permute-start(bf16[640,512]{1,0:T(8,128)(2,1)S(1)} %copy-done.7), channel_id=1, source_target_pairs={{29,8},{31,10},{25,12},{27,14},{13,24},{15,26},{9,28},{11,30},{28,... | collective-permute-start | bytes 1966088 | tf_op jit(solution)/shard_map/ppermute | solution.py:43
  19.1 1.7 collective-permute-start.5
  20.9 3.1 %shard_map.114 = (bf16[640,256]{1,0:T(8,128)(2,1)}, bf16[640,256]{1,0:T(8,128)(2,1)}, bf16[640,256]{1,0:T(8,128)(2,1)}, bf16[640,256]{1,0:T(8,128)(2,1)}) custom-call(s32[20]{0:T(128)} %stack.83.info_ref.s_ref, bf16[256,5120]{1,0:T(8,128)(2,1)} %bitcast.34, bf16[256,5120]{1,0:T(8,128)(2,1)} %bitcast.35, bf16[256,5120]{1,0:T(8,128)(2,1)} %bitcast.36, ...), custom_call_target="tpu_custom_call" | custom-call | bytes 2621440 | tf_op jit(solution)/shard_map/pallas_call | solution.py:103
  24.1 3.0 %collective-permute-start.10 = (bf16[640,256]{1,0:T(8,128)(2,1)}, bf16[640,256]{1,0:T(8,128)(2,1)S(1)}, u32[]{:S(2)}, u32[]{:S(2)}) collective-permute-start(bf16[640,256]{1,0:T(8,128)(2,1)} %get-tuple-element.22), channel_id=1, source_target_pairs={{2,0},{4,2},{6,4},{0,6},{10,8},{12,10},{14,12},{8,14},{18,16},{20,... | collective-permute-start | bytes 983048 | tf_op jit(solution)/shard_map/ppermute | solution.py:43
  27.0 5.9 %collective-permute-done.3.refs_2_ = bf16[640,512]{1,0:T(8,128)(2,1)S(1)} collective-permute-done((bf16[640,512]{1,0:T(8,128)(2,1)}, bf16[640,512]{1,0:T(8,128)(2,1)S(1)}, u32[]{:S(2)}, u32[]{:S(2)}) %collective-permute-start.3) | collective-permute-done | bytes 655392 | tf_op jit(solution)/shard_map/ppermute | solution.py:43
  33.0 1.4 collective-permute-start.11
  34.4 9.3 %collective-permute-done.4.refs_3_ = bf16[640,512]{1,0:T(8,128)(2,1)S(1)} collective-permute-done((bf16[640,512]{1,0:T(8,128)(2,1)S(1)}, bf16[640,512]{1,0:T(8,128)(2,1)S(1)}, u32[]{:S(2)}, u32[]{:S(2)}) %collective-permute-start.4) | collective-permute-done | bytes 655392 | tf_op jit(solution)/shard_map/ppermute | solution.py:43
  43.7 1.6 collective-permute-start.6
  45.3 1.6 collective-permute-start.7
  47.0 0.6 collective-permute-start.9
  47.5 4.0 %collective-permute-start.8 = (bf16[640,512]{1,0:T(8,128)(2,1)S(1)}, bf16[640,512]{1,0:T(8,128)(2,1)}, u32[]{:S(2)}, u32[]{:S(2)}) collective-permute-start(bf16[640,512]{1,0:T(8,128)(2,1)S(1)} %collective-permute-done.4.refs_3_), channel_id=1, source_target_pairs={{232,8},{234,10},{236,12},{238,14},{248,24},{250,26},{252,28},{254... | collective-permute-start | bytes 1966088 | tf_op jit(solution)/shard_map/ppermute | solution.py:43
  51.5 3.2 %shard_map.115 = (bf16[640,256]{1,0:T(8,128)(2,1)}, bf16[640,256]{1,0:T(8,128)(2,1)}, bf16[640,256]{1,0:T(8,128)(2,1)}, bf16[640,256]{1,0:T(8,128)(2,1)}) custom-call(s32[20]{0:T(128)} %stack.83.info_ref.s_ref, bf16[256,5120]{1,0:T(8,128)(2,1)} %bitcast.38, bf16[256,5120]{1,0:T(8,128)(2,1)} %bitcast.39, bf16[256,5120]{1,0:T(8,128)(2,1)} %bitcast.40, ...), custom_call_target="tpu_custom_call" | custom-call | bytes 2621440 | tf_op jit(solution)/shard_map/pallas_call | solution.py:103
  54.7 1.5 collective-permute-start.12
  56.2 1.5 collective-permute-start.13
  57.6 3.6 %collective-permute-start.14 = (bf16[640,256]{1,0:T(8,128)(2,1)}, bf16[640,256]{1,0:T(8,128)(2,1)S(1)}, u32[]{:S(2)}, u32[]{:S(2)}) collective-permute-start(bf16[640,256]{1,0:T(8,128)(2,1)} %get-tuple-element.26), channel_id=1, source_target_pairs={{3,0},{5,2},{7,4},{1,6},{11,8},{13,10},{15,12},{9,14},{19,16},{21,... | collective-permute-start | bytes 983048 | tf_op jit(solution)/shard_map/ppermute | solution.py:43
  61.2 3.3 %collective-permute-done.7.refs_6_ = bf16[640,512]{1,0:T(8,128)(2,1)S(1)} collective-permute-done((bf16[640,512]{1,0:T(8,128)(2,1)S(1)}, bf16[640,512]{1,0:T(8,128)(2,1)S(1)}, u32[]{:S(2)}, u32[]{:S(2)}) %collective-permute-start.7) | collective-permute-done | bytes 655392 | tf_op jit(solution)/shard_map/ppermute | solution.py:43
  64.8 6.5 %collective-permute-done.8.refs_7_ = bf16[640,512]{1,0:T(8,128)(2,1)} collective-permute-done((bf16[640,512]{1,0:T(8,128)(2,1)S(1)}, bf16[640,512]{1,0:T(8,128)(2,1)}, u32[]{:S(2)}, u32[]{:S(2)}) %collective-permute-start.8) | collective-permute-done | bytes 655392 | tf_op jit(solution)/shard_map/ppermute | solution.py:43
  71.4 3.4 %collective-permute-done.15.refs_14_.refs_7_ = bf16[640,256]{1,0:T(8,128)(2,1)S(1)} collective-permute-done((bf16[640,256]{1,0:T(8,128)(2,1)}, bf16[640,256]{1,0:T(8,128)(2,1)S(1)}, u32[]{:S(2)}, u32[]{:S(2)}) %collective-permute-start.15) | collective-permute-done | bytes 327712 | tf_op jit(solution)/shard_map/ppermute | solution.py:43
  75.0 0.7 copy-done.14
  75.7 8.7 %shard_map.116 = (f32[256,1024]{1,0:T(8,128)}, f32[256,1024]{1,0:T(8,128)}) custom-call(s32[20]{0:T(128)} %stack.83.info_ref.s_ref, bf16[256,5120]{1,0:T(8,128)(2,1)} %bitcast.42, bf16[256,2560]{1,0:T(8,128)(2,1)} %copy-done.15, bf16[640,1024]{1,0:T(8,128)(2,1)} %own_ref.3, bf16[640,512]{1,0:T(8,128)(2,1)} %copy-done.5, bf16[640,512]{1,0:T(8,128)(2,1)} %copy-done.17, ...), custom_call_target="tpu_custom_call" | custom-call | flops 2684354560 | bytes 13107200 | tf_op jit(solution)/shard_map/pallas_call | solution.py:155
  84.4 14.4 %collective-permute-start.16 = (f32[256,1024]{1,0:T(8,128)}, f32[256,1024]{1,0:T(8,128)S(1)}, u32[]{:S(2)}, u32[]{:S(2)}) collective-permute-start(f32[256,1024]{1,0:T(8,128)} %get-tuple-element.29), channel_id=1, source_target_pairs={{8,0},{10,2},{12,4},{14,6},{0,8},{2,10},{4,12},{6,14},{24,16},{26,... | collective-permute-start | bytes 3145736 | tf_op jit(solution)/shard_map/ppermute | solution.py:43
  98.8 2.5 %collective-permute-done.16.r_ref = f32[256,1024]{1,0:T(8,128)S(1)} collective-permute-done((f32[256,1024]{1,0:T(8,128)}, f32[256,1024]{1,0:T(8,128)S(1)}, u32[]{:S(2)}, u32[]{:S(2)}) %collective-permute-start.16) | collective-permute-done | bytes 1048608 | tf_op jit(solution)/shard_map/ppermute | solution.py:43
  101.3 1.2 copy-done.2
  102.6 1.0 shard_map.117.k_ref.refs_8_
  103.5 1.0 collective-permute-start.18
  104.5 0.7 collective-permute-start.17
  105.2 1.4 collective-permute-start.21
  106.6 1.7 collective-permute-start.19
  108.3 10.0 %collective-permute-done.18.refs_8_.refs_11_ = bf16[256,1024]{1,0:T(8,128)(2,1)S(1)} collective-permute-done((bf16[256,1024]{1,0:T(8,128)(2,1)S(1)}, bf16[256,1024]{1,0:T(8,128)(2,1)S(1)}, u32[]{:S(2)}, u32[]{:S(2)}) %collective-permute-start.18) | collective-permute-done | bytes 524320 | tf_op jit(solution)/shard_map/ppermute | solution.py:43
  118.3 0.6 collective-permute-start.23
  118.8 2.1 %collective-permute-start.24 = (bf16[256,1024]{1,0:T(8,128)(2,1)S(1)}, bf16[256,1024]{1,0:T(8,128)(2,1)}, u32[]{:S(2)}, u32[]{:S(2)}) collective-permute-start(bf16[256,1024]{1,0:T(8,128)(2,1)S(1)} %collective-permute-done.18.refs_8_.refs_11_), channel_id=1, source_target_pairs={{2,0},{4,2},{6,4},{0,6},{10,8},{12,10},{14,12},{8,14},{18,16},{20,... | collective-permute-start | bytes 1572872 | tf_op jit(solution)/shard_map/ppermute | solution.py:43
  120.9 1.4 collective-permute-start.25
  122.4 8.3 %collective-permute-done.19.refs_9_.refs_10_ = bf16[256,1024]{1,0:T(8,128)(2,1)S(1)} collective-permute-done((bf16[256,1024]{1,0:T(8,128)(2,1)S(1)}, bf16[256,1024]{1,0:T(8,128)(2,1)S(1)}, u32[]{:S(2)}, u32[]{:S(2)}) %collective-permute-start.19) | collective-permute-done | bytes 524320 | tf_op jit(solution)/shard_map/ppermute | solution.py:43
  130.7 1.2 collective-permute-done.20.refs_10_.refs_9_
  131.9 0.9 copy-done.25
  132.8 7.9 %shard_map.118 = (bf16[256,2560]{1,0:T(8,128)(2,1)}, bf16[256,2560]{1,0:T(8,128)(2,1)}) custom-call(s32[20]{0:T(128)} %stack.83.info_ref.s_ref, bf16[256,1024]{1,0:T(8,128)(2,1)} %copy-done, bf16[256,1024]{1,0:T(8,128)(2,1)} %copy-done.34, bf16[640,1024]{1,0:T(8,128)(2,1)} %own_ref.3, bf16[640,512]{1,0:T(8,128)(2,1)} %copy-done.5, ...), custom_call_target="tpu_custom_call" | custom-call | flops 2684354560 | bytes 13107200 | tf_op jit(solution)/shard_map/pallas_call | solution.py:222
  140.7 0.7 collective-permute-start.22
  142.2 1.0 tile.9.refs_17_
  143.2 12.6 %shard_map.120 = (f32[640,1024]{1,0:T(8,128)}, f32[4,320,128]{2,1,0:T(8,128)}, f32[320,128]{1,0:T(8,128)}, bf16[320,128]{1,0:T(8,128)(2,1)}, bf16[320,128]{1,0:T(8,128)(2,1)}, /*index=5*/bf16[320,128]{1,0:T(8,128)(2,1)}) custom-call(s32[20]{0:T(128)} %stack.83.info_ref.s_ref, bf16[640,256]{1,0:T(8,128)(2,1)} %get-tuple-element.32.refs_0_, ...), custom_call_target="tpu_custom_call" | custom-call | flops 2684354560 | bytes 12058624 | tf_op jit(solution)/shard_map/pallas_call | solution.py:299
  155.8 0.5 collective-permute-start.26
  156.3 2.4 %collective-permute-start.27 = (bf16[320,128]{1,0:T(8,128)(2,1)}, bf16[320,128]{1,0:T(8,128)(2,1)S(1)}, u32[]{:S(2)}, u32[]{:S(2)}) collective-permute-start(bf16[320,128]{1,0:T(8,128)(2,1)} %get-tuple-element.37), channel_id=1, source_target_pairs={{16,0},{18,2},{20,4},{22,6},{24,8},{26,10},{28,12},{30,14},{0,16},... | collective-permute-start | bytes 245768 | tf_op jit(solution)/shard_map/ppermute | solution.py:43
  159.1 5.4 %shard_map.121._ = f32[640,1024]{1,0:T(8,128)} custom-call(f32[640,1024]{1,0:T(8,128)} %get-tuple-element.33.blended_ref, f32[4,320,128]{2,1,0:T(8,128)} %get-tuple-element.34.corner_ref, bf16[2,64,128]{2,1,0:T(8,128)(2,1)} %constant.128.clone.refs_18_.left_ref, bf16[2,256,128]{2,1,0:T(8,128)(2,1)} %constant.129.clone.refs_19_.right_ref), custom_call_target="tpu_custom_call" | custom-call | flops 335544320 | bytes 5242880 | tf_op jit(solution)/shard_map/pallas_call | solution.py:320
  164.6 0.6 copy-done.27
  165.2 1.7 shard_map.122
  166.9 5.1 %collective-permute-start.29 = (bf16[320,128]{1,0:T(8,128)(2,1)}, bf16[320,128]{1,0:T(8,128)(2,1)S(1)}, u32[]{:S(2)}, u32[]{:S(2)}) collective-permute-start(bf16[320,128]{1,0:T(8,128)(2,1)} %shard_map.122), channel_id=1, source_target_pairs={{32,0},{34,2},{36,4},{38,6},{40,8},{42,10},{44,12},{46,14},{48,16}... | collective-permute-start | bytes 245768 | tf_op jit(solution)/shard_map/ppermute | solution.py:43
  172.0 3.1 %collective-permute-done.29 = bf16[320,128]{1,0:T(8,128)(2,1)S(1)} collective-permute-done((bf16[320,128]{1,0:T(8,128)(2,1)}, bf16[320,128]{1,0:T(8,128)(2,1)S(1)}, u32[]{:S(2)}, u32[]{:S(2)}) %collective-permute-start.29) | collective-permute-done | bytes 81952 | tf_op jit(solution)/shard_map/ppermute | solution.py:43
  175.2 0.9 add_convert_fusion.1
  176.2 3.8 %collective-permute-start.31 = (bf16[320,128]{1,0:T(8,128)(2,1)S(1)}, bf16[320,128]{1,0:T(8,128)(2,1)S(1)}, u32[]{:S(2)}, u32[]{:S(2)}) collective-permute-start(bf16[320,128]{1,0:T(8,128)(2,1)S(1)} %add_convert_fusion.1), channel_id=1, source_target_pairs={{128,0},{130,2},{132,4},{134,6},{136,8},{138,10},{140,12},{142,14}... | collective-permute-start | bytes 245768 | tf_op jit(solution)/shard_map/ppermute | solution.py:43
  179.9 1.9 collective-permute-start.32
  181.8 2.0 collective-permute-done.31
  183.8 6.0 %collective-permute-done.32 = bf16[320,128]{1,0:T(8,128)(2,1)S(1)} collective-permute-done((bf16[320,128]{1,0:T(8,128)(2,1)S(1)}, bf16[320,128]{1,0:T(8,128)(2,1)S(1)}, u32[]{:S(2)}, u32[]{:S(2)}) %collective-permute-start.32) | collective-permute-done | bytes 81952 | tf_op jit(solution)/shard_map/ppermute | solution.py:43
  189.9 0.6 collective-permute-start.33
  191.0 1.2 collective-permute-start.35
  192.3 1.1 copy-done.16
  193.3 3.4 %shard_map.119._ = bf16[256,5120]{1,0:T(8,128)(2,1)} custom-call(s32[20]{0:T(128)} %stack.83.info_ref.s_ref, bf16[256,2560]{1,0:T(8,128)(2,1)} %get-tuple-element.30.m_ref.refs_20_, bf16[256,2560]{1,0:T(8,128)(2,1)} %copy-done.16), custom_call_target="tpu_custom_call" | custom-call | bytes 5242880 | tf_op jit(solution)/shard_map/pallas_call | solution.py:239
  196.8 0.6 copy-done.30
  197.4 0.6 copy-done.32
  198.1 4.4 %shard_map.123 = bf16[640,1024]{1,0:T(8,128)(2,1)} custom-call(s32[20]{0:T(128)} %stack.83.info_ref.s_ref, bf16[320,128]{1,0:T(8,128)(2,1)} %copy-done.26, bf16[320,128]{1,0:T(8,128)(2,1)} %copy-done.30, bf16[320,128]{1,0:T(8,128)(2,1)} %copy-done.31, bf16[320,128]{1,0:T(8,128)(2,1)} %copy-done.32, bf16[2,64,128]{2,1,0:T(8,128)(2,1)} %constant.128.clone.refs_18_.left_ref, ...), custom_call_target="tpu_custom_call" | custom-call | tf_op jit(solution)/shard_map/pallas_call | solution.py:361
  (101 shorter events, 2.4 us)
Async XLA Ops:
  4.0 15.1 %collective-permute-start.1 = (bf16[640,512]{1,0:T(8,128)(2,1)}, bf16[640,512]{1,0:T(8,128)(2,1)S(1)}, u32[]{:S(2)}, u32[]{:S(2)}) collective-permute-start(bf16[640,512]{1,0:T(8,128)(2,1)} %shard_map.112.refs_4_), channel_id=1, source_target_pairs={{2,0},{4,2},{6,4},{0,6},{25,8},{27,10},{29,12},{31,14},{18,16},{20... | collective-permute-start | bytes 1966088 | tf_op jit(solution)/shard_map/ppermute | solution.py:43
  7.3 16.7 %collective-permute-start.2 = (bf16[640,512]{1,0:T(8,128)(2,1)}, bf16[640,512]{1,0:T(8,128)(2,1)S(1)}, u32[]{:S(2)}, u32[]{:S(2)}) collective-permute-start(bf16[640,512]{1,0:T(8,128)(2,1)} %shard_map.112.refs_4_), channel_id=1, source_target_pairs={{6,0},{0,2},{2,4},{4,6},{27,8},{29,10},{31,12},{25,14},{22,16},{16... | collective-permute-start | bytes 1966088 | tf_op jit(solution)/shard_map/ppermute | solution.py:43
  10.0 23.0 %collective-permute-start.3 = (bf16[640,512]{1,0:T(8,128)(2,1)}, bf16[640,512]{1,0:T(8,128)(2,1)S(1)}, u32[]{:S(2)}, u32[]{:S(2)}) collective-permute-start(bf16[640,512]{1,0:T(8,128)(2,1)} %shard_map.112.refs_4_), channel_id=1, source_target_pairs={{4,0},{6,2},{0,4},{2,6},{31,8},{25,10},{27,12},{29,14},{20,16},{22... | collective-permute-start | bytes 1966088 | tf_op jit(solution)/shard_map/ppermute | solution.py:43
  10.9 3.2 %copy-start.7 = (bf16[640,512]{1,0:T(8,128)(2,1)S(1)}, bf16[640,512]{1,0:T(8,128)(2,1)}, u32[]{:S(2)}) copy-start(bf16[640,512]{1,0:T(8,128)(2,1)} %shard_map.112.refs_4_) | copy-start | bytes 1966084
  14.1 42.0 %collective-permute-start = (bf16[256,2560]{1,0:T(8,128)(2,1)}, bf16[256,2560]{1,0:T(8,128)(2,1)S(1)}, u32[]{:S(2)}, u32[]{:S(2)}) collective-permute-start(bf16[256,2560]{1,0:T(8,128)(2,1)} %shard_map.113), channel_id=1, source_target_pairs={{8,0},{10,2},{12,4},{14,6},{0,8},{2,10},{4,12},{6,14},{24,16},{26,... | collective-permute-start | bytes 3932168 | tf_op jit(solution)/shard_map/ppermute | solution.py:43
  14.1 29.5 %collective-permute-start.4 = (bf16[640,512]{1,0:T(8,128)(2,1)S(1)}, bf16[640,512]{1,0:T(8,128)(2,1)S(1)}, u32[]{:S(2)}, u32[]{:S(2)}) collective-permute-start(bf16[640,512]{1,0:T(8,128)(2,1)S(1)} %copy-done.7), channel_id=1, source_target_pairs={{29,8},{31,10},{25,12},{27,14},{13,24},{15,26},{9,28},{11,30},{28,... | collective-permute-start | bytes 1966088 | tf_op jit(solution)/shard_map/ppermute | solution.py:43
  19.1 1.7 copy-start.5
  19.1 28.4 %collective-permute-start.5 = (bf16[640,512]{1,0:T(8,128)(2,1)S(1)}, bf16[640,512]{1,0:T(8,128)(2,1)S(1)}, u32[]{:S(2)}, u32[]{:S(2)}) collective-permute-start(bf16[640,512]{1,0:T(8,128)(2,1)S(1)} %collective-permute-done.1.refs_4_.refs_0_), channel_id=1, source_target_pairs={{32,0},{34,2},{36,4},{38,6},{232,8},{234,10},{236,12},{238,14},{48... | collective-permute-start | bytes 1966088 | tf_op jit(solution)/shard_map/ppermute | solution.py:43
  24.1 50.8 %copy-start.17 = (bf16[640,512]{1,0:T(8,128)(2,1)}, bf16[640,512]{1,0:T(8,128)(2,1)S(1)}, u32[]{:S(2)}) copy-start(bf16[640,512]{1,0:T(8,128)(2,1)S(1)} %collective-permute-done.2.refs_1_) | copy-start | bytes 1966084
  24.1 21.2 %collective-permute-start.10 = (bf16[640,256]{1,0:T(8,128)(2,1)}, bf16[640,256]{1,0:T(8,128)(2,1)S(1)}, u32[]{:S(2)}, u32[]{:S(2)}) collective-permute-start(bf16[640,256]{1,0:T(8,128)(2,1)} %get-tuple-element.22), channel_id=1, source_target_pairs={{2,0},{4,2},{6,4},{0,6},{10,8},{12,10},{14,12},{8,14},{18,16},{20,... | collective-permute-start | bytes 983048 | tf_op jit(solution)/shard_map/ppermute | solution.py:43
  33.0 41.9 %copy-start.18 = (bf16[640,512]{1,0:T(8,128)(2,1)}, bf16[640,512]{1,0:T(8,128)(2,1)S(1)}, u32[]{:S(2)}) copy-start(bf16[640,512]{1,0:T(8,128)(2,1)S(1)} %collective-permute-done.3.refs_2_) | copy-start | bytes 1966084
  33.0 14.0 %collective-permute-start.11 = (bf16[640,256]{1,0:T(8,128)(2,1)}, bf16[640,256]{1,0:T(8,128)(2,1)S(1)}, u32[]{:S(2)}, u32[]{:S(2)}) collective-permute-start(bf16[640,256]{1,0:T(8,128)(2,1)} %get-tuple-element.23), channel_id=1, source_target_pairs={{1,0},{3,2},{5,4},{7,6},{9,8},{11,10},{13,12},{15,14},{17,16},{19,... | collective-permute-start | bytes 983048 | tf_op jit(solution)/shard_map/ppermute | solution.py:43
  43.7 31.2 %copy-start.19 = (bf16[640,512]{1,0:T(8,128)(2,1)}, bf16[640,512]{1,0:T(8,128)(2,1)S(1)}, u32[]{:S(2)}) copy-start(bf16[640,512]{1,0:T(8,128)(2,1)S(1)} %collective-permute-done.4.refs_3_) | copy-start | bytes 1966084
  43.7 13.9 %collective-permute-start.6 = (bf16[640,512]{1,0:T(8,128)(2,1)S(1)}, bf16[640,512]{1,0:T(8,128)(2,1)S(1)}, u32[]{:S(2)}, u32[]{:S(2)}) collective-permute-start(bf16[640,512]{1,0:T(8,128)(2,1)S(1)} %collective-permute-done.2.refs_1_), channel_id=1, source_target_pairs={{32,0},{34,2},{36,4},{38,6},{232,8},{234,10},{236,12},{238,14},{48... | collective-permute-start | bytes 1966088 | tf_op jit(solution)/shard_map/ppermute | solution.py:43
  45.3 29.6 %copy-start.8 = (bf16[640,256]{1,0:T(8,128)(2,1)}, bf16[640,256]{1,0:T(8,128)(2,1)S(1)}, u32[]{:S(2)}) copy-start(bf16[640,256]{1,0:T(8,128)(2,1)S(1)} %collective-permute-done.10.refs_9_.refs_2_) | copy-start | bytes 983044
  45.3 19.2 %collective-permute-start.7 = (bf16[640,512]{1,0:T(8,128)(2,1)S(1)}, bf16[640,512]{1,0:T(8,128)(2,1)S(1)}, u32[]{:S(2)}, u32[]{:S(2)}) collective-permute-start(bf16[640,512]{1,0:T(8,128)(2,1)S(1)} %collective-permute-done.3.refs_2_), channel_id=1, source_target_pairs={{32,0},{34,2},{36,4},{38,6},{232,8},{234,10},{236,12},{238,14},{48... | collective-permute-start | bytes 1966088 | tf_op jit(solution)/shard_map/ppermute | solution.py:43
  47.0 27.9 %copy-start.9 = (bf16[640,256]{1,0:T(8,128)(2,1)}, bf16[640,256]{1,0:T(8,128)(2,1)S(1)}, u32[]{:S(2)}) copy-start(bf16[640,256]{1,0:T(8,128)(2,1)S(1)} %collective-permute-done.11.refs_10_.refs_3_) | copy-start | bytes 983044
  47.0 7.7 %collective-permute-start.9 = (bf16[640,256]{1,0:T(8,128)(2,1)}, bf16[640,256]{1,0:T(8,128)(2,1)S(1)}, u32[]{:S(2)}, u32[]{:S(2)}) collective-permute-start(bf16[640,256]{1,0:T(8,128)(2,1)} %get-tuple-element.21), channel_id=1, source_target_pairs={{6,0},{0,2},{2,4},{4,6},{14,8},{8,10},{10,12},{12,14},{22,16},{16,... | collective-permute-start | bytes 983048 | tf_op jit(solution)/shard_map/ppermute | solution.py:43
  47.5 4.0 %copy-start.6 = (bf16[640,512]{1,0:T(8,128)(2,1)}, bf16[640,512]{1,0:T(8,128)(2,1)S(1)}, u32[]{:S(2)}) copy-start(bf16[640,512]{1,0:T(8,128)(2,1)S(1)} %collective-permute-done.5.refs_4_) | copy-start | bytes 1966084
  47.5 23.9 %collective-permute-start.8 = (bf16[640,512]{1,0:T(8,128)(2,1)S(1)}, bf16[640,512]{1,0:T(8,128)(2,1)}, u32[]{:S(2)}, u32[]{:S(2)}) collective-permute-start(bf16[640,512]{1,0:T(8,128)(2,1)S(1)} %collective-permute-done.4.refs_3_), channel_id=1, source_target_pairs={{232,8},{234,10},{236,12},{238,14},{248,24},{250,26},{252,28},{254... | collective-permute-start | bytes 1966088 | tf_op jit(solution)/shard_map/ppermute | solution.py:43
  54.7 20.2 %copy-start.10 = (bf16[640,256]{1,0:T(8,128)(2,1)}, bf16[640,256]{1,0:T(8,128)(2,1)S(1)}, u32[]{:S(2)}) copy-start(bf16[640,256]{1,0:T(8,128)(2,1)S(1)} %collective-permute-done.9.refs_8_.refs_1_) | copy-start | bytes 983044
  54.7 16.7 %collective-permute-start.12 = (bf16[640,256]{1,0:T(8,128)(2,1)}, bf16[640,256]{1,0:T(8,128)(2,1)S(1)}, u32[]{:S(2)}, u32[]{:S(2)}) collective-permute-start(bf16[640,256]{1,0:T(8,128)(2,1)} %get-tuple-element.24), channel_id=1, source_target_pairs={{4,0},{6,2},{0,4},{2,6},{12,8},{14,10},{8,12},{10,14},{20,16},{22,... | collective-permute-start | bytes 983048 | tf_op jit(solution)/shard_map/ppermute | solution.py:43
  56.1 18.8 %copy-start.15 = (bf16[256,2560]{1,0:T(8,128)(2,1)}, bf16[256,2560]{1,0:T(8,128)(2,1)S(1)}, u32[]{:S(2)}) copy-start(bf16[256,2560]{1,0:T(8,128)(2,1)S(1)} %collective-permute-done.o_ref) | copy-start | bytes 3932164
  56.2 15.2 %collective-permute-start.13 = (bf16[640,256]{1,0:T(8,128)(2,1)}, bf16[640,256]{1,0:T(8,128)(2,1)S(1)}, u32[]{:S(2)}, u32[]{:S(2)}) collective-permute-start(bf16[640,256]{1,0:T(8,128)(2,1)} %get-tuple-element.25), channel_id=1, source_target_pairs={{7,0},{1,2},{3,4},{5,6},{15,8},{9,10},{11,12},{13,14},{23,16},{17,... | collective-permute-start | bytes 983048 | tf_op jit(solution)/shard_map/ppermute | solution.py:43
  57.6 17.3 %copy-start.20 = (bf16[640,512]{1,0:T(8,128)(2,1)}, bf16[640,512]{1,0:T(8,128)(2,1)S(1)}, u32[]{:S(2)}) copy-start(bf16[640,512]{1,0:T(8,128)(2,1)S(1)} %collective-permute-done.6.refs_5_) | copy-start | bytes 1966084
  57.6 13.8 %collective-permute-start.14 = (bf16[640,256]{1,0:T(8,128)(2,1)}, bf16[640,256]{1,0:T(8,128)(2,1)S(1)}, u32[]{:S(2)}, u32[]{:S(2)}) collective-permute-start(bf16[640,256]{1,0:T(8,128)(2,1)} %get-tuple-element.26), channel_id=1, source_target_pairs={{3,0},{5,2},{7,4},{1,6},{11,8},{13,10},{15,12},{9,14},{19,16},{21,... | collective-permute-start | bytes 983048 | tf_op jit(solution)/shard_map/ppermute | solution.py:43
  64.5 10.4 %copy-start.21 = (bf16[640,512]{1,0:T(8,128)(2,1)}, bf16[640,512]{1,0:T(8,128)(2,1)S(1)}, u32[]{:S(2)}) copy-start(bf16[640,512]{1,0:T(8,128)(2,1)S(1)} %collective-permute-done.7.refs_6_) | copy-start | bytes 1966084
  64.5 36.8 %copy-start.1 = (bf16[1,256,1024]{2,1,0:T(8,128)(2,1)S(1)}, bf16[1,256,1024]{2,1,0:T(8,128)(2,1)}, u32[]{:S(2)}) copy-start(bf16[1,256,1024]{2,1,0:T(8,128)(2,1)} %param.10) | copy-start | bytes 1572868
  64.5 36.8 %copy-start.3 = (s32[20]{0:T(128)S(1)}, s32[20]{0:T(128)}, u32[]{:S(2)}) copy-start(s32[20]{0:T(128)} %stack.83.info_ref.s_ref) | copy-start | bytes 244
  64.5 36.8 %copy-start.4 = (f32[1024]{0:T(1024)S(1)}, f32[1024]{0:T(1024)}, u32[]{:S(2)}) copy-start(f32[1024]{0:T(1024)} %param.13) | copy-start | bytes 12292
  64.6 10.3 %collective-permute-start.15 = (bf16[640,256]{1,0:T(8,128)(2,1)}, bf16[640,256]{1,0:T(8,128)(2,1)S(1)}, u32[]{:S(2)}, u32[]{:S(2)}) collective-permute-start(bf16[640,256]{1,0:T(8,128)(2,1)} %get-tuple-element.27), channel_id=1, source_target_pairs={{5,0},{7,2},{1,4},{3,6},{13,8},{15,10},{9,12},{11,14},{21,16},{23,... | collective-permute-start | bytes 983048 | tf_op jit(solution)/shard_map/ppermute | solution.py:43
  71.4 3.6 %copy-start.11 = (bf16[640,256]{1,0:T(8,128)(2,1)}, bf16[640,256]{1,0:T(8,128)(2,1)S(1)}, u32[]{:S(2)}) copy-start(bf16[640,256]{1,0:T(8,128)(2,1)S(1)} %collective-permute-done.12.refs_11_.refs_4_) | copy-start | bytes 983044
  71.4 3.6 %copy-start.12 = (bf16[640,256]{1,0:T(8,128)(2,1)}, bf16[640,256]{1,0:T(8,128)(2,1)S(1)}, u32[]{:S(2)}) copy-start(bf16[640,256]{1,0:T(8,128)(2,1)S(1)} %collective-permute-done.13.refs_12_.refs_5_) | copy-start | bytes 983044
  71.4 3.6 %copy-start.13 = (bf16[640,256]{1,0:T(8,128)(2,1)}, bf16[640,256]{1,0:T(8,128)(2,1)S(1)}, u32[]{:S(2)}) copy-start(bf16[640,256]{1,0:T(8,128)(2,1)S(1)} %collective-permute-done.14.refs_13_.refs_6_) | copy-start | bytes 983044
  84.4 16.9 %collective-permute-start.16 = (f32[256,1024]{1,0:T(8,128)}, f32[256,1024]{1,0:T(8,128)S(1)}, u32[]{:S(2)}, u32[]{:S(2)}) collective-permute-start(f32[256,1024]{1,0:T(8,128)} %get-tuple-element.29), channel_id=1, source_target_pairs={{8,0},{10,2},{12,4},{14,6},{0,8},{2,10},{4,12},{6,14},{24,16},{26,... | collective-permute-start | bytes 3145736 | tf_op jit(solution)/shard_map/ppermute | solution.py:43
  101.3 1.2 copy-start.2
  103.5 28.4 %copy-start = (bf16[256,1024]{1,0:T(8,128)(2,1)}, bf16[256,1024]{1,0:T(8,128)(2,1)S(1)}, u32[]{:S(2)}) copy-start(bf16[256,1024]{1,0:T(8,128)(2,1)S(1)} %shard_map.117.k_ref.refs_8_) | copy-start | bytes 1572868
  103.5 14.7 %collective-permute-start.18 = (bf16[256,1024]{1,0:T(8,128)(2,1)S(1)}, bf16[256,1024]{1,0:T(8,128)(2,1)S(1)}, u32[]{:S(2)}, u32[]{:S(2)}) collective-permute-start(bf16[256,1024]{1,0:T(8,128)(2,1)S(1)} %shard_map.117.k_ref.refs_8_), channel_id=1, source_target_pairs={{1,0},{3,2},{5,4},{7,6},{9,8},{11,10},{13,12},{15,14},{17,16},{19,... | collective-permute-start | bytes 1572872 | tf_op jit(solution)/shard_map/ppermute | solution.py:43
  104.5 14.3 %collective-permute-start.17 = (bf16[256,1024]{1,0:T(8,128)(2,1)S(1)}, bf16[256,1024]{1,0:T(8,128)(2,1)S(1)}, u32[]{:S(2)}, u32[]{:S(2)}) collective-permute-start(bf16[256,1024]{1,0:T(8,128)(2,1)S(1)} %shard_map.117.k_ref.refs_8_), channel_id=1, source_target_pairs={{8,0},{10,2},{12,4},{14,6},{0,8},{2,10},{4,12},{6,14},{24,16},{26,... | collective-permute-start | bytes 1572872 | tf_op jit(solution)/shard_map/ppermute | solution.py:43
  105.2 15.7 %collective-permute-start.21 = (bf16[256,1024]{1,0:T(8,128)(2,1)S(1)}, bf16[256,1024]{1,0:T(8,128)(2,1)S(1)}, u32[]{:S(2)}, u32[]{:S(2)}) collective-permute-start(bf16[256,1024]{1,0:T(8,128)(2,1)S(1)} %shard_map.117.k_ref.refs_8_), channel_id=1, source_target_pairs={{4,0},{6,2},{0,4},{2,6},{12,8},{14,10},{8,12},{10,14},{20,16},{22,... | collective-permute-start | bytes 1572872 | tf_op jit(solution)/shard_map/ppermute | solution.py:43
  106.6 24.1 %collective-permute-start.19 = (bf16[256,1024]{1,0:T(8,128)(2,1)S(1)}, bf16[256,1024]{1,0:T(8,128)(2,1)S(1)}, u32[]{:S(2)}, u32[]{:S(2)}) collective-permute-start(bf16[256,1024]{1,0:T(8,128)(2,1)S(1)} %shard_map.117.k_ref.refs_8_), channel_id=1, source_target_pairs={{2,0},{4,2},{6,4},{0,6},{10,8},{12,10},{14,12},{8,14},{18,16},{20,... | collective-permute-start | bytes 1572872 | tf_op jit(solution)/shard_map/ppermute | solution.py:43
  108.3 23.6 %collective-permute-start.20 = (bf16[256,1024]{1,0:T(8,128)(2,1)S(1)}, bf16[256,1024]{1,0:T(8,128)(2,1)S(1)}, u32[]{:S(2)}, u32[]{:S(2)}) collective-permute-start(bf16[256,1024]{1,0:T(8,128)(2,1)S(1)} %shard_map.117.k_ref.refs_8_), channel_id=1, source_target_pairs={{6,0},{0,2},{2,4},{4,6},{14,8},{8,10},{10,12},{12,14},{22,16},{16,... | collective-permute-start | bytes 1572872 | tf_op jit(solution)/shard_map/ppermute | solution.py:43
  108.3 33.2 %copy-start.33 = (s32[640]{0:T(1024)S(1)}, s32[640]{0:T(1024)}, u32[]{:S(2)}) copy-start(s32[640]{0:T(1024)} %param.14) | copy-start | bytes 7684
  118.3 13.6 %copy-start.22 = (bf16[256,1024]{1,0:T(8,128)(2,1)}, bf16[256,1024]{1,0:T(8,128)(2,1)S(1)}, u32[]{:S(2)}) copy-start(bf16[256,1024]{1,0:T(8,128)(2,1)S(1)} %collective-permute-done.18.refs_8_.refs_11_) | copy-start | bytes 1572868
  118.3 24.9 %collective-permute-start.23 = (bf16[256,1024]{1,0:T(8,128)(2,1)S(1)}, bf16[256,1024]{1,0:T(8,128)(2,1)}, u32[]{:S(2)}, u32[]{:S(2)}) collective-permute-start(bf16[256,1024]{1,0:T(8,128)(2,1)S(1)} %collective-permute-done.18.refs_8_.refs_11_), channel_id=1, source_target_pairs={{6,0},{0,2},{2,4},{4,6},{14,8},{8,10},{10,12},{12,14},{22,16},{16,... | collective-permute-start | bytes 1572872 | tf_op jit(solution)/shard_map/ppermute | solution.py:43
  118.8 13.1 %copy-start.34 = (bf16[256,1024]{1,0:T(8,128)(2,1)}, bf16[256,1024]{1,0:T(8,128)(2,1)S(1)}, u32[]{:S(2)}) copy-start(bf16[256,1024]{1,0:T(8,128)(2,1)S(1)} %collective-permute-done.17.o_ref) | copy-start | bytes 1572868
  118.8 24.3 %collective-permute-start.24 = (bf16[256,1024]{1,0:T(8,128)(2,1)S(1)}, bf16[256,1024]{1,0:T(8,128)(2,1)}, u32[]{:S(2)}, u32[]{:S(2)}) collective-permute-start(bf16[256,1024]{1,0:T(8,128)(2,1)S(1)} %collective-permute-done.18.refs_8_.refs_11_), channel_id=1, source_target_pairs={{2,0},{4,2},{6,4},{0,6},{10,8},{12,10},{14,12},{8,14},{18,16},{20,... | collective-permute-start | bytes 1572872 | tf_op jit(solution)/shard_map/ppermute | solution.py:43
  120.9 11.0 %copy-start.23 = (bf16[256,1024]{1,0:T(8,128)(2,1)}, bf16[256,1024]{1,0:T(8,128)(2,1)S(1)}, u32[]{:S(2)}) copy-start(bf16[256,1024]{1,0:T(8,128)(2,1)S(1)} %collective-permute-done.21.refs_11_.refs_12_) | copy-start | bytes 1572868
  120.9 22.2 %collective-permute-start.25 = (bf16[256,1024]{1,0:T(8,128)(2,1)S(1)}, bf16[256,1024]{1,0:T(8,128)(2,1)}, u32[]{:S(2)}, u32[]{:S(2)}) collective-permute-start(bf16[256,1024]{1,0:T(8,128)(2,1)S(1)} %collective-permute-done.21.refs_11_.refs_12_), channel_id=1, source_target_pairs={{1,0},{3,2},{5,4},{7,6},{9,8},{11,10},{13,12},{15,14},{17,16},{19,... | collective-permute-start | bytes 1572872 | tf_op jit(solution)/shard_map/ppermute | solution.py:43
  130.7 1.2 copy-start.24
  131.9 0.9 copy-start.25
  140.7 51.6 %collective-permute-start.22 = (bf16[256,2560]{1,0:T(8,128)(2,1)}, bf16[256,2560]{1,0:T(8,128)(2,1)S(1)}, u32[]{:S(2)}, u32[]{:S(2)}) collective-permute-start(bf16[256,2560]{1,0:T(8,128)(2,1)} %get-tuple-element.31), channel_id=1, source_target_pairs={{8,0},{10,2},{12,4},{14,6},{0,8},{2,10},{4,12},{6,14},{24,16},{26,... | collective-permute-start | bytes 3932168 | tf_op jit(solution)/shard_map/ppermute | solution.py:43
  155.8 8.7 %collective-permute-start.26 = (bf16[320,128]{1,0:T(8,128)(2,1)}, bf16[320,128]{1,0:T(8,128)(2,1)S(1)}, u32[]{:S(2)}, u32[]{:S(2)}) collective-permute-start(bf16[320,128]{1,0:T(8,128)(2,1)} %get-tuple-element.36), channel_id=1, source_target_pairs={{8,0},{10,2},{12,4},{14,6},{0,8},{2,10},{4,12},{6,14},{24,16},{26,... | collective-permute-start | bytes 245768 | tf_op jit(solution)/shard_map/ppermute | solution.py:43
  156.3 8.2 %collective-permute-start.27 = (bf16[320,128]{1,0:T(8,128)(2,1)}, bf16[320,128]{1,0:T(8,128)(2,1)S(1)}, u32[]{:S(2)}, u32[]{:S(2)}) collective-permute-start(bf16[320,128]{1,0:T(8,128)(2,1)} %get-tuple-element.37), channel_id=1, source_target_pairs={{16,0},{18,2},{20,4},{22,6},{24,8},{26,10},{28,12},{30,14},{0,16},... | collective-permute-start | bytes 245768 | tf_op jit(solution)/shard_map/ppermute | solution.py:43
  158.7 5.8 %collective-permute-start.28 = (bf16[320,128]{1,0:T(8,128)(2,1)}, bf16[320,128]{1,0:T(8,128)(2,1)S(1)}, u32[]{:S(2)}, u32[]{:S(2)}) collective-permute-start(bf16[320,128]{1,0:T(8,128)(2,1)} %get-tuple-element.38), channel_id=1, source_target_pairs={{24,0},{26,2},{28,4},{30,6},{16,8},{18,10},{20,12},{22,14},{8,16},... | collective-permute-start | bytes 245768 | tf_op jit(solution)/shard_map/ppermute | solution.py:43
  166.9 8.3 %collective-permute-start.29 = (bf16[320,128]{1,0:T(8,128)(2,1)}, bf16[320,128]{1,0:T(8,128)(2,1)S(1)}, u32[]{:S(2)}, u32[]{:S(2)}) collective-permute-start(bf16[320,128]{1,0:T(8,128)(2,1)} %shard_map.122), channel_id=1, source_target_pairs={{32,0},{34,2},{36,4},{38,6},{40,8},{42,10},{44,12},{46,14},{48,16}... | collective-permute-start | bytes 245768 | tf_op jit(solution)/shard_map/ppermute | solution.py:43
  176.1 5.7 %collective-permute-start.30 = (bf16[320,128]{1,0:T(8,128)(2,1)S(1)}, bf16[320,128]{1,0:T(8,128)(2,1)S(1)}, u32[]{:S(2)}, u32[]{:S(2)}) collective-permute-start(bf16[320,128]{1,0:T(8,128)(2,1)S(1)} %add_convert_fusion.1), channel_id=1, source_target_pairs={{64,0},{66,2},{68,4},{70,6},{72,8},{74,10},{76,12},{78,14},{80,16}... | collective-permute-start | bytes 245768 | tf_op jit(solution)/shard_map/ppermute | solution.py:43
  176.2 7.6 %collective-permute-start.31 = (bf16[320,128]{1,0:T(8,128)(2,1)S(1)}, bf16[320,128]{1,0:T(8,128)(2,1)S(1)}, u32[]{:S(2)}, u32[]{:S(2)}) collective-permute-start(bf16[320,128]{1,0:T(8,128)(2,1)S(1)} %add_convert_fusion.1), channel_id=1, source_target_pairs={{128,0},{130,2},{132,4},{134,6},{136,8},{138,10},{140,12},{142,14}... | collective-permute-start | bytes 245768 | tf_op jit(solution)/shard_map/ppermute | solution.py:43
  179.9 9.9 %collective-permute-start.32 = (bf16[320,128]{1,0:T(8,128)(2,1)S(1)}, bf16[320,128]{1,0:T(8,128)(2,1)S(1)}, u32[]{:S(2)}, u32[]{:S(2)}) collective-permute-start(bf16[320,128]{1,0:T(8,128)(2,1)S(1)} %add_convert_fusion.1), channel_id=1, source_target_pairs={{192,0},{194,2},{196,4},{198,6},{200,8},{202,10},{204,12},{206,14}... | collective-permute-start | bytes 245768 | tf_op jit(solution)/shard_map/ppermute | solution.py:43
  189.9 6.9 %copy-start.26 = (bf16[320,128]{1,0:T(8,128)(2,1)}, bf16[320,128]{1,0:T(8,128)(2,1)S(1)}, u32[]{:S(2)}) copy-start(bf16[320,128]{1,0:T(8,128)(2,1)S(1)} %add_convert_fusion.a) | copy-start | bytes 245764
  189.9 6.9 %collective-permute-start.33 = (bf16[320,128]{1,0:T(8,128)(2,1)S(1)}, bf16[320,128]{1,0:T(8,128)(2,1)S(1)}, u32[]{:S(2)}, u32[]{:S(2)}) collective-permute-start(bf16[320,128]{1,0:T(8,128)(2,1)S(1)} %add_convert_fusion.a), channel_id=1, source_target_pairs={{8,0},{10,2},{12,4},{14,6},{0,8},{2,10},{4,12},{6,14},{24,16},{26,... | collective-permute-start | bytes 245768 | tf_op jit(solution)/shard_map/ppermute | solution.py:43
  190.5 6.3 %collective-permute-start.34 = (bf16[320,128]{1,0:T(8,128)(2,1)S(1)}, bf16[320,128]{1,0:T(8,128)(2,1)S(1)}, u32[]{:S(2)}, u32[]{:S(2)}) collective-permute-start(bf16[320,128]{1,0:T(8,128)(2,1)S(1)} %add_convert_fusion.a), channel_id=1, source_target_pairs={{16,0},{18,2},{20,4},{22,6},{24,8},{26,10},{28,12},{30,14},{0,16},... | collective-permute-start | bytes 245768 | tf_op jit(solution)/shard_map/ppermute | solution.py:43
  191.0 5.8 %collective-permute-start.35 = (bf16[320,128]{1,0:T(8,128)(2,1)S(1)}, bf16[320,128]{1,0:T(8,128)(2,1)S(1)}, u32[]{:S(2)}, u32[]{:S(2)}) collective-permute-start(bf16[320,128]{1,0:T(8,128)(2,1)S(1)} %add_convert_fusion.a), channel_id=1, source_target_pairs={{24,0},{26,2},{28,4},{30,6},{16,8},{18,10},{20,12},{22,14},{8,16},... | collective-permute-start | bytes 245768 | tf_op jit(solution)/shard_map/ppermute | solution.py:43
  192.3 1.1 copy-start.16
  (7 other events, 4.6 us)

commit v4 on v3

--- a/solution.py
+++ b/solution.py
@@ -74,12 +74,12 @@
 
 def mm_left(table, value):
     high, low = split(value)
-    return mm(table[0], high) + mm(table[0], low) + mm(table[1], high)
+    return mm(jnp.concatenate([table[0], table[0], table[1]], axis=1), jnp.concatenate([high, low, high], axis=0))
 
 
 def mm_right(value, table):
     high, low = split(value)
-    return mm(high, table[0]) + mm(low, table[0]) + mm(high, table[1])
+    return mm(jnp.concatenate([high, low, high], axis=1), jnp.concatenate([table[0], table[0], table[1]], axis=0))
 
 
 def params(limit=56):
@@ -150,13 +150,13 @@
                     sums[n][h] = term if k == 0 else sums[n][h] + term
         for n in range(2):
             for h in range(2):
-                outs[n][:, HALF * h : HALF * h + HALF] = sums[n][h]
+                outs[n][:, HALF * h : HALF * h + HALF] = sums[n][h].astype(outs[n].dtype)
 
     return pl.pallas_call(
         kernel,
         in_specs=[SMEM, ANY, ANY, VMEM] + [ANY] * (8 + len(after)),
         out_specs=[VMEM] * 2,
-        out_shape=[jax.ShapeDtypeStruct((TOK, KV), f32)] * 2,
+        out_shape=[jax.ShapeDtypeStruct((TOK, KV), t) for t in (f32, bf16)],
         scratch_shapes=[
             pltpu.VMEM((4, TOK, ROWS), bf16),
             pltpu.VMEM((TOK, 4 * ROWS), bf16),
@@ -172,7 +172,7 @@
     def kernel(s_ref, m_ref, r_ref, ca_ref, cb_ref, ga_ref, gb_ref, *refs):
         out_ref = refs[-1]
         p = s_ref[PARITY]
-        both = m_ref[...] + r_ref[...]
+        both = m_ref[...] + r_ref[...].astype(f32)
         a, b = both[:, :HALF], both[:, HALF:]
         sa = ca_ref[...].astype(f32) * ga_ref[...]
         sb = cb_ref[...].astype(f32) * gb_ref[...]

time: 203 us -> 202 us (level)
  transfers between devices with their start and end apart: 36 -> 36, of which waited for: 13 -> 12; matrix products, arithmetic and copies ran while one was open for 1% -> 1% of each run, Pallas kernels for 20% -> 20%
where the time goes in v4:
time: 202 us; the launch traced here: 201 us
  starting transfers between devices  72.9 us (36%)
  waiting for transfers between devices  61.1 us (30%)
  Pallas kernels  56.7 us (28%)
  local copies, waits for them, and re-layouts  7.77 us (4%)
    ppermute x36, starting transfers between devices, pull(): return lax.ppermute(value, ('rep', 'shard'), pairs)  72.9 us
    ppermute x36, waiting for transfers between devices, pull(): return lax.ppermute(value, ('rep', 'shard'), pairs)  61.1 us
    pallas_call x1, Pallas kernels, blend(): pl.pallas_call(kernel, grid_spec=pltpu.PrefetchScalarGridSpec(num_scalar_...  12.2 us
    pallas_call x4, Pallas kernels, cut_columns(): pl.pallas_call(kernel, grid_spec=pltpu.PrefetchScalarGridSpec(num_scalar_...  12.2 us
    pallas_call x1, Pallas kernels, project(): pl.pallas_call(kernel, in_specs=[SMEM, ANY, ANY, VMEM] + [ANY] * (8 + len...  8.52 us
    pallas_call x1, Pallas kernels, token_gradient(): pl.pallas_call(kernel, in_specs=[SMEM] + [VMEM] * 11 + [ANY] * len(after)...  7.9 us
    unnamed x70, local copies, waits for them, and re-layouts  5.88 us
    pallas_call x1, Pallas kernels, remove_corner(): pl.pallas_call(kernel, grid=(4,), in_specs=[pl.BlockSpec((ROWS, 256), lam...  5.46 us
  transfers between devices with their start and end apart: 36, of which 12 were waited for; matrix products, arithmetic and copies ran while one was open for 1% of the time, Pallas kernels for 20%

profile of v4, /device:TPU:1, one launch (start us, length us, event | category | flops | bytes accessed | tf_op | source)
XLA Modules:
  0.0 201.2 jit_solution(13023857127409702377)
XLA Ops:
  0.8 0.7 stack.83.info_ref.s_ref
  1.5 2.6 %shard_map.112.refs_4_ = bf16[640,512]{1,0:T(8,128)(2,1)} custom-call(s32[20]{0:T(128)} %stack.83.info_ref.s_ref, bf16[640,1024]{1,0:T(8,128)(2,1)} %own_ref.3), custom_call_target="tpu_custom_call" | custom-call | bytes 1310720 | tf_op jit(solution)/shard_map/pallas_call | solution.py:103
  4.1 3.3 %collective-permute-start.1 = (bf16[640,512]{1,0:T(8,128)(2,1)}, bf16[640,512]{1,0:T(8,128)(2,1)S(1)}, u32[]{:S(2)}, u32[]{:S(2)}) collective-permute-start(bf16[640,512]{1,0:T(8,128)(2,1)} %shard_map.112.refs_4_), channel_id=1, source_target_pairs={{2,0},{4,2},{6,4},{0,6},{25,8},{27,10},{29,12},{31,14},{18,16},{20... | collective-permute-start | bytes 1966088 | tf_op jit(solution)/shard_map/ppermute | solution.py:43
  7.4 2.6 %collective-permute-start.2 = (bf16[640,512]{1,0:T(8,128)(2,1)}, bf16[640,512]{1,0:T(8,128)(2,1)S(1)}, u32[]{:S(2)}, u32[]{:S(2)}) collective-permute-start(bf16[640,512]{1,0:T(8,128)(2,1)} %shard_map.112.refs_4_), channel_id=1, source_target_pairs={{6,0},{0,2},{2,4},{4,6},{27,8},{29,10},{31,12},{25,14},{22,16},{16... | collective-permute-start | bytes 1966088 | tf_op jit(solution)/shard_map/ppermute | solution.py:43
  10.0 0.9 collective-permute-start.3
  11.0 3.2 %shard_map.113 = bf16[256,2560]{1,0:T(8,128)(2,1)} custom-call(s32[20]{0:T(128)} %stack.83.info_ref.s_ref, bf16[256,5120]{1,0:T(8,128)(2,1)} %bitcast.30, bf16[256,5120]{1,0:T(8,128)(2,1)} %bitcast.31, bf16[256,5120]{1,0:T(8,128)(2,1)} %bitcast.32, bf16[256,5120]{1,0:T(8,128)(2,1)} %bitcast.33, bf16[640,512]{1,0:T(8,128)(2,1)} %shard_map.112.refs_4_), custom_call_target="tpu_custom_call" | custom-call | bytes 2621440 | tf_op jit(solution)/shard_map/pallas_call | solution.py:103
  14.2 5.0 %collective-permute-start.4 = (bf16[640,512]{1,0:T(8,128)(2,1)S(1)}, bf16[640,512]{1,0:T(8,128)(2,1)S(1)}, u32[]{:S(2)}, u32[]{:S(2)}) collective-permute-start(bf16[640,512]{1,0:T(8,128)(2,1)S(1)} %copy-done.7), channel_id=1, source_target_pairs={{29,8},{31,10},{25,12},{27,14},{13,24},{15,26},{9,28},{11,30},{28,... | collective-permute-start | bytes 1966088 | tf_op jit(solution)/shard_map/ppermute | solution.py:43
  19.2 1.7 collective-permute-start.5
  20.9 3.2 %shard_map.114 = (bf16[640,256]{1,0:T(8,128)(2,1)}, bf16[640,256]{1,0:T(8,128)(2,1)}, bf16[640,256]{1,0:T(8,128)(2,1)}, bf16[640,256]{1,0:T(8,128)(2,1)}) custom-call(s32[20]{0:T(128)} %stack.83.info_ref.s_ref, bf16[256,5120]{1,0:T(8,128)(2,1)} %bitcast.34, bf16[256,5120]{1,0:T(8,128)(2,1)} %bitcast.35, bf16[256,5120]{1,0:T(8,128)(2,1)} %bitcast.36, ...), custom_call_target="tpu_custom_call" | custom-call | bytes 2621440 | tf_op jit(solution)/shard_map/pallas_call | solution.py:103
  24.1 3.0 %collective-permute-start.10 = (bf16[640,256]{1,0:T(8,128)(2,1)}, bf16[640,256]{1,0:T(8,128)(2,1)S(1)}, u32[]{:S(2)}, u32[]{:S(2)}) collective-permute-start(bf16[640,256]{1,0:T(8,128)(2,1)} %get-tuple-element.22), channel_id=1, source_target_pairs={{2,0},{4,2},{6,4},{0,6},{10,8},{12,10},{14,12},{8,14},{18,16},{20,... | collective-permute-start | bytes 983048 | tf_op jit(solution)/shard_map/ppermute | solution.py:43
  27.1 5.9 %collective-permute-done.3.refs_2_ = bf16[640,512]{1,0:T(8,128)(2,1)S(1)} collective-permute-done((bf16[640,512]{1,0:T(8,128)(2,1)}, bf16[640,512]{1,0:T(8,128)(2,1)S(1)}, u32[]{:S(2)}, u32[]{:S(2)}) %collective-permute-start.3) | collective-permute-done | bytes 655392 | tf_op jit(solution)/shard_map/ppermute | solution.py:43
  33.0 1.4 collective-permute-start.11
  34.4 9.3 %collective-permute-done.4.refs_3_ = bf16[640,512]{1,0:T(8,128)(2,1)S(1)} collective-permute-done((bf16[640,512]{1,0:T(8,128)(2,1)S(1)}, bf16[640,512]{1,0:T(8,128)(2,1)S(1)}, u32[]{:S(2)}, u32[]{:S(2)}) %collective-permute-start.4) | collective-permute-done | bytes 655392 | tf_op jit(solution)/shard_map/ppermute | solution.py:43
  43.7 1.6 collective-permute-start.6
  45.4 1.6 collective-permute-start.7
  47.0 0.6 collective-permute-start.9
  47.6 4.0 %collective-permute-start.8 = (bf16[640,512]{1,0:T(8,128)(2,1)S(1)}, bf16[640,512]{1,0:T(8,128)(2,1)}, u32[]{:S(2)}, u32[]{:S(2)}) collective-permute-start(bf16[640,512]{1,0:T(8,128)(2,1)S(1)} %collective-permute-done.4.refs_3_), channel_id=1, source_target_pairs={{232,8},{234,10},{236,12},{238,14},{248,24},{250,26},{252,28},{254... | collective-permute-start | bytes 1966088 | tf_op jit(solution)/shard_map/ppermute | solution.py:43
  51.6 3.1 %shard_map.115 = (bf16[640,256]{1,0:T(8,128)(2,1)}, bf16[640,256]{1,0:T(8,128)(2,1)}, bf16[640,256]{1,0:T(8,128)(2,1)}, bf16[640,256]{1,0:T(8,128)(2,1)}) custom-call(s32[20]{0:T(128)} %stack.83.info_ref.s_ref, bf16[256,5120]{1,0:T(8,128)(2,1)} %bitcast.38, bf16[256,5120]{1,0:T(8,128)(2,1)} %bitcast.39, bf16[256,5120]{1,0:T(8,128)(2,1)} %bitcast.40, ...), custom_call_target="tpu_custom_call" | custom-call | bytes 2621440 | tf_op jit(solution)/shard_map/pallas_call | solution.py:103
  54.7 1.5 collective-permute-start.12
  56.2 1.5 collective-permute-start.13
  57.6 3.6 %collective-permute-start.14 = (bf16[640,256]{1,0:T(8,128)(2,1)}, bf16[640,256]{1,0:T(8,128)(2,1)S(1)}, u32[]{:S(2)}, u32[]{:S(2)}) collective-permute-start(bf16[640,256]{1,0:T(8,128)(2,1)} %get-tuple-element.26), channel_id=1, source_target_pairs={{3,0},{5,2},{7,4},{1,6},{11,8},{13,10},{15,12},{9,14},{19,16},{21,... | collective-permute-start | bytes 983048 | tf_op jit(solution)/shard_map/ppermute | solution.py:43
  61.3 3.3 %collective-permute-done.7.refs_6_ = bf16[640,512]{1,0:T(8,128)(2,1)S(1)} collective-permute-done((bf16[640,512]{1,0:T(8,128)(2,1)S(1)}, bf16[640,512]{1,0:T(8,128)(2,1)S(1)}, u32[]{:S(2)}, u32[]{:S(2)}) %collective-permute-start.7) | collective-permute-done | bytes 655392 | tf_op jit(solution)/shard_map/ppermute | solution.py:43
  64.9 6.5 %collective-permute-done.8.refs_7_ = bf16[640,512]{1,0:T(8,128)(2,1)} collective-permute-done((bf16[640,512]{1,0:T(8,128)(2,1)S(1)}, bf16[640,512]{1,0:T(8,128)(2,1)}, u32[]{:S(2)}, u32[]{:S(2)}) %collective-permute-start.8) | collective-permute-done | bytes 655392 | tf_op jit(solution)/shard_map/ppermute | solution.py:43
  71.5 3.4 %collective-permute-done.15.refs_14_.refs_7_ = bf16[640,256]{1,0:T(8,128)(2,1)S(1)} collective-permute-done((bf16[640,256]{1,0:T(8,128)(2,1)}, bf16[640,256]{1,0:T(8,128)(2,1)S(1)}, u32[]{:S(2)}, u32[]{:S(2)}) %collective-permute-start.15) | collective-permute-done | bytes 327712 | tf_op jit(solution)/shard_map/ppermute | solution.py:43
  75.0 0.7 copy-done.14
  75.8 8.5 %shard_map.116 = (f32[256,1024]{1,0:T(8,128)}, bf16[256,1024]{1,0:T(8,128)(2,1)}) custom-call(s32[20]{0:T(128)} %stack.83.info_ref.s_ref, bf16[256,5120]{1,0:T(8,128)(2,1)} %bitcast.42, bf16[256,2560]{1,0:T(8,128)(2,1)} %copy-done.15, bf16[640,1024]{1,0:T(8,128)(2,1)} %own_ref.3, bf16[640,512]{1,0:T(8,128)(2,1)} %copy-done.5, bf16[640,512]{1,0:T(8,128)(2,1)} %copy-done.17, ...), custom_call_target="tpu_custom_call" | custom-call | flops 2684354560 | bytes 13107200 | tf_op jit(solution)/shard_map/pallas_call | solution.py:155
  84.3 14.4 %collective-permute-start.16 = (bf16[256,1024]{1,0:T(8,128)(2,1)}, bf16[256,1024]{1,0:T(8,128)(2,1)S(1)}, u32[]{:S(2)}, u32[]{:S(2)}) collective-permute-start(bf16[256,1024]{1,0:T(8,128)(2,1)} %get-tuple-element.29), channel_id=1, source_target_pairs={{8,0},{10,2},{12,4},{14,6},{0,8},{2,10},{4,12},{6,14},{24,16},{26,... | collective-permute-start | bytes 1572872 | tf_op jit(solution)/shard_map/ppermute | solution.py:43
  98.7 1.7 collective-permute-done.16.r_ref
  100.4 1.2 copy-done.2
  101.6 1.0 shard_map.117.k_ref.refs_8_
  102.7 1.0 collective-permute-start.18
  103.7 0.7 collective-permute-start.17
  104.4 1.4 collective-permute-start.21
  105.8 1.7 collective-permute-start.19
  107.4 9.9 %collective-permute-done.18.refs_8_.refs_11_ = bf16[256,1024]{1,0:T(8,128)(2,1)S(1)} collective-permute-done((bf16[256,1024]{1,0:T(8,128)(2,1)S(1)}, bf16[256,1024]{1,0:T(8,128)(2,1)S(1)}, u32[]{:S(2)}, u32[]{:S(2)}) %collective-permute-start.18) | collective-permute-done | bytes 524320 | tf_op jit(solution)/shard_map/ppermute | solution.py:43
  117.4 0.6 collective-permute-start.23
  118.0 2.1 %collective-permute-start.24 = (bf16[256,1024]{1,0:T(8,128)(2,1)S(1)}, bf16[256,1024]{1,0:T(8,128)(2,1)}, u32[]{:S(2)}, u32[]{:S(2)}) collective-permute-start(bf16[256,1024]{1,0:T(8,128)(2,1)S(1)} %collective-permute-done.18.refs_8_.refs_11_), channel_id=1, source_target_pairs={{2,0},{4,2},{6,4},{0,6},{10,8},{12,10},{14,12},{8,14},{18,16},{20,... | collective-permute-start | bytes 1572872 | tf_op jit(solution)/shard_map/ppermute | solution.py:43
  120.1 1.4 collective-permute-start.25
  121.5 8.4 %collective-permute-done.19.refs_9_.refs_10_ = bf16[256,1024]{1,0:T(8,128)(2,1)S(1)} collective-permute-done((bf16[256,1024]{1,0:T(8,128)(2,1)S(1)}, bf16[256,1024]{1,0:T(8,128)(2,1)S(1)}, u32[]{:S(2)}, u32[]{:S(2)}) %collective-permute-start.19) | collective-permute-done | bytes 524320 | tf_op jit(solution)/shard_map/ppermute | solution.py:43
  129.8 1.2 collective-permute-done.20.refs_10_.refs_9_
  131.1 0.8 copy-done.25
  131.9 7.9 %shard_map.118 = (bf16[256,2560]{1,0:T(8,128)(2,1)}, bf16[256,2560]{1,0:T(8,128)(2,1)}) custom-call(s32[20]{0:T(128)} %stack.83.info_ref.s_ref, bf16[256,1024]{1,0:T(8,128)(2,1)} %copy-done, bf16[256,1024]{1,0:T(8,128)(2,1)} %copy-done.34, bf16[640,1024]{1,0:T(8,128)(2,1)} %own_ref.3, bf16[640,512]{1,0:T(8,128)(2,1)} %copy-done.5, ...), custom_call_target="tpu_custom_call" | custom-call | flops 2684354560 | bytes 13107200 | tf_op jit(solution)/shard_map/pallas_call | solution.py:222
  139.8 0.7 collective-permute-start.22
  141.3 1.0 tile.9.refs_17_
  142.3 12.2 %shard_map.120 = (f32[640,1024]{1,0:T(8,128)}, f32[4,320,128]{2,1,0:T(8,128)}, f32[320,128]{1,0:T(8,128)}, bf16[320,128]{1,0:T(8,128)(2,1)}, bf16[320,128]{1,0:T(8,128)(2,1)}, /*index=5*/bf16[320,128]{1,0:T(8,128)(2,1)}) custom-call(s32[20]{0:T(128)} %stack.83.info_ref.s_ref, bf16[640,256]{1,0:T(8,128)(2,1)} %get-tuple-element.32.refs_0_, ...), custom_call_target="tpu_custom_call" | custom-call | flops 2684354560 | bytes 12058624 | tf_op jit(solution)/shard_map/pallas_call | solution.py:299
  154.5 0.5 collective-permute-start.26
  155.0 2.4 %collective-permute-start.27 = (bf16[320,128]{1,0:T(8,128)(2,1)}, bf16[320,128]{1,0:T(8,128)(2,1)S(1)}, u32[]{:S(2)}, u32[]{:S(2)}) collective-permute-start(bf16[320,128]{1,0:T(8,128)(2,1)} %get-tuple-element.37), channel_id=1, source_target_pairs={{16,0},{18,2},{20,4},{22,6},{24,8},{26,10},{28,12},{30,14},{0,16},... | collective-permute-start | bytes 245768 | tf_op jit(solution)/shard_map/ppermute | solution.py:43
  157.8 5.5 %shard_map.121._ = f32[640,1024]{1,0:T(8,128)} custom-call(f32[640,1024]{1,0:T(8,128)} %get-tuple-element.33.blended_ref, f32[4,320,128]{2,1,0:T(8,128)} %get-tuple-element.34.corner_ref, bf16[2,64,128]{2,1,0:T(8,128)(2,1)} %constant.128.clone.refs_18_.left_ref, bf16[2,256,128]{2,1,0:T(8,128)(2,1)} %constant.129.clone.refs_19_.right_ref), custom_call_target="tpu_custom_call" | custom-call | flops 335544320 | bytes 5242880 | tf_op jit(solution)/shard_map/pallas_call | solution.py:320
  163.3 0.6 copy-done.27
  163.9 1.7 shard_map.122
  165.6 5.1 %collective-permute-start.29 = (bf16[320,128]{1,0:T(8,128)(2,1)}, bf16[320,128]{1,0:T(8,128)(2,1)S(1)}, u32[]{:S(2)}, u32[]{:S(2)}) collective-permute-start(bf16[320,128]{1,0:T(8,128)(2,1)} %shard_map.122), channel_id=1, source_target_pairs={{32,0},{34,2},{36,4},{38,6},{40,8},{42,10},{44,12},{46,14},{48,16}... | collective-permute-start | bytes 245768 | tf_op jit(solution)/shard_map/ppermute | solution.py:43
  170.7 3.1 %collective-permute-done.29 = bf16[320,128]{1,0:T(8,128)(2,1)S(1)} collective-permute-done((bf16[320,128]{1,0:T(8,128)(2,1)}, bf16[320,128]{1,0:T(8,128)(2,1)S(1)}, u32[]{:S(2)}, u32[]{:S(2)}) %collective-permute-start.29) | collective-permute-done | bytes 81952 | tf_op jit(solution)/shard_map/ppermute | solution.py:43
  173.9 0.9 add_convert_fusion.1
  174.9 3.8 %collective-permute-start.31 = (bf16[320,128]{1,0:T(8,128)(2,1)S(1)}, bf16[320,128]{1,0:T(8,128)(2,1)S(1)}, u32[]{:S(2)}, u32[]{:S(2)}) collective-permute-start(bf16[320,128]{1,0:T(8,128)(2,1)S(1)} %add_convert_fusion.1), channel_id=1, source_target_pairs={{128,0},{130,2},{132,4},{134,6},{136,8},{138,10},{140,12},{142,14}... | collective-permute-start | bytes 245768 | tf_op jit(solution)/shard_map/ppermute | solution.py:43
  178.7 1.8 collective-permute-start.32
  180.5 2.1 %collective-permute-done.31 = bf16[320,128]{1,0:T(8,128)(2,1)S(1)} collective-permute-done((bf16[320,128]{1,0:T(8,128)(2,1)S(1)}, bf16[320,128]{1,0:T(8,128)(2,1)S(1)}, u32[]{:S(2)}, u32[]{:S(2)}) %collective-permute-start.31) | collective-permute-done | bytes 81952 | tf_op jit(solution)/shard_map/ppermute | solution.py:43
  182.6 5.9 %collective-permute-done.32 = bf16[320,128]{1,0:T(8,128)(2,1)S(1)} collective-permute-done((bf16[320,128]{1,0:T(8,128)(2,1)S(1)}, bf16[320,128]{1,0:T(8,128)(2,1)S(1)}, u32[]{:S(2)}, u32[]{:S(2)}) %collective-permute-start.32) | collective-permute-done | bytes 81952 | tf_op jit(solution)/shard_map/ppermute | solution.py:43
  188.6 0.6 collective-permute-start.33
  189.8 1.2 collective-permute-start.35
  191.0 1.1 copy-done.16
  192.1 3.4 %shard_map.119._ = bf16[256,5120]{1,0:T(8,128)(2,1)} custom-call(s32[20]{0:T(128)} %stack.83.info_ref.s_ref, bf16[256,2560]{1,0:T(8,128)(2,1)} %get-tuple-element.30.m_ref.refs_20_, bf16[256,2560]{1,0:T(8,128)(2,1)} %copy-done.16), custom_call_target="tpu_custom_call" | custom-call | bytes 5242880 | tf_op jit(solution)/shard_map/pallas_call | solution.py:239
  195.6 0.6 copy-done.30
  196.2 0.6 copy-done.32
  196.8 4.4 %shard_map.123 = bf16[640,1024]{1,0:T(8,128)(2,1)} custom-call(s32[20]{0:T(128)} %stack.83.info_ref.s_ref, bf16[320,128]{1,0:T(8,128)(2,1)} %copy-done.26, bf16[320,128]{1,0:T(8,128)(2,1)} %copy-done.30, bf16[320,128]{1,0:T(8,128)(2,1)} %copy-done.31, bf16[320,128]{1,0:T(8,128)(2,1)} %copy-done.32, bf16[2,64,128]{2,1,0:T(8,128)(2,1)} %constant.128.clone.refs_18_.left_ref, ...), custom_call_target="tpu_custom_call" | custom-call | tf_op jit(solution)/shard_map/pallas_call | solution.py:361
  (101 shorter events, 2.3 us)
Async XLA Ops:
  4.1 15.1 %collective-permute-start.1 = (bf16[640,512]{1,0:T(8,128)(2,1)}, bf16[640,512]{1,0:T(8,128)(2,1)S(1)}, u32[]{:S(2)}, u32[]{:S(2)}) collective-permute-start(bf16[640,512]{1,0:T(8,128)(2,1)} %shard_map.112.refs_4_), channel_id=1, source_target_pairs={{2,0},{4,2},{6,4},{0,6},{25,8},{27,10},{29,12},{31,14},{18,16},{20... | collective-permute-start | bytes 1966088 | tf_op jit(solution)/shard_map/ppermute | solution.py:43
  7.4 16.7 %collective-permute-start.2 = (bf16[640,512]{1,0:T(8,128)(2,1)}, bf16[640,512]{1,0:T(8,128)(2,1)S(1)}, u32[]{:S(2)}, u32[]{:S(2)}) collective-permute-start(bf16[640,512]{1,0:T(8,128)(2,1)} %shard_map.112.refs_4_), channel_id=1, source_target_pairs={{6,0},{0,2},{2,4},{4,6},{27,8},{29,10},{31,12},{25,14},{22,16},{16... | collective-permute-start | bytes 1966088 | tf_op jit(solution)/shard_map/ppermute | solution.py:43
  10.0 23.0 %collective-permute-start.3 = (bf16[640,512]{1,0:T(8,128)(2,1)}, bf16[640,512]{1,0:T(8,128)(2,1)S(1)}, u32[]{:S(2)}, u32[]{:S(2)}) collective-permute-start(bf16[640,512]{1,0:T(8,128)(2,1)} %shard_map.112.refs_4_), channel_id=1, source_target_pairs={{4,0},{6,2},{0,4},{2,6},{31,8},{25,10},{27,12},{29,14},{20,16},{22... | collective-permute-start | bytes 1966088 | tf_op jit(solution)/shard_map/ppermute | solution.py:43
  11.0 3.2 %copy-start.7 = (bf16[640,512]{1,0:T(8,128)(2,1)S(1)}, bf16[640,512]{1,0:T(8,128)(2,1)}, u32[]{:S(2)}) copy-start(bf16[640,512]{1,0:T(8,128)(2,1)} %shard_map.112.refs_4_) | copy-start | bytes 1966084
  14.2 42.0 %collective-permute-start = (bf16[256,2560]{1,0:T(8,128)(2,1)}, bf16[256,2560]{1,0:T(8,128)(2,1)S(1)}, u32[]{:S(2)}, u32[]{:S(2)}) collective-permute-start(bf16[256,2560]{1,0:T(8,128)(2,1)} %shard_map.113), channel_id=1, source_target_pairs={{8,0},{10,2},{12,4},{14,6},{0,8},{2,10},{4,12},{6,14},{24,16},{26,... | collective-permute-start | bytes 3932168 | tf_op jit(solution)/shard_map/ppermute | solution.py:43
  14.2 29.5 %collective-permute-start.4 = (bf16[640,512]{1,0:T(8,128)(2,1)S(1)}, bf16[640,512]{1,0:T(8,128)(2,1)S(1)}, u32[]{:S(2)}, u32[]{:S(2)}) collective-permute-start(bf16[640,512]{1,0:T(8,128)(2,1)S(1)} %copy-done.7), channel_id=1, source_target_pairs={{29,8},{31,10},{25,12},{27,14},{13,24},{15,26},{9,28},{11,30},{28,... | collective-permute-start | bytes 1966088 | tf_op jit(solution)/shard_map/ppermute | solution.py:43
  19.2 1.7 copy-start.5
  19.2 28.4 %collective-permute-start.5 = (bf16[640,512]{1,0:T(8,128)(2,1)S(1)}, bf16[640,512]{1,0:T(8,128)(2,1)S(1)}, u32[]{:S(2)}, u32[]{:S(2)}) collective-permute-start(bf16[640,512]{1,0:T(8,128)(2,1)S(1)} %collective-permute-done.1.refs_4_.refs_0_), channel_id=1, source_target_pairs={{32,0},{34,2},{36,4},{38,6},{232,8},{234,10},{236,12},{238,14},{48... | collective-permute-start | bytes 1966088 | tf_op jit(solution)/shard_map/ppermute | solution.py:43
  24.1 50.8 %copy-start.17 = (bf16[640,512]{1,0:T(8,128)(2,1)}, bf16[640,512]{1,0:T(8,128)(2,1)S(1)}, u32[]{:S(2)}) copy-start(bf16[640,512]{1,0:T(8,128)(2,1)S(1)} %collective-permute-done.2.refs_1_) | copy-start | bytes 1966084
  24.1 21.2 %collective-permute-start.10 = (bf16[640,256]{1,0:T(8,128)(2,1)}, bf16[640,256]{1,0:T(8,128)(2,1)S(1)}, u32[]{:S(2)}, u32[]{:S(2)}) collective-permute-start(bf16[640,256]{1,0:T(8,128)(2,1)} %get-tuple-element.22), channel_id=1, source_target_pairs={{2,0},{4,2},{6,4},{0,6},{10,8},{12,10},{14,12},{8,14},{18,16},{20,... | collective-permute-start | bytes 983048 | tf_op jit(solution)/shard_map/ppermute | solution.py:43
  33.0 41.9 %copy-start.18 = (bf16[640,512]{1,0:T(8,128)(2,1)}, bf16[640,512]{1,0:T(8,128)(2,1)S(1)}, u32[]{:S(2)}) copy-start(bf16[640,512]{1,0:T(8,128)(2,1)S(1)} %collective-permute-done.3.refs_2_) | copy-start | bytes 1966084
  33.0 14.0 %collective-permute-start.11 = (bf16[640,256]{1,0:T(8,128)(2,1)}, bf16[640,256]{1,0:T(8,128)(2,1)S(1)}, u32[]{:S(2)}, u32[]{:S(2)}) collective-permute-start(bf16[640,256]{1,0:T(8,128)(2,1)} %get-tuple-element.23), channel_id=1, source_target_pairs={{1,0},{3,2},{5,4},{7,6},{9,8},{11,10},{13,12},{15,14},{17,16},{19,... | collective-permute-start | bytes 983048 | tf_op jit(solution)/shard_map/ppermute | solution.py:43
  43.7 31.2 %copy-start.19 = (bf16[640,512]{1,0:T(8,128)(2,1)}, bf16[640,512]{1,0:T(8,128)(2,1)S(1)}, u32[]{:S(2)}) copy-start(bf16[640,512]{1,0:T(8,128)(2,1)S(1)} %collective-permute-done.4.refs_3_) | copy-start | bytes 1966084
  43.7 13.9 %collective-permute-start.6 = (bf16[640,512]{1,0:T(8,128)(2,1)S(1)}, bf16[640,512]{1,0:T(8,128)(2,1)S(1)}, u32[]{:S(2)}, u32[]{:S(2)}) collective-permute-start(bf16[640,512]{1,0:T(8,128)(2,1)S(1)} %collective-permute-done.2.refs_1_), channel_id=1, source_target_pairs={{32,0},{34,2},{36,4},{38,6},{232,8},{234,10},{236,12},{238,14},{48... | collective-permute-start | bytes 1966088 | tf_op jit(solution)/shard_map/ppermute | solution.py:43
  45.4 29.6 %copy-start.8 = (bf16[640,256]{1,0:T(8,128)(2,1)}, bf16[640,256]{1,0:T(8,128)(2,1)S(1)}, u32[]{:S(2)}) copy-start(bf16[640,256]{1,0:T(8,128)(2,1)S(1)} %collective-permute-done.10.refs_9_.refs_2_) | copy-start | bytes 983044
  45.4 19.2 %collective-permute-start.7 = (bf16[640,512]{1,0:T(8,128)(2,1)S(1)}, bf16[640,512]{1,0:T(8,128)(2,1)S(1)}, u32[]{:S(2)}, u32[]{:S(2)}) collective-permute-start(bf16[640,512]{1,0:T(8,128)(2,1)S(1)} %collective-permute-done.3.refs_2_), channel_id=1, source_target_pairs={{32,0},{34,2},{36,4},{38,6},{232,8},{234,10},{236,12},{238,14},{48... | collective-permute-start | bytes 1966088 | tf_op jit(solution)/shard_map/ppermute | solution.py:43
  47.0 27.9 %copy-start.9 = (bf16[640,256]{1,0:T(8,128)(2,1)}, bf16[640,256]{1,0:T(8,128)(2,1)S(1)}, u32[]{:S(2)}) copy-start(bf16[640,256]{1,0:T(8,128)(2,1)S(1)} %collective-permute-done.11.refs_10_.refs_3_) | copy-start | bytes 983044
  47.0 7.7 %collective-permute-start.9 = (bf16[640,256]{1,0:T(8,128)(2,1)}, bf16[640,256]{1,0:T(8,128)(2,1)S(1)}, u32[]{:S(2)}, u32[]{:S(2)}) collective-permute-start(bf16[640,256]{1,0:T(8,128)(2,1)} %get-tuple-element.21), channel_id=1, source_target_pairs={{6,0},{0,2},{2,4},{4,6},{14,8},{8,10},{10,12},{12,14},{22,16},{16,... | collective-permute-start | bytes 983048 | tf_op jit(solution)/shard_map/ppermute | solution.py:43
  47.6 4.0 %copy-start.6 = (bf16[640,512]{1,0:T(8,128)(2,1)}, bf16[640,512]{1,0:T(8,128)(2,1)S(1)}, u32[]{:S(2)}) copy-start(bf16[640,512]{1,0:T(8,128)(2,1)S(1)} %collective-permute-done.5.refs_4_) | copy-start | bytes 1966084
  47.6 23.9 %collective-permute-start.8 = (bf16[640,512]{1,0:T(8,128)(2,1)S(1)}, bf16[640,512]{1,0:T(8,128)(2,1)}, u32[]{:S(2)}, u32[]{:S(2)}) collective-permute-start(bf16[640,512]{1,0:T(8,128)(2,1)S(1)} %collective-permute-done.4.refs_3_), channel_id=1, source_target_pairs={{232,8},{234,10},{236,12},{238,14},{248,24},{250,26},{252,28},{254... | collective-permute-start | bytes 1966088 | tf_op jit(solution)/shard_map/ppermute | solution.py:43
  54.7 20.2 %copy-start.10 = (bf16[640,256]{1,0:T(8,128)(2,1)}, bf16[640,256]{1,0:T(8,128)(2,1)S(1)}, u32[]{:S(2)}) copy-start(bf16[640,256]{1,0:T(8,128)(2,1)S(1)} %collective-permute-done.9.refs_8_.refs_1_) | copy-start | bytes 983044
  54.7 16.7 %collective-permute-start.12 = (bf16[640,256]{1,0:T(8,128)(2,1)}, bf16[640,256]{1,0:T(8,128)(2,1)S(1)}, u32[]{:S(2)}, u32[]{:S(2)}) collective-permute-start(bf16[640,256]{1,0:T(8,128)(2,1)} %get-tuple-element.24), channel_id=1, source_target_pairs={{4,0},{6,2},{0,4},{2,6},{12,8},{14,10},{8,12},{10,14},{20,16},{22,... | collective-permute-start | bytes 983048 | tf_op jit(solution)/shard_map/ppermute | solution.py:43
  56.2 18.8 %copy-start.15 = (bf16[256,2560]{1,0:T(8,128)(2,1)}, bf16[256,2560]{1,0:T(8,128)(2,1)S(1)}, u32[]{:S(2)}) copy-start(bf16[256,2560]{1,0:T(8,128)(2,1)S(1)} %collective-permute-done.o_ref) | copy-start | bytes 3932164
  56.2 15.3 %collective-permute-start.13 = (bf16[640,256]{1,0:T(8,128)(2,1)}, bf16[640,256]{1,0:T(8,128)(2,1)S(1)}, u32[]{:S(2)}, u32[]{:S(2)}) collective-permute-start(bf16[640,256]{1,0:T(8,128)(2,1)} %get-tuple-element.25), channel_id=1, source_target_pairs={{7,0},{1,2},{3,4},{5,6},{15,8},{9,10},{11,12},{13,14},{23,16},{17,... | collective-permute-start | bytes 983048 | tf_op jit(solution)/shard_map/ppermute | solution.py:43
  57.6 17.3 %copy-start.20 = (bf16[640,512]{1,0:T(8,128)(2,1)}, bf16[640,512]{1,0:T(8,128)(2,1)S(1)}, u32[]{:S(2)}) copy-start(bf16[640,512]{1,0:T(8,128)(2,1)S(1)} %collective-permute-done.6.refs_5_) | copy-start | bytes 1966084
  57.6 13.8 %collective-permute-start.14 = (bf16[640,256]{1,0:T(8,128)(2,1)}, bf16[640,256]{1,0:T(8,128)(2,1)S(1)}, u32[]{:S(2)}, u32[]{:S(2)}) collective-permute-start(bf16[640,256]{1,0:T(8,128)(2,1)} %get-tuple-element.26), channel_id=1, source_target_pairs={{3,0},{5,2},{7,4},{1,6},{11,8},{13,10},{15,12},{9,14},{19,16},{21,... | collective-permute-start | bytes 983048 | tf_op jit(solution)/shard_map/ppermute | solution.py:43
  64.6 10.4 %copy-start.21 = (bf16[640,512]{1,0:T(8,128)(2,1)}, bf16[640,512]{1,0:T(8,128)(2,1)S(1)}, u32[]{:S(2)}) copy-start(bf16[640,512]{1,0:T(8,128)(2,1)S(1)} %collective-permute-done.7.refs_6_) | copy-start | bytes 1966084
  64.6 35.8 %copy-start.1 = (bf16[1,256,1024]{2,1,0:T(8,128)(2,1)S(1)}, bf16[1,256,1024]{2,1,0:T(8,128)(2,1)}, u32[]{:S(2)}) copy-start(bf16[1,256,1024]{2,1,0:T(8,128)(2,1)} %param.10) | copy-start | bytes 1572868
  64.6 35.8 %copy-start.3 = (s32[20]{0:T(128)S(1)}, s32[20]{0:T(128)}, u32[]{:S(2)}) copy-start(s32[20]{0:T(128)} %stack.83.info_ref.s_ref) | copy-start | bytes 244
  64.6 35.8 %copy-start.4 = (f32[1024]{0:T(1024)S(1)}, f32[1024]{0:T(1024)}, u32[]{:S(2)}) copy-start(f32[1024]{0:T(1024)} %param.13) | copy-start | bytes 12292
  64.6 10.3 %collective-permute-start.15 = (bf16[640,256]{1,0:T(8,128)(2,1)}, bf16[640,256]{1,0:T(8,128)(2,1)S(1)}, u32[]{:S(2)}, u32[]{:S(2)}) collective-permute-start(bf16[640,256]{1,0:T(8,128)(2,1)} %get-tuple-element.27), channel_id=1, source_target_pairs={{5,0},{7,2},{1,4},{3,6},{13,8},{15,10},{9,12},{11,14},{21,16},{23,... | collective-permute-start | bytes 983048 | tf_op jit(solution)/shard_map/ppermute | solution.py:43
  71.4 3.6 %copy-start.11 = (bf16[640,256]{1,0:T(8,128)(2,1)}, bf16[640,256]{1,0:T(8,128)(2,1)S(1)}, u32[]{:S(2)}) copy-start(bf16[640,256]{1,0:T(8,128)(2,1)S(1)} %collective-permute-done.12.refs_11_.refs_4_) | copy-start | bytes 983044
  71.5 3.6 %copy-start.12 = (bf16[640,256]{1,0:T(8,128)(2,1)}, bf16[640,256]{1,0:T(8,128)(2,1)S(1)}, u32[]{:S(2)}) copy-start(bf16[640,256]{1,0:T(8,128)(2,1)S(1)} %collective-permute-done.13.refs_12_.refs_5_) | copy-start | bytes 983044
  71.5 3.6 %copy-start.13 = (bf16[640,256]{1,0:T(8,128)(2,1)}, bf16[640,256]{1,0:T(8,128)(2,1)S(1)}, u32[]{:S(2)}) copy-start(bf16[640,256]{1,0:T(8,128)(2,1)S(1)} %collective-permute-done.14.refs_13_.refs_6_) | copy-start | bytes 983044
  84.3 16.1 %collective-permute-start.16 = (bf16[256,1024]{1,0:T(8,128)(2,1)}, bf16[256,1024]{1,0:T(8,128)(2,1)S(1)}, u32[]{:S(2)}, u32[]{:S(2)}) collective-permute-start(bf16[256,1024]{1,0:T(8,128)(2,1)} %get-tuple-element.29), channel_id=1, source_target_pairs={{8,0},{10,2},{12,4},{14,6},{0,8},{2,10},{4,12},{6,14},{24,16},{26,... | collective-permute-start | bytes 1572872 | tf_op jit(solution)/shard_map/ppermute | solution.py:43
  100.4 1.2 copy-start.2
  102.6 28.4 %copy-start = (bf16[256,1024]{1,0:T(8,128)(2,1)}, bf16[256,1024]{1,0:T(8,128)(2,1)S(1)}, u32[]{:S(2)}) copy-start(bf16[256,1024]{1,0:T(8,128)(2,1)S(1)} %shard_map.117.k_ref.refs_8_) | copy-start | bytes 1572868
  102.7 14.7 %collective-permute-start.18 = (bf16[256,1024]{1,0:T(8,128)(2,1)S(1)}, bf16[256,1024]{1,0:T(8,128)(2,1)S(1)}, u32[]{:S(2)}, u32[]{:S(2)}) collective-permute-start(bf16[256,1024]{1,0:T(8,128)(2,1)S(1)} %shard_map.117.k_ref.refs_8_), channel_id=1, source_target_pairs={{1,0},{3,2},{5,4},{7,6},{9,8},{11,10},{13,12},{15,14},{17,16},{19,... | collective-permute-start | bytes 1572872 | tf_op jit(solution)/shard_map/ppermute | solution.py:43
  103.7 14.3 %collective-permute-start.17 = (bf16[256,1024]{1,0:T(8,128)(2,1)S(1)}, bf16[256,1024]{1,0:T(8,128)(2,1)S(1)}, u32[]{:S(2)}, u32[]{:S(2)}) collective-permute-start(bf16[256,1024]{1,0:T(8,128)(2,1)S(1)} %shard_map.117.k_ref.refs_8_), channel_id=1, source_target_pairs={{8,0},{10,2},{12,4},{14,6},{0,8},{2,10},{4,12},{6,14},{24,16},{26,... | collective-permute-start | bytes 1572872 | tf_op jit(solution)/shard_map/ppermute | solution.py:43
  104.4 15.7 %collective-permute-start.21 = (bf16[256,1024]{1,0:T(8,128)(2,1)S(1)}, bf16[256,1024]{1,0:T(8,128)(2,1)S(1)}, u32[]{:S(2)}, u32[]{:S(2)}) collective-permute-start(bf16[256,1024]{1,0:T(8,128)(2,1)S(1)} %shard_map.117.k_ref.refs_8_), channel_id=1, source_target_pairs={{4,0},{6,2},{0,4},{2,6},{12,8},{14,10},{8,12},{10,14},{20,16},{22,... | collective-permute-start | bytes 1572872 | tf_op jit(solution)/shard_map/ppermute | solution.py:43
  105.8 24.1 %collective-permute-start.19 = (bf16[256,1024]{1,0:T(8,128)(2,1)S(1)}, bf16[256,1024]{1,0:T(8,128)(2,1)S(1)}, u32[]{:S(2)}, u32[]{:S(2)}) collective-permute-start(bf16[256,1024]{1,0:T(8,128)(2,1)S(1)} %shard_map.117.k_ref.refs_8_), channel_id=1, source_target_pairs={{2,0},{4,2},{6,4},{0,6},{10,8},{12,10},{14,12},{8,14},{18,16},{20,... | collective-permute-start | bytes 1572872 | tf_op jit(solution)/shard_map/ppermute | solution.py:43
  107.4 23.6 %collective-permute-start.20 = (bf16[256,1024]{1,0:T(8,128)(2,1)S(1)}, bf16[256,1024]{1,0:T(8,128)(2,1)S(1)}, u32[]{:S(2)}, u32[]{:S(2)}) collective-permute-start(bf16[256,1024]{1,0:T(8,128)(2,1)S(1)} %shard_map.117.k_ref.refs_8_), channel_id=1, source_target_pairs={{6,0},{0,2},{2,4},{4,6},{14,8},{8,10},{10,12},{12,14},{22,16},{16,... | collective-permute-start | bytes 1572872 | tf_op jit(solution)/shard_map/ppermute | solution.py:43
  107.4 33.2 %copy-start.33 = (s32[640]{0:T(1024)S(1)}, s32[640]{0:T(1024)}, u32[]{:S(2)}) copy-start(s32[640]{0:T(1024)} %param.14) | copy-start | bytes 7684
  117.4 13.7 %copy-start.22 = (bf16[256,1024]{1,0:T(8,128)(2,1)}, bf16[256,1024]{1,0:T(8,128)(2,1)S(1)}, u32[]{:S(2)}) copy-start(bf16[256,1024]{1,0:T(8,128)(2,1)S(1)} %collective-permute-done.18.refs_8_.refs_11_) | copy-start | bytes 1572868
  117.4 24.9 %collective-permute-start.23 = (bf16[256,1024]{1,0:T(8,128)(2,1)S(1)}, bf16[256,1024]{1,0:T(8,128)(2,1)}, u32[]{:S(2)}, u32[]{:S(2)}) collective-permute-start(bf16[256,1024]{1,0:T(8,128)(2,1)S(1)} %collective-permute-done.18.refs_8_.refs_11_), channel_id=1, source_target_pairs={{6,0},{0,2},{2,4},{4,6},{14,8},{8,10},{10,12},{12,14},{22,16},{16,... | collective-permute-start | bytes 1572872 | tf_op jit(solution)/shard_map/ppermute | solution.py:43
  118.0 13.1 %copy-start.34 = (bf16[256,1024]{1,0:T(8,128)(2,1)}, bf16[256,1024]{1,0:T(8,128)(2,1)S(1)}, u32[]{:S(2)}) copy-start(bf16[256,1024]{1,0:T(8,128)(2,1)S(1)} %collective-permute-done.17.o_ref) | copy-start | bytes 1572868
  118.0 24.3 %collective-permute-start.24 = (bf16[256,1024]{1,0:T(8,128)(2,1)S(1)}, bf16[256,1024]{1,0:T(8,128)(2,1)}, u32[]{:S(2)}, u32[]{:S(2)}) collective-permute-start(bf16[256,1024]{1,0:T(8,128)(2,1)S(1)} %collective-permute-done.18.refs_8_.refs_11_), channel_id=1, source_target_pairs={{2,0},{4,2},{6,4},{0,6},{10,8},{12,10},{14,12},{8,14},{18,16},{20,... | collective-permute-start | bytes 1572872 | tf_op jit(solution)/shard_map/ppermute | solution.py:43
  120.1 11.0 %copy-start.23 = (bf16[256,1024]{1,0:T(8,128)(2,1)}, bf16[256,1024]{1,0:T(8,128)(2,1)S(1)}, u32[]{:S(2)}) copy-start(bf16[256,1024]{1,0:T(8,128)(2,1)S(1)} %collective-permute-done.21.refs_11_.refs_12_) | copy-start | bytes 1572868
  120.1 22.2 %collective-permute-start.25 = (bf16[256,1024]{1,0:T(8,128)(2,1)S(1)}, bf16[256,1024]{1,0:T(8,128)(2,1)}, u32[]{:S(2)}, u32[]{:S(2)}) collective-permute-start(bf16[256,1024]{1,0:T(8,128)(2,1)S(1)} %collective-permute-done.21.refs_11_.refs_12_), channel_id=1, source_target_pairs={{1,0},{3,2},{5,4},{7,6},{9,8},{11,10},{13,12},{15,14},{17,16},{19,... | collective-permute-start | bytes 1572872 | tf_op jit(solution)/shard_map/ppermute | solution.py:43
  129.8 1.2 copy-start.24
  131.1 0.8 copy-start.25
  139.8 51.2 %collective-permute-start.22 = (bf16[256,2560]{1,0:T(8,128)(2,1)}, bf16[256,2560]{1,0:T(8,128)(2,1)S(1)}, u32[]{:S(2)}, u32[]{:S(2)}) collective-permute-start(bf16[256,2560]{1,0:T(8,128)(2,1)} %get-tuple-element.31), channel_id=1, source_target_pairs={{8,0},{10,2},{12,4},{14,6},{0,8},{2,10},{4,12},{6,14},{24,16},{26,... | collective-permute-start | bytes 3932168 | tf_op jit(solution)/shard_map/ppermute | solution.py:43
  154.5 8.8 %collective-permute-start.26 = (bf16[320,128]{1,0:T(8,128)(2,1)}, bf16[320,128]{1,0:T(8,128)(2,1)S(1)}, u32[]{:S(2)}, u32[]{:S(2)}) collective-permute-start(bf16[320,128]{1,0:T(8,128)(2,1)} %get-tuple-element.36), channel_id=1, source_target_pairs={{8,0},{10,2},{12,4},{14,6},{0,8},{2,10},{4,12},{6,14},{24,16},{26,... | collective-permute-start | bytes 245768 | tf_op jit(solution)/shard_map/ppermute | solution.py:43
  155.0 8.2 %collective-permute-start.27 = (bf16[320,128]{1,0:T(8,128)(2,1)}, bf16[320,128]{1,0:T(8,128)(2,1)S(1)}, u32[]{:S(2)}, u32[]{:S(2)}) collective-permute-start(bf16[320,128]{1,0:T(8,128)(2,1)} %get-tuple-element.37), channel_id=1, source_target_pairs={{16,0},{18,2},{20,4},{22,6},{24,8},{26,10},{28,12},{30,14},{0,16},... | collective-permute-start | bytes 245768 | tf_op jit(solution)/shard_map/ppermute | solution.py:43
  157.5 5.8 %collective-permute-start.28 = (bf16[320,128]{1,0:T(8,128)(2,1)}, bf16[320,128]{1,0:T(8,128)(2,1)S(1)}, u32[]{:S(2)}, u32[]{:S(2)}) collective-permute-start(bf16[320,128]{1,0:T(8,128)(2,1)} %get-tuple-element.38), channel_id=1, source_target_pairs={{24,0},{26,2},{28,4},{30,6},{16,8},{18,10},{20,12},{22,14},{8,16},... | collective-permute-start | bytes 245768 | tf_op jit(solution)/shard_map/ppermute | solution.py:43
  165.6 8.2 %collective-permute-start.29 = (bf16[320,128]{1,0:T(8,128)(2,1)}, bf16[320,128]{1,0:T(8,128)(2,1)S(1)}, u32[]{:S(2)}, u32[]{:S(2)}) collective-permute-start(bf16[320,128]{1,0:T(8,128)(2,1)} %shard_map.122), channel_id=1, source_target_pairs={{32,0},{34,2},{36,4},{38,6},{40,8},{42,10},{44,12},{46,14},{48,16}... | collective-permute-start | bytes 245768 | tf_op jit(solution)/shard_map/ppermute | solution.py:43
  174.8 5.7 %collective-permute-start.30 = (bf16[320,128]{1,0:T(8,128)(2,1)S(1)}, bf16[320,128]{1,0:T(8,128)(2,1)S(1)}, u32[]{:S(2)}, u32[]{:S(2)}) collective-permute-start(bf16[320,128]{1,0:T(8,128)(2,1)S(1)} %add_convert_fusion.1), channel_id=1, source_target_pairs={{64,0},{66,2},{68,4},{70,6},{72,8},{74,10},{76,12},{78,14},{80,16}... | collective-permute-start | bytes 245768 | tf_op jit(solution)/shard_map/ppermute | solution.py:43
  174.9 7.8 %collective-permute-start.31 = (bf16[320,128]{1,0:T(8,128)(2,1)S(1)}, bf16[320,128]{1,0:T(8,128)(2,1)S(1)}, u32[]{:S(2)}, u32[]{:S(2)}) collective-permute-start(bf16[320,128]{1,0:T(8,128)(2,1)S(1)} %add_convert_fusion.1), channel_id=1, source_target_pairs={{128,0},{130,2},{132,4},{134,6},{136,8},{138,10},{140,12},{142,14}... | collective-permute-start | bytes 245768 | tf_op jit(solution)/shard_map/ppermute | solution.py:43
  178.7 9.9 %collective-permute-start.32 = (bf16[320,128]{1,0:T(8,128)(2,1)S(1)}, bf16[320,128]{1,0:T(8,128)(2,1)S(1)}, u32[]{:S(2)}, u32[]{:S(2)}) collective-permute-start(bf16[320,128]{1,0:T(8,128)(2,1)S(1)} %add_convert_fusion.1), channel_id=1, source_target_pairs={{192,0},{194,2},{196,4},{198,6},{200,8},{202,10},{204,12},{206,14}... | collective-permute-start | bytes 245768 | tf_op jit(solution)/shard_map/ppermute | solution.py:43
  188.6 6.9 %copy-start.26 = (bf16[320,128]{1,0:T(8,128)(2,1)}, bf16[320,128]{1,0:T(8,128)(2,1)S(1)}, u32[]{:S(2)}) copy-start(bf16[320,128]{1,0:T(8,128)(2,1)S(1)} %add_convert_fusion.a) | copy-start | bytes 245764
  188.6 6.9 %collective-permute-start.33 = (bf16[320,128]{1,0:T(8,128)(2,1)S(1)}, bf16[320,128]{1,0:T(8,128)(2,1)S(1)}, u32[]{:S(2)}, u32[]{:S(2)}) collective-permute-start(bf16[320,128]{1,0:T(8,128)(2,1)S(1)} %add_convert_fusion.a), channel_id=1, source_target_pairs={{8,0},{10,2},{12,4},{14,6},{0,8},{2,10},{4,12},{6,14},{24,16},{26,... | collective-permute-start | bytes 245768 | tf_op jit(solution)/shard_map/ppermute | solution.py:43
  189.3 6.3 %collective-permute-start.34 = (bf16[320,128]{1,0:T(8,128)(2,1)S(1)}, bf16[320,128]{1,0:T(8,128)(2,1)S(1)}, u32[]{:S(2)}, u32[]{:S(2)}) collective-permute-start(bf16[320,128]{1,0:T(8,128)(2,1)S(1)} %add_convert_fusion.a), channel_id=1, source_target_pairs={{16,0},{18,2},{20,4},{22,6},{24,8},{26,10},{28,12},{30,14},{0,16},... | collective-permute-start | bytes 245768 | tf_op jit(solution)/shard_map/ppermute | solution.py:43
  189.8 5.8 %collective-permute-start.35 = (bf16[320,128]{1,0:T(8,128)(2,1)S(1)}, bf16[320,128]{1,0:T(8,128)(2,1)S(1)}, u32[]{:S(2)}, u32[]{:S(2)}) collective-permute-start(bf16[320,128]{1,0:T(8,128)(2,1)S(1)} %add_convert_fusion.a), channel_id=1, source_target_pairs={{24,0},{26,2},{28,4},{30,6},{16,8},{18,10},{20,12},{22,14},{8,16},... | collective-permute-start | bytes 245768 | tf_op jit(solution)/shard_map/ppermute | solution.py:43
  191.0 1.1 copy-start.16
  (7 other events, 4.6 us)
